TPU v7x, 32 devices: a whole 2x2x4 slice. The times are simulated.
32 devices in a mesh: groups: 2 (over y), hst: 4 (over z), mp: 2 (over x), rep: 2 (over core).
Axes of the slice: x: 2, y: 2, z: 4, core: 2. Of those that a mesh axis runs over, the one named last changes fastest.
Arguments:
- activations: bfloat16 [4, 1024, 6144], P(None, ('groups', 'hst', 'rep'), 'mp'), parts along dimension 1, may hold values from -6 to 6
- shrink_weight: bfloat16 [128, 16, 6144], P('hst', None, 'mp'), may hold values from -0.078125 to 0.078125
- expand_weight: bfloat16 [128, 16, 6144], P('hst', None, 'mp'), may hold values from -1.5 to 1.5
- former_layout_list: int32 [256], P('groups'), parts along dimension 0, may hold values from 0 to 127, as said below
- host_layout_list: int32 [256], P('groups'), parts along dimension 0, may hold values from 0 to 127, as said below
- target_host: int32 [4, 1024, 1], P(None, ('groups', 'hst', 'rep')), parts along dimension 1, may hold values from 0 to 3; in each aligned block of 64 rows (0 to 63, 64 to 127, ..., all dimensions but the last counted through in order) at most 32 rows name the same one
- target_position: int32 [4, 1024], P(None, ('groups', 'hst', 'rep')), parts along dimension 1, may hold values from 0 to 31
Outputs:
- lora_delta: bfloat16 [4, 1024, 6144], P(None, ('groups', 'hst', 'rep'), 'mp'), parts along dimension 1
There are 2 independent parts, one for each index of `groups`. A program takes and returns all parts, laid end to end along the dimension named above; an argument that names none is the same for every part. Nothing has to cross between parts.
Inputs may be any that keep to these rules, and one draw needn't show every extreme that they name: `former_layout_list`: a permutation of the adapters. `host_layout_list`: positions h * 32 to (h + 1) * 32 - 1 belong to host h; of one host's positions exactly 8 hold adapters whose old positions lie with each owner; an adapter may stand on several hosts. `target_host`: in each step, the 64 requests of one device name one host at most 32 times.
All inputs are finite; a program needn't handle non-finite values.
Results may differ from a plain program's by a relative error of at most 0.0051.
Values may be sent and summed in bfloat16 or wider, within the bound.
No kernel may reach another device: no remote copies, remote signals or barrier semaphores. Data moves between devices by JAX's collectives and lax.ppermute only.
A program may use at most 64 MiB of HBM per device.

v0:
```python
import jax
import jax.numpy as jnp
from jax import lax
from jax.sharding import PartitionSpec as P


def local(
    activations,
    shrink_weight,
    expand_weight,
    former_layout_list,
    host_layout_list,
    target_host,
    target_position,
):
    host_count = lax.axis_size("hst")
    host_index = lax.axis_index("hst")
    local_adapters = shrink_weight.shape[0]
    rank_extent = shrink_weight.shape[1]
    portion_width = shrink_weight.shape[2]
    move_cap = local_adapters // host_count
    table_size = former_layout_list.shape[0]
    matched = host_layout_list[:, None] == former_layout_list[None, :]
    source = jnp.sum(
        jnp.where(matched, jnp.arange(table_size, dtype=jnp.int32)[None, :], 0), axis=1
    )
    owners = (source // local_adapters).reshape(host_count, local_adapters)
    within = (source % local_adapters).reshape(host_count, local_adapters)
    same_owner = owners[:, :, None] == owners[:, None, :]
    earlier = jnp.arange(local_adapters)[None, :] < jnp.arange(local_adapters)[:, None]
    order_rank = jnp.sum((same_owner & earlier[None, :, :]).astype(jnp.int32), axis=2)
    matches = (
        (owners == host_index)[:, :, None, None]
        & (order_rank[:, :, None, None] == jnp.arange(move_cap)[None, None, :, None])
        & (within[:, :, None, None] == jnp.arange(local_adapters)[None, None, None, :])
    )
    adapter_picker_mask = jnp.sum(matches.astype(jnp.int32), axis=1).astype(jnp.bfloat16)
    send_a = jnp.einsum(
        "bgl,lvu->bgvu", adapter_picker_mask, shrink_weight, preferred_element_type=jnp.float32
    ).astype(jnp.bfloat16)
    send_b = jnp.einsum(
        "bgl,lvu->bgvu", adapter_picker_mask, expand_weight, preferred_element_type=jnp.float32
    ).astype(jnp.bfloat16)
    own_owner = lax.dynamic_index_in_dim(owners, host_index, 0, keepdims=False)
    own_rank = lax.dynamic_index_in_dim(order_rank, host_index, 0, keepdims=False)
    picker = (
        (own_owner[:, None, None] == jnp.arange(host_count)[None, :, None])
        & (own_rank[:, None, None] == jnp.arange(move_cap)[None, None, :])
    ).astype(jnp.bfloat16)

    def settle(received):
        return jnp.einsum(
            "shk,hkrd->srd", picker, received, preferred_element_type=jnp.float32
        ).astype(jnp.bfloat16)

    recv_a, recv_b = (
        lax.all_to_all(send_a, "hst", split_axis=0, concat_axis=0, tiled=True),
        lax.all_to_all(send_b, "hst", split_axis=0, concat_axis=0, tiled=True),
    )
    new_a = settle(recv_a)
    new_b = settle(recv_b)
    flat_a = new_a.reshape(local_adapters * rank_extent, portion_width)
    flat_b = new_b.reshape(local_adapters * rank_extent, portion_width)
    results = []
    for step_index in range(activations.shape[0]):
        inputs_now = activations[step_index]
        host_now = target_host[step_index, :, 0]
        slot_now = target_position[step_index]
        row_count = inputs_now.shape[0]
        slot_cap = 2 * row_count // host_count
        dest_onehot = (host_now[:, None] == jnp.arange(host_count)[None, :]).astype(jnp.int32)
        before = jnp.cumsum(dest_onehot, axis=0) - dest_onehot
        row_rank = jnp.sum(before * dest_onehot, axis=1)
        target = host_now * slot_cap + row_rank
        placer = (target[None, :] == jnp.arange(host_count * slot_cap)[:, None]).astype(
            jnp.bfloat16
        )
        outgoing = jnp.dot(placer, inputs_now, preferred_element_type=jnp.float32).astype(
            jnp.bfloat16
        )
        outgoing = outgoing.reshape(host_count, slot_cap, portion_width)
        slot_sent = jnp.dot(
            placer, slot_now.astype(jnp.bfloat16)[:, None], preferred_element_type=jnp.float32
        )
        slot_sent = slot_sent.astype(jnp.bfloat16).reshape(host_count, slot_cap)
        serve_inputs_now = lax.all_to_all(outgoing, "hst", split_axis=0, concat_axis=0, tiled=True)
        serve_slot_now = lax.all_to_all(slot_sent, "hst", split_axis=0, concat_axis=0, tiled=True)
        in_shape = serve_inputs_now.shape
        flat_rows = serve_inputs_now.reshape(-1, in_shape[-1])
        slot_ids = serve_slot_now.reshape(-1).astype(jnp.float32)
        partial_value = lax.dot_general(
            flat_rows, flat_a, (((1,), (1,)), ((), ())), preferred_element_type=jnp.float32
        )
        slot_mask = (
            slot_ids[:, None] == jnp.arange(local_adapters, dtype=jnp.float32)[None, :]
        ).astype(jnp.float32)
        reduced = jnp.sum(
            partial_value.reshape(-1, local_adapters, rank_extent) * slot_mask[:, :, None], axis=1
        )
        summed = lax.psum(reduced, "mp")
        shrink = summed.astype(jnp.bfloat16)
        spread = (slot_mask.astype(jnp.bfloat16)[:, :, None] * shrink[:, None, :]).reshape(
            -1, local_adapters * rank_extent
        )
        adapted = jnp.dot(spread, flat_b, preferred_element_type=jnp.float32).astype(jnp.bfloat16)
        returned = lax.all_to_all(
            adapted.reshape(in_shape), "hst", split_axis=0, concat_axis=0, tiled=True
        )
        returned = returned.reshape(host_count * slot_cap, portion_width)
        adapted_rows = lax.dot_general(
            placer, returned, (((0,), (0,)), ((), ())), preferred_element_type=jnp.float32
        )
        results.append(adapted_rows.astype(jnp.bfloat16))
    return jnp.stack(results)


def solution(mesh):
    return jax.shard_map(
        local,
        mesh=mesh,
        in_specs=(
            P(None, ("groups", "hst", "rep"), "mp"),
            P("hst", None, "mp"),
            P("hst", None, "mp"),
            P("groups"),
            P("groups"),
            P(None, ("groups", "hst", "rep"), None),
            P(None, ("groups", "hst", "rep")),
        ),
        out_specs=P(None, ("groups", "hst", "rep"), "mp"),
        check_vma=False,
    )
```

profile of v0, /device:TPU:0, one launch (start us, length us, event | category | flops | bytes accessed | tf_op | source)
XLA Modules:
  0.0 375.9 jit_solution(1816512152631604066)
XLA Ops:
  4.0 6.3 %all-to-all-start = ((bf16[4,1,32]{2,1,0:T(2,128)(2,1)}), bf16[4,1,32]{2,1,0:T(2,128)(2,1)S(1)}, u32[]{:S(2)}, u32[]{:S(2)}) async-start(bf16[4,1,32]{2,1,0:T(2,128)(2,1)} %all_to_all.72), calls=%async_computation | async-start | bytes 4096 | tf_op jit(solution)/shard_map/all_to_all | solution.py:87
  11.1 4.6 %all-to-all-done = bf16[4,1,32]{2,1,0:T(2,128)(2,1)S(1)} async-done(((bf16[4,1,32]{2,1,0:T(2,128)(2,1)}), bf16[4,1,32]{2,1,0:T(2,128)(2,1)S(1)}, u32[]{:S(2)}, u32[]{:S(2)}) %all-to-all-start) | async-done | bytes 288 | tf_op jit(solution)/shard_map/all_to_all | solution.py:87
  15.7 3.2 all-to-all-start.5
  19.8 4.6 %all-to-all-done.5 = bf16[4,1,32]{2,1,0:T(2,128)(2,1)S(1)} async-done(((bf16[4,1,32]{2,1,0:T(2,128)(2,1)}), bf16[4,1,32]{2,1,0:T(2,128)(2,1)S(1)}, u32[]{:S(2)}, u32[]{:S(2)}) %all-to-all-start.5) | async-done | bytes 288 | tf_op jit(solution)/shard_map/all_to_all | solution.py:87
  24.4 3.2 all-to-all-start.8
  28.5 4.5 %all-to-all-done.8 = bf16[4,1,32]{2,1,0:T(2,128)(2,1)S(1)} async-done(((bf16[4,1,32]{2,1,0:T(2,128)(2,1)}), bf16[4,1,32]{2,1,0:T(2,128)(2,1)S(1)}, u32[]{:S(2)}, u32[]{:S(2)}) %all-to-all-start.8) | async-done | bytes 288 | tf_op jit(solution)/shard_map/all_to_all | solution.py:87
  33.0 3.2 all-to-all-start.11
  36.2 2.2 convolution_convert_fusion.5
  38.5 3.2 all-to-all-done.11
  41.7 3.5 all-to-all-start.1
  45.2 2.2 convolution_convert_fusion.4
  47.4 13.5 %all-to-all-done.1 = bf16[4,32,3072]{2,1,0:T(8,128)(2,1)S(1)} async-done(((bf16[4,32,3072]{2,1,0:T(8,128)(2,1)}), bf16[4,32,3072]{2,1,0:T(8,128)(2,1)S(1)}, u32[]{:S(2)}, u32[]{:S(2)}) %all-to-all-start.1) | async-done | bytes 786464 | tf_op jit(solution)/shard_map/all_to_all | solution.py:86
  61.8 4.2 %all-to-all-start.6 = ((bf16[4,32,3072]{2,1,0:T(8,128)(2,1)}), bf16[4,32,3072]{2,1,0:T(8,128)(2,1)}, u32[]{:S(2)}, u32[]{:S(2)}) async-start(bf16[4,32,3072]{2,1,0:T(8,128)(2,1)} %bitcast.29), calls=%async_computation.6 | async-start | bytes 1572864 | tf_op jit(solution)/shard_map/all_to_all | solution.py:86
  66.0 2.4 convolution_convert_fusion.3
  68.4 14.1 %all-to-all-done.6 = bf16[4,32,3072]{2,1,0:T(8,128)(2,1)} async-done(((bf16[4,32,3072]{2,1,0:T(8,128)(2,1)}), bf16[4,32,3072]{2,1,0:T(8,128)(2,1)}, u32[]{:S(2)}, u32[]{:S(2)}) %all-to-all-start.6) | async-done | bytes 786464 | tf_op jit(solution)/shard_map/all_to_all | solution.py:86
  82.6 4.2 %all-to-all-start.9 = ((bf16[4,32,3072]{2,1,0:T(8,128)(2,1)}), bf16[4,32,3072]{2,1,0:T(8,128)(2,1)}, u32[]{:S(2)}, u32[]{:S(2)}) async-start(bf16[4,32,3072]{2,1,0:T(8,128)(2,1)} %bitcast.161), calls=%async_computation.9 | async-start | bytes 1572864 | tf_op jit(solution)/shard_map/all_to_all | solution.py:86
  87.3 2.2 convolution_convert_fusion.2
  89.5 14.7 %all-to-all-done.9 = bf16[4,32,3072]{2,1,0:T(8,128)(2,1)} async-done(((bf16[4,32,3072]{2,1,0:T(8,128)(2,1)}), bf16[4,32,3072]{2,1,0:T(8,128)(2,1)}, u32[]{:S(2)}, u32[]{:S(2)}) %all-to-all-start.9) | async-done | bytes 786464 | tf_op jit(solution)/shard_map/all_to_all | solution.py:86
  104.2 4.2 %all-to-all-start.12 = ((bf16[4,32,3072]{2,1,0:T(8,128)(2,1)}), bf16[4,32,3072]{2,1,0:T(8,128)(2,1)}, u32[]{:S(2)}, u32[]{:S(2)}) async-start(bf16[4,32,3072]{2,1,0:T(8,128)(2,1)} %bitcast.162), calls=%async_computation.12 | async-start | bytes 1572864 | tf_op jit(solution)/shard_map/all_to_all | solution.py:86
  108.8 6.0 %convolution_convert_fusion.1 = bf16[4,8,16,3072]{3,1,2,0:T(8,128)(2,1)} fusion(bf16[32,16,3072]{2,1,0:T(8,128)(2,1)S(1)} %copy-done, s32[4,8,32]{2,1,0:T(8,128)S(1)} %convert_reduce_fusion), kind=kOutput, calls=%fused_computation.3 | convolution fusion | flops 102237184 | bytes 6295552 | tf_op jit(solution)/shard_map/bgl,lvu->bgvu/dot_general | solution.py:38
  114.8 11.9 %all-to-all-done.12 = bf16[4,32,3072]{2,1,0:T(8,128)(2,1)} async-done(((bf16[4,32,3072]{2,1,0:T(8,128)(2,1)}), bf16[4,32,3072]{2,1,0:T(8,128)(2,1)}, u32[]{:S(2)}, u32[]{:S(2)}) %all-to-all-start.12) | async-done | bytes 786464 | tf_op jit(solution)/shard_map/all_to_all | solution.py:86
  126.7 3.7 all-to-all-start.2
  130.4 7.9 %convolution_convert_fusion = bf16[4,8,16,3072]{3,1,2,0:T(8,128)(2,1)} fusion(bf16[32,16,3072]{2,1,0:T(8,128)(2,1)} %param.9, s32[4,8,32]{2,1,0:T(8,128)S(1)} %convert_reduce_fusion), kind=kOutput, calls=%fused_computation.2 | convolution fusion | flops 102237184 | bytes 6295552 | tf_op jit(solution)/shard_map/bgl,lvu->bgvu/dot_general | solution.py:41
  138.3 62.1 %all-to-all-done.2 = bf16[4,8,16,3072]{3,1,2,0:T(8,128)(2,1)S(1)} async-done(((bf16[4,8,16,3072]{3,1,2,0:T(8,128)(2,1)}), bf16[4,8,16,3072]{3,1,2,0:T(8,128)(2,1)S(1)}, u32[]{:S(2)}, u32[]{:S(2)}) %all-to-all-start.2) | async-done | bytes 3145760 | tf_op jit(solution)/shard_map/all_to_all | solution.py:57
  200.4 4.8 %all-to-all-start.3 = ((bf16[4,8,16,3072]{3,1,2,0:T(8,128)(2,1)}), bf16[4,8,16,3072]{3,1,2,0:T(8,128)(2,1)}, u32[]{:S(2)}, u32[]{:S(2)}) async-start(bf16[4,8,16,3072]{3,1,2,0:T(8,128)(2,1)} %convolution_convert_fusion), calls=%async_computation.3 | async-start | bytes 6291456 | tf_op jit(solution)/shard_map/all_to_all | solution.py:58
  205.7 1.0 bitcast_convert_fusion.1
  207.9 2.1 fusion.13
  210.0 2.1 fusion.14
  212.1 2.1 fusion.15
  214.2 8.4 %all-reduce = (bf16[128,16]{0,1:T(8,128)(2,1)S(1)}, bf16[128,16]{0,1:T(8,128)(2,1)S(1)}, bf16[128,16]{0,1:T(8,128)(2,1)S(1)}, bf16[128,16]{0,1:T(8,128)(2,1)S(1)}) all-reduce(f32[128,16]{0,1:T(8,128)S(1)} %fusion.15, f32[128,16]{0,1:T(8,128)S(1)} %fusion.14, ...), channel_id=1, replica_groups=mesh['groups'=2,'hst'=4,'mp'=2,'rep'=2] {'mp'}, use_global_device_ids=true, to_apply=%region_18.19 | all-reduce | flops 8192 | bytes 49152 | tf_op jit(solution)/shard_map/psum | solution.py:100
  222.6 52.6 %all-to-all-done.3 = bf16[4,8,16,3072]{3,1,2,0:T(8,128)(2,1)} async-done(((bf16[4,8,16,3072]{3,1,2,0:T(8,128)(2,1)}), bf16[4,8,16,3072]{3,1,2,0:T(8,128)(2,1)}, u32[]{:S(2)}, u32[]{:S(2)}) %all-to-all-start.3) | async-done | bytes 3145760 | tf_op jit(solution)/shard_map/all_to_all | solution.py:58
  275.2 2.9 bitcast_convert_fusion
  278.1 1.5 fusion
  279.7 4.2 %all-to-all-start.4 = ((bf16[4,32,3072]{2,1,0:T(8,128)(2,1)}), bf16[4,32,3072]{2,1,0:T(8,128)(2,1)}, u32[]{:S(2)}, u32[]{:S(2)}) async-start(bf16[4,32,3072]{2,1,0:T(8,128)(2,1)} %bitcast.167), calls=%async_computation.4 | async-start | bytes 1572864 | tf_op jit(solution)/shard_map/all_to_all | solution.py:106
  283.8 1.5 fusion.1
  285.3 18.2 %all-to-all-done.4 = bf16[4,32,3072]{2,1,0:T(8,128)(2,1)} async-done(((bf16[4,32,3072]{2,1,0:T(8,128)(2,1)}), bf16[4,32,3072]{2,1,0:T(8,128)(2,1)}, u32[]{:S(2)}, u32[]{:S(2)}) %all-to-all-start.4) | async-done | bytes 786464 | tf_op jit(solution)/shard_map/all_to_all | solution.py:106
  303.5 4.2 %all-to-all-start.7 = ((bf16[4,32,3072]{2,1,0:T(8,128)(2,1)}), bf16[4,32,3072]{2,1,0:T(8,128)(2,1)}, u32[]{:S(2)}, u32[]{:S(2)}) async-start(bf16[4,32,3072]{2,1,0:T(8,128)(2,1)} %bitcast.166), calls=%async_computation.7 | async-start | bytes 1572864 | tf_op jit(solution)/shard_map/all_to_all | solution.py:106
  307.7 1.5 fusion.2
  309.2 18.1 %all-to-all-done.7 = bf16[4,32,3072]{2,1,0:T(8,128)(2,1)} async-done(((bf16[4,32,3072]{2,1,0:T(8,128)(2,1)}), bf16[4,32,3072]{2,1,0:T(8,128)(2,1)}, u32[]{:S(2)}, u32[]{:S(2)}) %all-to-all-start.7) | async-done | bytes 786464 | tf_op jit(solution)/shard_map/all_to_all | solution.py:106
  327.4 4.2 %all-to-all-start.10 = ((bf16[4,32,3072]{2,1,0:T(8,128)(2,1)}), bf16[4,32,3072]{2,1,0:T(8,128)(2,1)}, u32[]{:S(2)}, u32[]{:S(2)}) async-start(bf16[4,32,3072]{2,1,0:T(8,128)(2,1)} %bitcast.165), calls=%async_computation.10 | async-start | bytes 1572864 | tf_op jit(solution)/shard_map/all_to_all | solution.py:106
  331.5 1.5 fusion.3
  333.0 18.2 %all-to-all-done.10 = bf16[4,32,3072]{2,1,0:T(8,128)(2,1)} async-done(((bf16[4,32,3072]{2,1,0:T(8,128)(2,1)}), bf16[4,32,3072]{2,1,0:T(8,128)(2,1)}, u32[]{:S(2)}, u32[]{:S(2)}) %all-to-all-start.10) | async-done | bytes 786464 | tf_op jit(solution)/shard_map/all_to_all | solution.py:106
  351.2 3.5 all-to-all-start.13
  354.7 1.4 fusion.4
  356.2 1.4 fusion.5
  357.6 1.4 fusion.6
  359.1 15.2 %all-to-all-done.13 = bf16[4,32,3072]{2,1,0:T(8,128)(2,1)S(1)} async-done(((bf16[4,32,3072]{2,1,0:T(8,128)(2,1)}), bf16[4,32,3072]{2,1,0:T(8,128)(2,1)S(1)}, u32[]{:S(2)}, u32[]{:S(2)}) %all-to-all-start.13) | async-done | bytes 786464 | tf_op jit(solution)/shard_map/all_to_all | solution.py:106
  374.6 1.3 pad_maximum_fusion
  (57 shorter events, 10.1 us)
Async XLA Ops:
  4.0 11.7 %all-to-all-start = ((bf16[4,1,32]{2,1,0:T(2,128)(2,1)}), bf16[4,1,32]{2,1,0:T(2,128)(2,1)S(1)}, u32[]{:S(2)}, u32[]{:S(2)}) async-start(bf16[4,1,32]{2,1,0:T(2,128)(2,1)} %all_to_all.72), calls=%async_computation | async-start | bytes 4096 | tf_op jit(solution)/shard_map/all_to_all | solution.py:87
  15.7 8.7 %all-to-all-start.5 = ((bf16[4,1,32]{2,1,0:T(2,128)(2,1)}), bf16[4,1,32]{2,1,0:T(2,128)(2,1)S(1)}, u32[]{:S(2)}, u32[]{:S(2)}) async-start(bf16[4,1,32]{2,1,0:T(2,128)(2,1)} %all_to_all.73), calls=%async_computation.5 | async-start | bytes 4096 | tf_op jit(solution)/shard_map/all_to_all | solution.py:87
  24.4 8.6 %all-to-all-start.8 = ((bf16[4,1,32]{2,1,0:T(2,128)(2,1)}), bf16[4,1,32]{2,1,0:T(2,128)(2,1)S(1)}, u32[]{:S(2)}, u32[]{:S(2)}) async-start(bf16[4,1,32]{2,1,0:T(2,128)(2,1)} %all_to_all.74), calls=%async_computation.8 | async-start | bytes 4096 | tf_op jit(solution)/shard_map/all_to_all | solution.py:87
  33.0 8.7 %all-to-all-start.11 = ((bf16[4,1,32]{2,1,0:T(2,128)(2,1)}), bf16[4,1,32]{2,1,0:T(2,128)(2,1)S(1)}, u32[]{:S(2)}, u32[]{:S(2)}) async-start(bf16[4,1,32]{2,1,0:T(2,128)(2,1)} %all_to_all.75), calls=%async_computation.11 | async-start | bytes 4096 | tf_op jit(solution)/shard_map/all_to_all | solution.py:87
  41.7 19.3 %all-to-all-start.1 = ((bf16[4,32,3072]{2,1,0:T(8,128)(2,1)}), bf16[4,32,3072]{2,1,0:T(8,128)(2,1)S(1)}, u32[]{:S(2)}, u32[]{:S(2)}) async-start(bf16[4,32,3072]{2,1,0:T(8,128)(2,1)} %bitcast.5), calls=%async_computation.1 | async-start | bytes 1572864 | tf_op jit(solution)/shard_map/all_to_all | solution.py:86
  45.2 41.6 %copy-start.3 = (s32[128]{0:T(128)S(1)}, s32[128]{0:T(128)}, u32[]{:S(2)}) copy-start(s32[128]{0:T(128)} %param.10) | copy-start | bytes 1540
  45.2 41.6 %copy-start.4 = (s32[128]{0:T(128)S(1)}, s32[128]{0:T(128)}, u32[]{:S(2)}) copy-start(s32[128]{0:T(128)} %param.11) | copy-start | bytes 1540
  60.9 0.9 copy-start.1
  61.8 20.7 %all-to-all-start.6 = ((bf16[4,32,3072]{2,1,0:T(8,128)(2,1)}), bf16[4,32,3072]{2,1,0:T(8,128)(2,1)}, u32[]{:S(2)}, u32[]{:S(2)}) async-start(bf16[4,32,3072]{2,1,0:T(8,128)(2,1)} %bitcast.29), calls=%async_computation.6 | async-start | bytes 1572864 | tf_op jit(solution)/shard_map/all_to_all | solution.py:86
  66.0 42.8 %copy-start = (bf16[32,16,3072]{2,1,0:T(8,128)(2,1)S(1)}, bf16[32,16,3072]{2,1,0:T(8,128)(2,1)}, u32[]{:S(2)}) copy-start(bf16[32,16,3072]{2,1,0:T(8,128)(2,1)} %param.8) | copy-start | bytes 9437188
  82.6 21.6 %all-to-all-start.9 = ((bf16[4,32,3072]{2,1,0:T(8,128)(2,1)}), bf16[4,32,3072]{2,1,0:T(8,128)(2,1)}, u32[]{:S(2)}, u32[]{:S(2)}) async-start(bf16[4,32,3072]{2,1,0:T(8,128)(2,1)} %bitcast.161), calls=%async_computation.9 | async-start | bytes 1572864 | tf_op jit(solution)/shard_map/all_to_all | solution.py:86
  104.2 22.5 %all-to-all-start.12 = ((bf16[4,32,3072]{2,1,0:T(8,128)(2,1)}), bf16[4,32,3072]{2,1,0:T(8,128)(2,1)}, u32[]{:S(2)}, u32[]{:S(2)}) async-start(bf16[4,32,3072]{2,1,0:T(8,128)(2,1)} %bitcast.162), calls=%async_computation.12 | async-start | bytes 1572864 | tf_op jit(solution)/shard_map/all_to_all | solution.py:86
  126.7 73.7 %all-to-all-start.2 = ((bf16[4,8,16,3072]{3,1,2,0:T(8,128)(2,1)}), bf16[4,8,16,3072]{3,1,2,0:T(8,128)(2,1)S(1)}, u32[]{:S(2)}, u32[]{:S(2)}) async-start(bf16[4,8,16,3072]{3,1,2,0:T(8,128)(2,1)} %convolution_convert_fusion.1), calls=%async_computation.2 | async-start | bytes 6291456 | tf_op jit(solution)/shard_map/all_to_all | solution.py:57
  200.4 74.9 %all-to-all-start.3 = ((bf16[4,8,16,3072]{3,1,2,0:T(8,128)(2,1)}), bf16[4,8,16,3072]{3,1,2,0:T(8,128)(2,1)}, u32[]{:S(2)}, u32[]{:S(2)}) async-start(bf16[4,8,16,3072]{3,1,2,0:T(8,128)(2,1)} %convolution_convert_fusion), calls=%async_computation.3 | async-start | bytes 6291456 | tf_op jit(solution)/shard_map/all_to_all | solution.py:58
  205.7 1.1 copy-start.2
  279.7 23.8 %all-to-all-start.4 = ((bf16[4,32,3072]{2,1,0:T(8,128)(2,1)}), bf16[4,32,3072]{2,1,0:T(8,128)(2,1)}, u32[]{:S(2)}, u32[]{:S(2)}) async-start(bf16[4,32,3072]{2,1,0:T(8,128)(2,1)} %bitcast.167), calls=%async_computation.4 | async-start | bytes 1572864 | tf_op jit(solution)/shard_map/all_to_all | solution.py:106
  303.5 23.9 %all-to-all-start.7 = ((bf16[4,32,3072]{2,1,0:T(8,128)(2,1)}), bf16[4,32,3072]{2,1,0:T(8,128)(2,1)}, u32[]{:S(2)}, u32[]{:S(2)}) async-start(bf16[4,32,3072]{2,1,0:T(8,128)(2,1)} %bitcast.166), calls=%async_computation.7 | async-start | bytes 1572864 | tf_op jit(solution)/shard_map/all_to_all | solution.py:106
  327.4 23.8 %all-to-all-start.10 = ((bf16[4,32,3072]{2,1,0:T(8,128)(2,1)}), bf16[4,32,3072]{2,1,0:T(8,128)(2,1)}, u32[]{:S(2)}, u32[]{:S(2)}) async-start(bf16[4,32,3072]{2,1,0:T(8,128)(2,1)} %bitcast.165), calls=%async_computation.10 | async-start | bytes 1572864 | tf_op jit(solution)/shard_map/all_to_all | solution.py:106
  351.2 23.1 %all-to-all-start.13 = ((bf16[4,32,3072]{2,1,0:T(8,128)(2,1)}), bf16[4,32,3072]{2,1,0:T(8,128)(2,1)S(1)}, u32[]{:S(2)}, u32[]{:S(2)}) async-start(bf16[4,32,3072]{2,1,0:T(8,128)(2,1)} %bitcast.164), calls=%async_computation.13 | async-start | bytes 1572864 | tf_op jit(solution)/shard_map/all_to_all | solution.py:106
where the time goes:
time: 377 us; the launch traced here: 376 us
  waiting for transfers between devices  255 us (68%)
  starting transfers between devices  56.7 us (15%)
  matrix products  45.4 us (12%)
  blocking collectives  8.4 us (2%)
  local copies, waits for them, and re-layouts  4.89 us (1%)
  other arithmetic  4.74 us (1%)
    all_to_all x4, waiting for transfers between devices, local(): lax.all_to_all(adapted.reshape(in_shape), 'hst', split_axis=0, concat_axi...  69.7 us
    all_to_all x1, waiting for transfers between devices, local(): lax.all_to_all(send_a, 'hst', split_axis=0, concat_axis=0, tiled=True)  62.1 us
    all_to_all x4, waiting for transfers between devices, local(): lax.all_to_all(outgoing, 'hst', split_axis=0, concat_axis=0, tiled=True)  54.2 us
    all_to_all x1, waiting for transfers between devices, local(): lax.all_to_all(send_b, 'hst', split_axis=0, concat_axis=0, tiled=True)  52.6 us
    all_to_all x4, waiting for transfers between devices, local(): lax.all_to_all(slot_sent, 'hst', split_axis=0, concat_axis=0, tiled=True)  16.9 us
    all_to_all x4, starting transfers between devices, local(): lax.all_to_all(outgoing, 'hst', split_axis=0, concat_axis=0, tiled=True)  16.1 us
    all_to_all x4, starting transfers between devices, local(): lax.all_to_all(adapted.reshape(in_shape), 'hst', split_axis=0, concat_axi...  16.1 us
    all_to_all x4, starting transfers between devices, local(): lax.all_to_all(slot_sent, 'hst', split_axis=0, concat_axis=0, tiled=True)  16 us
  transfers between devices with their start and end apart: 14, of which 14 were waited for; matrix products, arithmetic and copies ran while one was open for 11% of the time, Pallas kernels for 0%

commit v1 on v0

v1 whole, which is shorter than its diff:
```python
import jax
import jax.numpy as jnp
from jax import lax
from jax.sharding import PartitionSpec as P

FIRST_ROUNDS = 2


def local(
    activations,
    shrink_weight,
    expand_weight,
    former_layout_list,
    host_layout_list,
    target_host,
    target_position,
):
    host_count = lax.axis_size("hst")
    shares = lax.axis_size("mp")
    local_adapters, rank_extent, width = shrink_weight.shape
    steps, step_rows, _ = activations.shape
    rows = steps * step_rows
    table_size = former_layout_list.shape[0]
    block = 8 * -(-3 * rows // (4 * host_count * 8))
    slots = block - 1

    flat_x = activations.reshape(rows, width)
    flat_a = shrink_weight.reshape(local_adapters * rank_extent, width)
    flat_b = expand_weight.reshape(local_adapters * rank_extent, width)

    table = jnp.arange(table_size, dtype=jnp.int32)
    source = jnp.sum(
        jnp.where(host_layout_list[:, None] == former_layout_list[None, :], table[None, :], 0),
        axis=1,
    )
    wanted = (target_host[:, :, 0] * local_adapters + target_position).reshape(rows)
    served = jnp.sum(jnp.where(wanted[:, None] == table[None, :], source[None, :], 0), axis=1)
    owner = served // local_adapters
    within = served % local_adapters

    hosts = jnp.arange(host_count, dtype=jnp.int32)
    by_owner = owner[:, None] == hosts[None, :]
    row_ids = jnp.arange(rows, dtype=jnp.int32)
    earlier = (row_ids[None, :] < row_ids[:, None]).astype(jnp.bfloat16)
    before = jnp.dot(
        earlier, by_owner.astype(jnp.bfloat16), preferred_element_type=jnp.float32
    ).astype(jnp.int32)
    row_rank = jnp.sum(jnp.where(by_owner, before, 0), axis=1)
    rounds = lax.pmax(jnp.max(row_rank) // slots + 1, ("groups", "hst", "mp", "rep"))

    place_owner = jnp.repeat(hosts, block)
    place_slot = jnp.tile(jnp.arange(block, dtype=jnp.int32), host_count)
    is_slot = place_slot < slots
    adapters = jnp.arange(local_adapters, dtype=jnp.int32)
    columns = jnp.arange(width, dtype=jnp.int32)

    def place(number):
        chosen = (
            (place_owner[:, None] == owner[None, :])
            & (place_slot[:, None] + number * slots == row_rank[None, :])
            & is_slot[:, None]
        )
        return chosen.astype(jnp.bfloat16)

    def send(number):
        placer = place(number)
        column_slot = number * slots + columns
        named = jnp.sum(
            jnp.where(
                (owner[:, None, None] == hosts[None, :, None])
                & (row_rank[:, None, None] == column_slot[None, None, :slots]),
                (within + 1)[:, None, None],
                0,
            ),
            axis=0,
        )
        named = jnp.pad(named.astype(jnp.float32), ((0, 0), (0, width - slots)))
        sent = jnp.dot(placer, flat_x, preferred_element_type=jnp.float32)
        sent = sent.reshape(host_count, block, width) + jnp.where(
            (jnp.arange(block) == slots)[None, :, None], named[:, None, :], 0.0
        )
        return lax.all_to_all(
            sent.astype(jnp.bfloat16), "hst", split_axis=0, concat_axis=0, tiled=True
        )

    def serve(received):
        named = received[:, slots, :block].astype(jnp.int32)
        named = jnp.where(jnp.arange(block)[None, :] < slots, named, 0).reshape(-1)
        mask = named[:, None] == adapters[None, :] + 1
        partial = lax.dot_general(
            received.reshape(-1, width),
            flat_a,
            (((1,), (1,)), ((), ())),
            preferred_element_type=jnp.float32,
        )
        partial = jnp.sum(
            jnp.where(
                mask[:, :, None], partial.reshape(-1, local_adapters, rank_extent), 0.0
            ),
            axis=1,
        )
        total = partial
        for hop in range(1, shares):
            total = total + lax.ppermute(
                partial, "mp", [(i, (i + hop) % shares) for i in range(shares)]
            )
        shrink = total.astype(jnp.bfloat16)
        spread = jnp.where(mask[:, :, None], shrink[:, None, :], 0).reshape(
            -1, local_adapters * rank_extent
        )
        adapted = jnp.dot(spread, flat_b, preferred_element_type=jnp.float32)
        return lax.all_to_all(
            adapted.astype(jnp.bfloat16).reshape(received.shape),
            "hst",
            split_axis=0,
            concat_axis=0,
            tiled=True,
        )

    def back(number, returned):
        return lax.dot_general(
            place(number),
            returned.reshape(-1, width),
            (((0,), (0,)), ((), ())),
            preferred_element_type=jnp.float32,
        )

    sent = [send(number) for number in range(FIRST_ROUNDS)]
    returned = [serve(received) for received in sent]
    result = back(0, returned[0]).astype(jnp.bfloat16)
    for number in range(1, FIRST_ROUNDS):
        result = (back(number, returned[number]) + result).astype(jnp.bfloat16)

    def more(state):
        number, so_far = state
        added = back(number, serve(send(number)))
        return number + 1, (added + so_far).astype(jnp.bfloat16)

    _, result = lax.while_loop(
        lambda state: state[0] < rounds, more, (jnp.int32(FIRST_ROUNDS), result)
    )
    return result.reshape(steps, step_rows, width)


def solution(mesh):
    return jax.shard_map(
        local,
        mesh=mesh,
        in_specs=(
            P(None, ("groups", "hst", "rep"), "mp"),
            P("hst", None, "mp"),
            P("hst", None, "mp"),
            P("groups"),
            P("groups"),
            P(None, ("groups", "hst", "rep"), None),
            P(None, ("groups", "hst", "rep")),
        ),
        out_specs=P(None, ("groups", "hst", "rep"), "mp"),
        check_vma=False,
    )
```

time: 377 us -> 177 us (0.47)
  waiting for transfers between devices: 255 us -> 71.6 us
  blocking collectives: 8.4 us -> 45.8 us
  starting transfers between devices: 56.7 us -> 20 us
  matrix products: 45.4 us -> 29.4 us
    all_to_all x14 -> x4, waiting for transfers between devices: 255 us -> 67.1 us  [the longest x2 53.3 us: send(): lax.all_to_all(sent.astype(jnp.bfloat16), 'hst', split_axis=0, concat_axi...]
    pmax x0 -> x1, blocking collectives: none -> 45.8 us  [local(): lax.pmax(jnp.max(row_rank) // slots + 1, ('groups', 'hst', 'mp', 'rep'))]
    all_to_all x14 -> x4, starting transfers between devices: 56.7 us -> 16.9 us  [the longest x2 9.85 us: send(): lax.all_to_all(sent.astype(jnp.bfloat16), 'hst', split_axis=0, concat_axi...]
    dot_general x24 -> x9, matrix products: 45.4 us -> 29.4 us  [the longest x2 10 us: serve(): adapted = jnp.dot(spread, flat_b, preferred_element_type=jnp.float32)]
    psum x1 -> x0, blocking collectives: 8.4 us -> none  [local(): summed = lax.psum(reduced, 'mp')]
    ppermute x0 -> x2, waiting for transfers between devices: none -> 4.49 us  [serve(): lax.ppermute(partial, 'mp', [(i, (i + hop) % shares) for i in range(share...]
  transfers between devices with their start and end apart: 14 -> 6, of which waited for: 14 -> 5; matrix products, arithmetic and copies ran while one was open for 11% -> 9% of each run, Pallas kernels for 0% -> 0%
where the time goes in v1:
time: 177 us; the launch traced here: 176 us
  waiting for transfers between devices  71.6 us (40%)
  blocking collectives  45.8 us (26%)
  matrix products  29.4 us (17%)
  starting transfers between devices  20 us (11%)
  other arithmetic  4.32 us (2%)
  between operations  2.12 us (1%)
  local copies, waits for them, and re-layouts  1.85 us (1%)
    all_to_all x2, waiting for transfers between devices, send(): lax.all_to_all(sent.astype(jnp.bfloat16), 'hst', split_axis=0, concat_axi...  53.3 us
    pmax x1, blocking collectives, local(): lax.pmax(jnp.max(row_rank) // slots + 1, ('groups', 'hst', 'mp', 'rep'))  45.8 us
    all_to_all x2, waiting for transfers between devices, serve(): lax.all_to_all(adapted.astype(jnp.bfloat16).reshape(received.shape), 'hst...  13.9 us
    dot_general x2, matrix products, serve(): adapted = jnp.dot(spread, flat_b, preferred_element_type=jnp.float32)  10 us
    all_to_all x2, starting transfers between devices, send(): lax.all_to_all(sent.astype(jnp.bfloat16), 'hst', split_axis=0, concat_axi...  9.85 us
    dot_general x2, matrix products, serve(): lax.dot_general(received.reshape(-1, width), flat_a, (((1,), (1,)), ((),...  8.27 us
    all_to_all x2, starting transfers between devices, serve(): lax.all_to_all(adapted.astype(jnp.bfloat16).reshape(received.shape), 'hst...  7.06 us
    dot_general x2, matrix products, send(): sent = jnp.dot(placer, flat_x, preferred_element_type=jnp.float32)  5.89 us
  transfers between devices with their start and end apart: 6, of which 5 were waited for; matrix products, arithmetic and copies ran while one was open for 9% of the time, Pallas kernels for 0%

profile of v1, /device:TPU:0, one launch (start us, length us, event | category | flops | bytes accessed | tf_op | source)
XLA Modules:
  0.0 175.8 jit_solution(16249033582413766075)
XLA Ops:
  0.0 0.7 bitcast_add_fusion
  0.7 0.1 eq.421
  0.8 0.8 select_reduce_fusion.4
  1.6 0.2 select_reduce_fusion.3
  1.8 0.2 fusion.58
  2.1 0.1 broadcast_compare_fusion.3
  2.2 1.7 select_reduce_fusion.2
  3.9 0.1 copy.35
  4.0 2.9 %fusion.36 = bf16[4,48,3072]{2,1,0:T(8,128)(2,1)} fusion(bf16[256,3072,1]{1,0,2:T(8,128)(2,1)} %bitcast.4, f32[4,3072]{1,0:T(4,128)S(1)} %pad.15.clone, pred[48]{0:T(512)(128)(4,1)S(1)} %iota_compare_fusion.11, s32[256]{0:T(256)S(1)} %fusion.58, s32[256]{0:T(256)S(1)} %get-tuple-element.311, pred[4,48]{1,0:T(4,128)(4,1)S(1)} %iota_compare_fusion.10), kind=kOutput, calls=%fused_computation.51 | convolution fusion | flops 303955968 | bytes 2803952 | tf_op jit(solution)/shard_map/dot_general | solution.py:78
  6.9 6.3 %all-to-all-start.4 = ((bf16[4,48,3072]{2,1,0:T(8,128)(2,1)}), bf16[4,48,3072]{2,1,0:T(8,128)(2,1)S(1)}, u32[]{:S(2)}, u32[]{:S(2)}) async-start(bf16[4,48,3072]{2,1,0:T(8,128)(2,1)} %fusion.36), calls=%async_computation.4 | async-start | bytes 2359296 | tf_op jit(solution)/shard_map/all_to_all | solution.py:82
  13.2 0.1 copy.34
  13.3 2.9 %fusion.35 = bf16[4,48,3072]{2,1,0:T(8,128)(2,1)} fusion(bf16[256,3072,1]{1,0,2:T(8,128)(2,1)} %bitcast.4, f32[4,3072]{1,0:T(4,128)S(1)} %pad.14.clone, pred[48]{0:T(512)(128)(4,1)S(1)} %iota_compare_fusion.11, s32[256]{0:T(256)S(1)} %fusion.58, s32[4,48]{1,0:T(4,128)S(1)} %iota_add_fusion.2, s32[256]{0:T(256)S(1)} %get-tuple-element.311, ...), kind=kOutput, calls=%fused_computation.50 | convolution fusion | flops 303955968 | bytes 2804720 | tf_op jit(solution)/shard_map/dot_general | solution.py:78
  16.3 25.5 %all-to-all-done.4 = bf16[4,48,3072]{2,1,0:T(8,128)(2,1)S(1)} async-done(((bf16[4,48,3072]{2,1,0:T(8,128)(2,1)}), bf16[4,48,3072]{2,1,0:T(8,128)(2,1)S(1)}, u32[]{:S(2)}, u32[]{:S(2)}) %all-to-all-start.4) | async-done | bytes 1179680 | tf_op jit(solution)/shard_map/all_to_all | solution.py:82
  41.8 3.5 %all-to-all-start.2 = ((bf16[4,48,3072]{2,1,0:T(8,128)(2,1)}), bf16[4,48,3072]{2,1,0:T(8,128)(2,1)S(1)}, u32[]{:S(2)}, u32[]{:S(2)}) async-start(bf16[4,48,3072]{2,1,0:T(8,128)(2,1)} %fusion.35), calls=%async_computation.2 | async-start | bytes 2359296 | tf_op jit(solution)/shard_map/all_to_all | solution.py:82
  45.3 0.1 broadcast_in_dim.316
  45.4 0.1 reshape.594
  45.5 27.8 %all-to-all-done.2 = bf16[4,48,3072]{2,1,0:T(8,128)(2,1)S(1)} async-done(((bf16[4,48,3072]{2,1,0:T(8,128)(2,1)}), bf16[4,48,3072]{2,1,0:T(8,128)(2,1)S(1)}, u32[]{:S(2)}, u32[]{:S(2)}) %all-to-all-start.2) | async-done | bytes 1179680 | tf_op jit(solution)/shard_map/all_to_all | solution.py:82
  73.3 0.1 reshape.593
  73.4 0.1 broadcast_compare_fusion.6
  73.5 4.1 %fusion.51 = f32[192,16]{0,1:T(8,128)S(1)} fusion(bf16[192,3072,1]{1,0,2:T(8,128)(2,1)S(1)} %bitcast.80, bf16[32,16,3072]{2,1,0:T(8,128)(2,1)} %param.10, pred[192,32]{0,1:T(8,128)(4,1)S(1)} %get-tuple-element.247), kind=kOutput, calls=%fused_computation.62 | convolution fusion | flops 604173312 | bytes 4343808 | tf_op jit(solution)/shard_map/dot_general | solution.py:90
  77.6 1.6 collective-permute-start.2
  79.2 2.2 %collective-permute-done.2 = f32[192,16]{0,1:T(8,128)S(1)} collective-permute-done((f32[192,16]{0,1:T(8,128)S(1)}, f32[192,16]{0,1:T(8,128)S(1)}, u32[]{:S(2)}, u32[]{:S(2)}) %collective-permute-start.2) | collective-permute-done | bytes 12320 | tf_op jit(solution)/shard_map/ppermute | solution.py:104
  81.5 5.0 %fusion.38 = bf16[192,3072]{1,0:T(8,128)(2,1)} fusion(bf16[32,16,3072]{2,1,0:T(8,128)(2,1)} %param.11, pred[192,32]{0,1:T(8,128)(4,1)S(1)} %get-tuple-element.247, bf16[192,16]{0,1:T(8,128)(2,1)S(1)} %add_convert_fusion.2), kind=kOutput, calls=%fused_computation.53 | convolution fusion | flops 604667904 | bytes 4337664 | tf_op jit(solution)/shard_map/dot_general | solution.py:111
  86.5 3.5 %all-to-all-start.5 = ((bf16[4,48,3072]{2,1,0:T(8,128)(2,1)}), bf16[4,48,3072]{2,1,0:T(8,128)(2,1)S(1)}, u32[]{:S(2)}, u32[]{:S(2)}) async-start(bf16[4,48,3072]{2,1,0:T(8,128)(2,1)} %bitcast.15), calls=%async_computation.5 | async-start | bytes 2359296 | tf_op jit(solution)/shard_map/all_to_all | solution.py:112
  90.0 4.1 %fusion.54 = f32[192,16]{0,1:T(8,128)S(1)} fusion(bf16[192,3072,1]{1,0,2:T(8,128)(2,1)S(1)} %bitcast.81, bf16[32,16,3072]{2,1,0:T(8,128)(2,1)} %param.10, pred[192,32]{0,1:T(8,128)(4,1)S(1)} %get-tuple-element.246), kind=kOutput, calls=%fused_computation.63 | convolution fusion | flops 604173312 | bytes 4343808 | tf_op jit(solution)/shard_map/dot_general | solution.py:90
  94.1 1.6 collective-permute-start.1
  95.7 2.2 %collective-permute-done.1 = f32[192,16]{0,1:T(8,128)S(1)} collective-permute-done((f32[192,16]{0,1:T(8,128)S(1)}, f32[192,16]{0,1:T(8,128)S(1)}, u32[]{:S(2)}, u32[]{:S(2)}) %collective-permute-start.1) | collective-permute-done | bytes 12320 | tf_op jit(solution)/shard_map/ppermute | solution.py:104
  97.9 5.0 %fusion.37 = bf16[192,3072]{1,0:T(8,128)(2,1)} fusion(bf16[32,16,3072]{2,1,0:T(8,128)(2,1)} %param.11, pred[192,32]{0,1:T(8,128)(4,1)S(1)} %get-tuple-element.246, bf16[192,16]{0,1:T(8,128)(2,1)S(1)} %add_convert_fusion.3), kind=kOutput, calls=%fused_computation.52 | convolution fusion | flops 604667904 | bytes 4337664 | tf_op jit(solution)/shard_map/dot_general | solution.py:111
  103.0 13.9 %all-to-all-done.5 = bf16[4,48,3072]{2,1,0:T(8,128)(2,1)S(1)} async-done(((bf16[4,48,3072]{2,1,0:T(8,128)(2,1)}), bf16[4,48,3072]{2,1,0:T(8,128)(2,1)S(1)}, u32[]{:S(2)}, u32[]{:S(2)}) %all-to-all-start.5) | async-done | bytes 1179680 | tf_op jit(solution)/shard_map/all_to_all | solution.py:112
  116.8 3.5 %all-to-all-start.3 = ((bf16[4,48,3072]{2,1,0:T(8,128)(2,1)}), bf16[4,48,3072]{2,1,0:T(8,128)(2,1)S(1)}, u32[]{:S(2)}, u32[]{:S(2)}) async-start(bf16[4,48,3072]{2,1,0:T(8,128)(2,1)} %bitcast.82), calls=%async_computation.3 | async-start | bytes 2359296 | tf_op jit(solution)/shard_map/all_to_all | solution.py:112
  120.4 0.6 reduce_max.9
  123.0 45.8 %pmax.7 = s32[]{:T(128)} all-reduce(s32[]{:T(128)S(6)} %add.177), channel_id=1, replica_groups=mesh['groups'=2,'hst'=4,'mp'=2,'rep'=2] {'groups','hst','mp','rep'}, use_global_device_ids=true, to_apply=%region_8.9 | all-reduce | flops 1 | bytes 8 | tf_op jit(solution)/shard_map/pmax | solution.py:49
  168.7 0.1 broadcast_in_dim_tile.16
  168.8 0.1 eq.419
  168.9 2.4 %fusion.34 = f32[256,3072]{1,0:T(8,128)} fusion(bf16[192,3072]{1,0:T(8,128)(2,1)S(1)} %bitcast.78, s32[256]{0:T(256)S(1)} %fusion.58, s32[256]{0:T(256)S(1)} %get-tuple-element.311, s32[192]{0:T(256)S(1)} %broadcast_in_dim_tile.16, s32[192]{0:T(256)S(1)} %eq.419, pred[192]{0:T(512)(128)(4,1)S(1)} %broadcast_compare_fusion.7), kind=kOutput, calls=%fused_computation.47 | convolution fusion | flops 303759360 | bytes 4329152 | tf_op jit(solution)/shard_map/dot_general | solution.py:121
  171.3 0.0 all-to-all-done.3
  171.3 2.7 %fusion.33 = bf16[256,3072]{1,0:T(8,128)(2,1)S(1)} fusion(f32[256,3072]{1,0:T(8,128)} %fusion.34, bf16[192,3072]{1,0:T(8,128)(2,1)S(1)} %bitcast.79, s32[256]{0:T(256)S(1)} %fusion.58, s32[256]{0:T(256)S(1)} %get-tuple-element.311, s32[192]{0:T(256)S(1)} %broadcast_add_fusion.1, s32[192]{0:T(256)S(1)} %eq.419, pred[192]{0:T(512)(128)(4,1)S(1)} %broadcast_compare_fusion.7), kind=kOutput, calls=%fused_computation.45 | convolution fusion | flops 303759360 | bytes 5902016 | tf_op jit(solution)/shard_map/dot_general | solution.py:121
  174.0 0.6 while.13
  174.6 0.0 copy-start
  174.6 1.1 copy-done
  (22 shorter events, 0.2 us)
Async XLA Ops:
  6.9 34.9 %all-to-all-start.4 = ((bf16[4,48,3072]{2,1,0:T(8,128)(2,1)}), bf16[4,48,3072]{2,1,0:T(8,128)(2,1)S(1)}, u32[]{:S(2)}, u32[]{:S(2)}) async-start(bf16[4,48,3072]{2,1,0:T(8,128)(2,1)} %fusion.36), calls=%async_computation.4 | async-start | bytes 2359296 | tf_op jit(solution)/shard_map/all_to_all | solution.py:82
  41.8 31.5 %all-to-all-start.2 = ((bf16[4,48,3072]{2,1,0:T(8,128)(2,1)}), bf16[4,48,3072]{2,1,0:T(8,128)(2,1)S(1)}, u32[]{:S(2)}, u32[]{:S(2)}) async-start(bf16[4,48,3072]{2,1,0:T(8,128)(2,1)} %fusion.35), calls=%async_computation.2 | async-start | bytes 2359296 | tf_op jit(solution)/shard_map/all_to_all | solution.py:82
  77.6 3.8 %collective-permute-start.2 = (f32[192,16]{0,1:T(8,128)S(1)}, f32[192,16]{0,1:T(8,128)S(1)}, u32[]{:S(2)}, u32[]{:S(2)}) collective-permute-start(f32[192,16]{0,1:T(8,128)S(1)} %fusion.51), channel_id=1, source_target_pairs={{0,2},{2,0},{1,3},{3,1},{4,6},{6,4},{5,7},{7,5},{8,10},{10,8},{9,1... | collective-permute-start | bytes 36872 | tf_op jit(solution)/shard_map/ppermute | solution.py:104
  86.5 30.4 %all-to-all-start.5 = ((bf16[4,48,3072]{2,1,0:T(8,128)(2,1)}), bf16[4,48,3072]{2,1,0:T(8,128)(2,1)S(1)}, u32[]{:S(2)}, u32[]{:S(2)}) async-start(bf16[4,48,3072]{2,1,0:T(8,128)(2,1)} %bitcast.15), calls=%async_computation.5 | async-start | bytes 2359296 | tf_op jit(solution)/shard_map/all_to_all | solution.py:112
  94.1 3.8 %collective-permute-start.1 = (f32[192,16]{0,1:T(8,128)S(1)}, f32[192,16]{0,1:T(8,128)S(1)}, u32[]{:S(2)}, u32[]{:S(2)}) collective-permute-start(f32[192,16]{0,1:T(8,128)S(1)} %fusion.54), channel_id=1, source_target_pairs={{0,2},{2,0},{1,3},{3,1},{4,6},{6,4},{5,7},{7,5},{8,10},{10,8},{9,1... | collective-permute-start | bytes 36872 | tf_op jit(solution)/shard_map/ppermute | solution.py:104
  116.8 54.5 %all-to-all-start.3 = ((bf16[4,48,3072]{2,1,0:T(8,128)(2,1)}), bf16[4,48,3072]{2,1,0:T(8,128)(2,1)S(1)}, u32[]{:S(2)}, u32[]{:S(2)}) async-start(bf16[4,48,3072]{2,1,0:T(8,128)(2,1)} %bitcast.82), calls=%async_computation.3 | async-start | bytes 2359296 | tf_op jit(solution)/shard_map/all_to_all | solution.py:112
  174.6 1.1 copy-start

commit v2 on v1

v2 whole, which is shorter than its diff:
```python
import jax
import jax.numpy as jnp
from jax import lax
from jax.sharding import PartitionSpec as P

MOST_SHIFTS = 8
LANES = 128


def round_up(value, unit):
    return unit * -(-value // unit)


def local(
    activations,
    shrink_weight,
    expand_weight,
    former_layout_list,
    host_layout_list,
    target_host,
    target_position,
):
    host_count = lax.axis_size("hst")
    shares = lax.axis_size("mp")
    me = lax.axis_index("hst")
    local_adapters, rank_extent, width = shrink_weight.shape
    steps, step_rows, _ = activations.shape
    rows = steps * step_rows
    spots = local_adapters * rank_extent
    folded = LANES if spots % LANES == 0 and LANES % rank_extent == 0 else spots
    table_size = former_layout_list.shape[0]
    by_shift = host_count <= MOST_SHIFTS
    first_block = round_up(11 * rows // (8 * host_count), 8)
    more_block = min(first_block, 16)

    flat_x = activations.reshape(rows, width)
    flat_a = shrink_weight.reshape(spots, width)
    flat_b = expand_weight.reshape(spots, width)

    table = jnp.arange(table_size, dtype=jnp.int32)
    source = jnp.sum(
        jnp.where(host_layout_list[:, None] == former_layout_list[None, :], table[None, :], 0),
        axis=1,
    )
    wanted = (target_host[:, :, 0] * local_adapters + target_position).reshape(rows)
    served = jnp.sum(jnp.where(wanted[:, None] == table[None, :], source[None, :], 0), axis=1)
    owner = served // local_adapters
    named_row = served % local_adapters + 1
    ahead = lax.rem(owner - me + host_count, host_count)
    key = ahead if by_shift else jnp.where(ahead == 0, host_count, owner)

    hosts = jnp.arange(host_count, dtype=jnp.int32)
    in_block = key[:, None] == hosts[None, :]
    row_ids = jnp.arange(rows, dtype=jnp.int32)
    earlier = (row_ids[None, :] < row_ids[:, None]).astype(jnp.bfloat16)
    before = jnp.dot(
        earlier, in_block.astype(jnp.bfloat16), preferred_element_type=jnp.float32
    ).astype(jnp.int32)
    row_rank = jnp.sum(jnp.where(in_block, before, 0), axis=1)
    left = jnp.max(jnp.where(ahead == 0, 0, row_rank + 1)) - (first_block - 1)
    own_rounds = jnp.maximum(0, (left + more_block - 2) // (more_block - 1))

    columns = jnp.arange(width, dtype=jnp.int32)
    spot_adapter = jnp.arange(spots, dtype=jnp.int32) // rank_extent + 1

    def place(member, start, block):
        slot = jnp.arange(block, dtype=jnp.int32)[:, None]
        chosen = (
            (key[None, :] == member)
            & (slot + start == row_rank[None, :])
            & (slot < block - 1)
        )
        return chosen

    def pack(member, start, block):
        chosen = place(member, start, block)
        at_column = (key[:, None] == member) & (row_rank[:, None] == columns[None, :LANES] + start)
        names = jnp.sum(jnp.where(at_column, named_row[:, None], 0), axis=0)
        lane = columns[:LANES]
        names = jnp.where(lane < block - 1, names, jnp.where(lane == block - 1, own_rounds, 0))
        names = jnp.pad(names.astype(jnp.float32), (0, width - LANES))
        rows_out = jnp.dot(chosen.astype(jnp.bfloat16), flat_x, preferred_element_type=jnp.float32)
        last = (jnp.arange(block) == block - 1)[:, None]
        return jnp.where(last, names[None, :], rows_out).astype(jnp.bfloat16)

    def swap(values, step):
        return lax.ppermute(
            values, "hst", [(i, (i + step) % host_count) for i in range(host_count)]
        )

    def exchange(values):
        split = values.reshape(host_count, -1, values.shape[-1])
        split = lax.all_to_all(split, "hst", split_axis=0, concat_axis=0, tiled=True)
        return split.reshape(values.shape)

    def fold(values):
        parts = [values[:, i : i + folded] for i in range(0, spots, folded)]
        total = parts[0]
        for part in parts[1:]:
            total = total + part
        return total

    def adapt(inputs, names):
        mask = names[:, None] == spot_adapter[None, :]
        partial = lax.dot_general(
            inputs, flat_a, (((1,), (1,)), ((), ())), preferred_element_type=jnp.float32
        )
        partial = fold(jnp.where(mask, partial, 0.0))
        total = partial
        for hop in range(1, shares):
            total = total + lax.ppermute(
                partial, "mp", [(i, (i + hop) % shares) for i in range(shares)]
            )
        shrink = jnp.tile(total.astype(jnp.bfloat16), (1, spots // folded))
        spread = jnp.where(mask, shrink, 0)
        return jnp.dot(spread, flat_b, preferred_element_type=jnp.float32)

    def serve(received, block):
        names = received.reshape(-1, block, width)[:, block - 1, :LANES].astype(jnp.int32)
        rounds = jnp.max(names[:, block - 1])
        names = jnp.where(jnp.arange(block)[None, :] < block - 1, names[:, :block], 0)
        return adapt(received, names.reshape(-1)).astype(jnp.bfloat16), rounds

    def back(member, start, block, returned):
        return lax.dot_general(
            place(member, start, block).astype(jnp.bfloat16),
            returned,
            (((0,), (0,)), ((), ())),
            preferred_element_type=jnp.float32,
        )

    def one_round(start, block, base):
        if not by_shift:
            packed = jnp.concatenate([pack(member, start, block) for member in range(host_count)])
            adapted, rounds = serve(exchange(packed), block)
            returned = exchange(adapted).reshape(host_count, block, width)
            for member in range(host_count):
                base = base + back(member, start, block, returned[member])
            return base.astype(jnp.bfloat16), jnp.maximum(rounds, own_rounds)
        order = sorted(range(1, host_count), key=lambda s: min(s, host_count - s))
        received = {s: swap(pack(s, start, block), s) for s in order}
        rounds = own_rounds
        returned = {}
        for s in order:
            adapted, theirs = serve(received[s], block)
            rounds = jnp.maximum(rounds, theirs)
            returned[s] = swap(adapted, host_count - s)
        for s in order:
            base = (base + back(s, start, block, returned[s])).astype(jnp.bfloat16)
        return base, rounds

    own = adapt(flat_x, jnp.where(ahead == 0, named_row, 0)).astype(jnp.bfloat16)
    result, rounds = one_round(0, first_block, own)
    rounds = jnp.full((1, LANES), rounds, jnp.int32)
    for axis in ("rep", "groups"):
        size = lax.axis_size(axis)
        most = rounds
        for hop in range(1, size):
            most = jnp.maximum(
                most, lax.ppermute(rounds, axis, [(i, (i + hop) % size) for i in range(size)])
            )
        rounds = most

    def more(state):
        number, so_far = state
        start = first_block - 1 + number * (more_block - 1)
        so_far, _ = one_round(start, more_block, so_far)
        return number + 1, so_far

    _, result = lax.while_loop(
        lambda state: state[0] < rounds[0, 0], more, (jnp.int32(0), result)
    )
    return result.reshape(steps, step_rows, width)


def solution(mesh):
    return jax.shard_map(
        local,
        mesh=mesh,
        in_specs=(
            P(None, ("groups", "hst", "rep"), "mp"),
            P("hst", None, "mp"),
            P("hst", None, "mp"),
            P("groups"),
            P("groups"),
            P(None, ("groups", "hst", "rep"), None),
            P(None, ("groups", "hst", "rep")),
        ),
        out_specs=P(None, ("groups", "hst", "rep"), "mp"),
        check_vma=False,
    )
```

time: 177 us -> 130 us (0.73)
  the two profiles are of different devices: /device:TPU:0 before, /device:TPU:24 now
where the time goes in v2:
time: 130 us
  waiting for transfers between devices  75.9 us (58%)
  matrix products  20.8 us (16%)
  starting transfers between devices  17.4 us (13%)
  other arithmetic  9.96 us (8%)
  between operations  2.98 us (2%)
  local copies, waits for them, and re-layouts  2.01 us (2%)
    ppermute x6, waiting for transfers between devices, swap(): lax.ppermute(values, 'hst', [(i, (i + step) % host_count) for i in range(...  74.5 us
    ppermute x6, starting transfers between devices, swap(): lax.ppermute(values, 'hst', [(i, (i + step) % host_count) for i in range(...  11.2 us
    dot_general x4, matrix products, adapt(): lax.dot_general(inputs, flat_a, (((1,), (1,)), ((), ())), preferred_eleme...  7.87 us
    dot_general x4, matrix products, adapt(): return jnp.dot(spread, flat_b, preferred_element_type=jnp.float32)  4.62 us
    ppermute x4, starting transfers between devices, adapt(): lax.ppermute(partial, 'mp', [(i, (i + hop) % shares) for i in range(share...  4.48 us
    dot_general x3, matrix products, pack(): jnp.dot(chosen.astype(jnp.bfloat16), flat_x, preferred_element_type=jnp.f...  4.12 us
    dot_general x3, matrix products, back(): lax.dot_general(place(member, start, block).astype(jnp.bfloat16), returne...  3.26 us
  transfers between devices with their start and end apart: 12, of which 5 were waited for; matrix products, arithmetic and copies ran while one was open for 15% of the time, Pallas kernels for 0%

profile of v2, /device:TPU:24, one launch (start us, length us, event | category | flops | bytes accessed | tf_op | source)
XLA Modules:
  0.0 129.9 jit_solution(713174089716377457)
XLA Ops:
  0.0 0.9 bitcast_add_fusion
  0.9 0.1 eq.563
  0.9 0.9 select_reduce_fusion.7
  1.8 0.2 select_reduce_fusion.6
  2.0 0.6 broadcast_select_fusion
  2.6 1.0 fusion.81
  3.6 1.3 %select_reduce_fusion.8 = s32[]{:T(128)} fusion(s32[256]{0:T(256)S(1)} %fusion.81, s32[256]{0:T(256)} %get-tuple-element.380), kind=kLoop, calls=%fused_computation.237 | loop fusion | flops 1023 | bytes 2052 | tf_op jit(solution)/shard_map/reduce_max | solution.py:60
  5.6 0.7 broadcast_compare_fusion.4
  6.3 0.3 select_reduce_fusion.5
  6.6 1.8 %fusion.79 = bf16[88,3072]{1,0:T(8,128)(2,1)S(1)} fusion(bf16[256,3072]{1,0:T(8,128)(2,1)} %bitcast.190, bf16[3072]{0:T(1024)(128)(2,1)S(1)} %pad.31, pred[88]{0:T(512)(128)(4,1)S(1)} %get-tuple-element.285, s32[256]{0:T(256)S(1)} %fusion.81, pred[88]{0:T(512)(128)(4,1)S(1)} %get-tuple-element.286, pred[256]{0:T(512)(128)(4,1)S(1)} %get-tuple-element.280), kind=kOutput, calls=%fused_computation.137 | convolution fusion | flops 138749952 | bytes 2121136 | tf_op jit(solution)/shard_map/dot_general | solution.py:82
  8.4 0.4 collective-permute-start.16
  8.8 1.8 %fusion.78 = bf16[88,3072]{1,0:T(8,128)(2,1)S(1)} fusion(bf16[256,3072]{1,0:T(8,128)(2,1)} %bitcast.191, bf16[3072]{0:T(1024)(128)(2,1)S(1)} %pad.30, pred[88]{0:T(512)(128)(4,1)S(1)} %get-tuple-element.285, s32[256]{0:T(256)S(1)} %fusion.81, pred[88]{0:T(512)(128)(4,1)S(1)} %get-tuple-element.286, pred[256]{0:T(512)(128)(4,1)S(1)} %get-tuple-element.281), kind=kOutput, calls=%fused_computation.136 | convolution fusion | flops 138749952 | bytes 2121136 | tf_op jit(solution)/shard_map/dot_general | solution.py:82
  10.7 0.2 collective-permute-start.13
  10.9 2.5 %convolution_select_fusion.9 = f32[256,512]{1,0:T(8,128)S(1)} fusion(bf16[256,3072]{1,0:T(8,128)(2,1)} %bitcast.192, bf16[512,3072]{1,0:T(8,128)(2,1)S(1)} %bitcast.187, s32[512]{0:T(512)S(1)} %fusion.123, s32[256]{0:T(256)S(1)} %get-tuple-element.266), kind=kOutput, calls=%fused_computation.138 | convolution fusion | flops 805568512 | bytes 5245952 | tf_op jit(solution)/shard_map/dot_general | solution.py:105
  13.5 1.9 %collective-permute-start.9 = (f32[256,128]{1,0:T(8,128)S(1)}, f32[256,128]{1,0:T(8,128)S(1)}, u32[]{:S(2)}, u32[]{:S(2)}) collective-permute-start(f32[256,128]{1,0:T(8,128)S(1)} %slice_add_fusion.9), channel_id=1, source_target_pairs={{0,2},{2,0},{1,3},{3,1},{4,6},{6,4},{5,7},{7,5},{8,10},{10,8},{9,1... | collective-permute-start | bytes 393224 | tf_op jit(solution)/shard_map/ppermute | solution.py:111
  15.3 0.4 fusion.77
  15.8 3.4 %collective-permute-start.10 = (bf16[88,3072]{1,0:T(8,128)(2,1)S(1)}, bf16[88,3072]{1,0:T(8,128)(2,1)S(1)}, u32[]{:S(2)}, u32[]{:S(2)}) collective-permute-start(bf16[88,3072]{1,0:T(8,128)(2,1)S(1)} %fusion.77), channel_id=1, source_target_pairs={{0,4},{4,8},{8,12},{12,0},{1,5},{5,9},{9,13},{13,1},{2,6},{6,10},{... | collective-permute-start | bytes 1622024 | tf_op jit(solution)/shard_map/ppermute | solution.py:87
  19.3 0.9 compare_select_fusion.7
  20.2 2.7 %fusion.76 = f32[256,3072]{1,0:T(8,128)} fusion(bf16[512,3072]{1,0:T(8,128)(2,1)S(1)} %bitcast.180, bf16[32,8,4,128]{3,2,1,0:T(4,128)(2,1)S(1)} %bitcast.201), kind=kOutput, calls=%fused_computation.128 | convolution fusion | flops 806879232 | bytes 6553600 | tf_op jit(solution)/shard_map/dot_general | solution.py:116
  22.8 13.3 %collective-permute-done.13 = bf16[88,3072]{1,0:T(8,128)(2,1)S(1)} collective-permute-done((bf16[88,3072]{1,0:T(8,128)(2,1)S(1)}, bf16[88,3072]{1,0:T(8,128)(2,1)S(1)}, u32[]{:S(2)}, u32[]{:S(2)}) %collective-permute-start.13) | collective-permute-done | bytes 540704 | tf_op jit(solution)/shard_map/ppermute | solution.py:87
  36.2 16.9 %collective-permute-done.10 = bf16[88,3072]{1,0:T(8,128)(2,1)S(1)} collective-permute-done((bf16[88,3072]{1,0:T(8,128)(2,1)S(1)}, bf16[88,3072]{1,0:T(8,128)(2,1)S(1)}, u32[]{:S(2)}, u32[]{:S(2)}) %collective-permute-start.10) | collective-permute-done | bytes 540704 | tf_op jit(solution)/shard_map/ppermute | solution.py:87
  53.1 0.7 slice.256
  53.7 0.5 slice.255
  54.3 0.7 slice.257
  55.0 1.1 convolution_select_fusion.10
  56.1 0.6 slice_add_fusion.12
  56.7 0.5 collective-permute-start.17
  57.2 1.1 convolution_select_fusion.11
  58.3 0.6 slice_add_fusion.15
  59.0 1.5 %collective-permute-start.14 = (f32[88,128]{1,0:T(8,128)}, f32[88,128]{1,0:T(8,128)}, u32[]{:S(2)}, u32[]{:S(2)}) collective-permute-start(f32[88,128]{1,0:T(8,128)} %slice_add_fusion.15), channel_id=1, source_target_pairs={{0,2},{2,0},{1,3},{3,1},{4,6},{6,4},{5,7},{7,5},{8,10},{10,8},{9,1... | collective-permute-start | bytes 135176 | tf_op jit(solution)/shard_map/ppermute | solution.py:111
  62.4 3.2 %convolution_select_fusion.12 = f32[88,512]{1,0:T(8,128)S(1)} fusion(bf16[88,3072]{1,0:T(8,128)(2,1)} %copy-done.9, bf16[512,3072]{1,0:T(8,128)(2,1)} %bitcast.185, s32[512]{0:T(512)S(1)} %fusion.123, s32[88]{0:T(128)S(1)} %select_bitcast_fusion.5), kind=kOutput, calls=%fused_computation.141 | convolution fusion | flops 276914176 | bytes 3869024 | tf_op jit(solution)/shard_map/dot_general | solution.py:105
  65.6 1.6 %collective-permute-start.20 = (s32[1,128]{1,0:T(1,128)S(1)}, s32[1,128]{1,0:T(1,128)S(1)}, u32[]{:S(2)}, u32[]{:S(2)}) collective-permute-start(s32[1,128]{1,0:T(1,128)S(1)} %broadcast_maximum_fusion), channel_id=1, source_target_pairs={{0,16},{16,0},{1,17},{17,1},{2,18},{18,2},{3,19},{19,3},{4,20},{20... | collective-permute-start | bytes 1544 | tf_op jit(solution)/shard_map/ppermute | solution.py:160
  67.2 0.6 collective-permute-start.11
  67.8 1.4 %collective-permute-done.20 = s32[1,128]{1,0:T(1,128)S(1)} collective-permute-done((s32[1,128]{1,0:T(1,128)S(1)}, s32[1,128]{1,0:T(1,128)S(1)}, u32[]{:S(2)}, u32[]{:S(2)}) %collective-permute-start.20) | collective-permute-done | bytes 544 | tf_op jit(solution)/shard_map/ppermute | solution.py:160
  69.2 0.5 fusion.168
  69.7 0.8 add_convert_fusion.4
  70.5 0.8 add_convert_fusion.5
  71.4 0.8 compare_select_fusion.10
  72.1 0.7 convolution_convert_fusion.5
  72.9 0.7 convolution_convert_fusion.4
  73.5 7.1 %collective-permute-start.18 = (bf16[88,3072]{1,0:T(8,128)(2,1)S(1)}, bf16[88,3072]{1,0:T(8,128)(2,1)S(1)}, u32[]{:S(2)}, u32[]{:S(2)}) collective-permute-start(bf16[88,3072]{1,0:T(8,128)(2,1)S(1)} %convolution_convert_fusion.4), channel_id=1, source_target_pairs={{0,8},{4,12},{8,0},{12,4},{1,9},{5,13},{9,1},{13,5},{2,10},{6,14},... | collective-permute-start | bytes 1622024 | tf_op jit(solution)/shard_map/ppermute | solution.py:87
  80.6 0.7 convolution_convert_fusion.6
  81.4 9.0 %collective-permute-done.15 = bf16[88,3072]{1,0:T(8,128)(2,1)S(1)} collective-permute-done((bf16[88,3072]{1,0:T(8,128)(2,1)S(1)}, bf16[88,3072]{1,0:T(8,128)(2,1)S(1)}, u32[]{:S(2)}, u32[]{:S(2)}) %collective-permute-start.15) | collective-permute-done | bytes 540704 | tf_op jit(solution)/shard_map/ppermute | solution.py:87
  90.4 0.7 fusion.99
  91.1 35.3 %collective-permute-done.18 = bf16[88,3072]{1,0:T(8,128)(2,1)S(1)} collective-permute-done((bf16[88,3072]{1,0:T(8,128)(2,1)S(1)}, bf16[88,3072]{1,0:T(8,128)(2,1)S(1)}, u32[]{:S(2)}, u32[]{:S(2)}) %collective-permute-start.18) | collective-permute-done | bytes 540704 | tf_op jit(solution)/shard_map/ppermute | solution.py:87
  126.3 0.7 fusion.96
  127.0 1.9 %fusion.75 = bf16[256,3072]{1,0:T(8,128)(2,1)} fusion(f32[256,3072]{1,0:T(8,128)S(1)} %fusion.96, f32[256,3072]{1,0:T(8,128)S(1)} %fusion.99, f32[256,3072]{1,0:T(8,128)S(1)} %copy-done.8, bf16[88,3072]{1,0:T(8,128)(2,1)S(1)} %collective-permute-done.12, s32[256]{0:T(256)S(1)} %fusion.81, pred[88]{0:T(512)(128)(4,1)S(1)} %get-tuple-element.286, ...), kind=kOutput, calls=%fused_computation.126 | convolution fusion | flops 144771072 | bytes 11552088 | tf_op jit(solution)/shard_map/dot_general | solution.py:125
  128.9 0.8 while.14
  (44 shorter events, 0.4 us)
Async XLA Ops:
  0.0 10.9 %copy-start.1 = (bf16[32,16,3072]{2,1,0:T(8,128)(2,1)S(1)}, bf16[32,16,3072]{2,1,0:T(8,128)(2,1)}, u32[]{:S(2)}) copy-start(bf16[32,16,3072]{2,1,0:T(8,128)(2,1)} %param.10) | copy-start | bytes 9437188
  8.4 45.9 %collective-permute-start.16 = (bf16[88,3072]{1,0:T(8,128)(2,1)S(1)}, bf16[88,3072]{1,0:T(8,128)(2,1)S(1)}, u32[]{:S(2)}, u32[]{:S(2)}) collective-permute-start(bf16[88,3072]{1,0:T(8,128)(2,1)S(1)} %fusion.79), channel_id=1, source_target_pairs={{0,8},{4,12},{8,0},{12,4},{1,9},{5,13},{9,1},{13,5},{2,10},{6,14},... | collective-permute-start | bytes 1622024 | tf_op jit(solution)/shard_map/ppermute | solution.py:87
  10.7 25.5 %collective-permute-start.13 = (bf16[88,3072]{1,0:T(8,128)(2,1)S(1)}, bf16[88,3072]{1,0:T(8,128)(2,1)S(1)}, u32[]{:S(2)}, u32[]{:S(2)}) collective-permute-start(bf16[88,3072]{1,0:T(8,128)(2,1)S(1)} %fusion.78), channel_id=1, source_target_pairs={{0,12},{4,0},{8,4},{12,8},{1,13},{5,1},{9,5},{13,9},{2,14},{6,2},{... | collective-permute-start | bytes 1622024 | tf_op jit(solution)/shard_map/ppermute | solution.py:87
  10.9 4.5 %copy-start.4 = (bf16[4,64,3072]{2,1,0:T(8,128)(2,1)S(1)}, bf16[4,64,3072]{2,1,0:T(8,128)(2,1)}, u32[]{:S(2)}) copy-start(bf16[4,64,3072]{2,1,0:T(8,128)(2,1)} %param.9) | copy-start | bytes 4718596
  13.4 6.7 %copy-start = (bf16[32,16,3072]{2,1,0:T(8,128)(2,1)S(1)}, bf16[32,16,3072]{2,1,0:T(8,128)(2,1)}, u32[]{:S(2)}) copy-start(bf16[32,16,3072]{2,1,0:T(8,128)(2,1)} %param.11) | copy-start | bytes 9437188
  13.5 5.8 %collective-permute-start.9 = (f32[256,128]{1,0:T(8,128)S(1)}, f32[256,128]{1,0:T(8,128)S(1)}, u32[]{:S(2)}, u32[]{:S(2)}) collective-permute-start(f32[256,128]{1,0:T(8,128)S(1)} %slice_add_fusion.9), channel_id=1, source_target_pairs={{0,2},{2,0},{1,3},{3,1},{4,6},{6,4},{5,7},{7,5},{8,10},{10,8},{9,1... | collective-permute-start | bytes 393224 | tf_op jit(solution)/shard_map/ppermute | solution.py:111
  15.8 37.3 %collective-permute-start.10 = (bf16[88,3072]{1,0:T(8,128)(2,1)S(1)}, bf16[88,3072]{1,0:T(8,128)(2,1)S(1)}, u32[]{:S(2)}, u32[]{:S(2)}) collective-permute-start(bf16[88,3072]{1,0:T(8,128)(2,1)S(1)} %fusion.77), channel_id=1, source_target_pairs={{0,4},{4,8},{8,12},{12,0},{1,5},{5,9},{9,13},{13,1},{2,6},{6,10},{... | collective-permute-start | bytes 1622024 | tf_op jit(solution)/shard_map/ppermute | solution.py:87
  20.1 34.9 %copy-start.2 = (bf16[32,16,3072]{2,1,0:T(8,128)(2,1)S(1)}, bf16[32,16,3072]{2,1,0:T(8,128)(2,1)}, u32[]{:S(2)}) copy-start(bf16[32,16,3072]{2,1,0:T(8,128)(2,1)} %param.10) | copy-start | bytes 9437188
  53.1 1.3 copy-start.9
  56.7 13.0 %collective-permute-start.17 = (f32[88,128]{1,0:T(8,128)}, f32[88,128]{1,0:T(8,128)}, u32[]{:S(2)}, u32[]{:S(2)}) collective-permute-start(f32[88,128]{1,0:T(8,128)} %slice_add_fusion.12), channel_id=1, source_target_pairs={{0,2},{2,0},{1,3},{3,1},{4,6},{6,4},{5,7},{7,5},{8,10},{10,8},{9,1... | collective-permute-start | bytes 135176 | tf_op jit(solution)/shard_map/ppermute | solution.py:111
  59.0 11.6 %collective-permute-start.14 = (f32[88,128]{1,0:T(8,128)}, f32[88,128]{1,0:T(8,128)}, u32[]{:S(2)}, u32[]{:S(2)}) collective-permute-start(f32[88,128]{1,0:T(8,128)} %slice_add_fusion.15), channel_id=1, source_target_pairs={{0,2},{2,0},{1,3},{3,1},{4,6},{6,4},{5,7},{7,5},{8,10},{10,8},{9,1... | collective-permute-start | bytes 135176 | tf_op jit(solution)/shard_map/ppermute | solution.py:111
  62.3 3.2 %collective-permute-start.19 = (s32[1,128]{1,0:T(1,128)S(1)}, s32[1,128]{1,0:T(1,128)S(1)}, u32[]{:S(2)}, u32[]{:S(2)}) collective-permute-start(s32[1,128]{1,0:T(1,128)S(1)} %broadcast_in_dim.359), channel_id=1, source_target_pairs={{0,1},{1,0},{2,3},{3,2},{4,5},{5,4},{6,7},{7,6},{8,9},{9,8},{10,11... | collective-permute-start | bytes 1544 | tf_op jit(solution)/shard_map/ppermute | solution.py:160
  65.6 3.6 %collective-permute-start.20 = (s32[1,128]{1,0:T(1,128)S(1)}, s32[1,128]{1,0:T(1,128)S(1)}, u32[]{:S(2)}, u32[]{:S(2)}) collective-permute-start(s32[1,128]{1,0:T(1,128)S(1)} %broadcast_maximum_fusion), channel_id=1, source_target_pairs={{0,16},{16,0},{1,17},{17,1},{2,18},{18,2},{3,19},{19,3},{4,20},{20... | collective-permute-start | bytes 1544 | tf_op jit(solution)/shard_map/ppermute | solution.py:160
  67.2 4.2 %collective-permute-start.11 = (f32[88,128]{1,0:T(8,128)S(1)}, f32[88,128]{1,0:T(8,128)S(1)}, u32[]{:S(2)}, u32[]{:S(2)}) collective-permute-start(f32[88,128]{1,0:T(8,128)S(1)} %slice_add_fusion.18), channel_id=1, source_target_pairs={{0,2},{2,0},{1,3},{3,1},{4,6},{6,4},{5,7},{7,5},{8,10},{10,8},{9,1... | collective-permute-start | bytes 135176 | tf_op jit(solution)/shard_map/ppermute | solution.py:111
  72.8 17.6 %collective-permute-start.15 = (bf16[88,3072]{1,0:T(8,128)(2,1)S(1)}, bf16[88,3072]{1,0:T(8,128)(2,1)S(1)}, u32[]{:S(2)}, u32[]{:S(2)}) collective-permute-start(bf16[88,3072]{1,0:T(8,128)(2,1)S(1)} %convolution_convert_fusion.5), channel_id=1, source_target_pairs={{0,4},{4,8},{8,12},{12,0},{1,5},{5,9},{9,13},{13,1},{2,6},{6,10},{... | collective-permute-start | bytes 1622024 | tf_op jit(solution)/shard_map/ppermute | solution.py:87
  73.5 52.8 %collective-permute-start.18 = (bf16[88,3072]{1,0:T(8,128)(2,1)S(1)}, bf16[88,3072]{1,0:T(8,128)(2,1)S(1)}, u32[]{:S(2)}, u32[]{:S(2)}) collective-permute-start(bf16[88,3072]{1,0:T(8,128)(2,1)S(1)} %convolution_convert_fusion.4), channel_id=1, source_target_pairs={{0,8},{4,12},{8,0},{12,4},{1,9},{5,13},{9,1},{13,5},{2,10},{6,14},... | collective-permute-start | bytes 1622024 | tf_op jit(solution)/shard_map/ppermute | solution.py:87
  81.3 45.7 %copy-start.8 = (f32[256,3072]{1,0:T(8,128)S(1)}, f32[256,3072]{1,0:T(8,128)}, u32[]{:S(2)}) copy-start(f32[256,3072]{1,0:T(8,128)} %fusion.76) | copy-start | bytes 9437188
  81.3 45.7 %collective-permute-start.12 = (bf16[88,3072]{1,0:T(8,128)(2,1)S(1)}, bf16[88,3072]{1,0:T(8,128)(2,1)S(1)}, u32[]{:S(2)}, u32[]{:S(2)}) collective-permute-start(bf16[88,3072]{1,0:T(8,128)(2,1)S(1)} %convolution_convert_fusion.6), channel_id=1, source_target_pairs={{0,12},{4,0},{8,4},{12,8},{1,13},{5,1},{9,5},{13,9},{2,14},{6,2},{... | collective-permute-start | bytes 1622024 | tf_op jit(solution)/shard_map/ppermute | solution.py:87

commit v3 on v2

--- a/solution.py
+++ b/solution.py
@@ -137,15 +137,28 @@
             for member in range(host_count):
                 base = base + back(member, start, block, returned[member])
             return base.astype(jnp.bfloat16), jnp.maximum(rounds, own_rounds)
-        order = sorted(range(1, host_count), key=lambda s: min(s, host_count - s))
-        received = {s: swap(pack(s, start, block), s) for s in order}
+        early = [s for s in range(1, host_count) if 2 * min(s, host_count - s) < host_count]
+        late = [s for s in range(1, host_count) if s not in early]
+        packed = {s: pack(s, start, block) for s in early + late}
+        received = {s: swap(packed[s], s) for s in early}
+        *held, base = lax.optimization_barrier(tuple(packed[s] for s in late) + (base,))
+        packed = dict(zip(late, held))
+        received.update({s: swap(packed[s], s) for s in late})
         rounds = own_rounds
         returned = {}
-        for s in order:
-            adapted, theirs = serve(received[s], block)
-            rounds = jnp.maximum(rounds, theirs)
-            returned[s] = swap(adapted, host_count - s)
-        for s in order:
+        for group in (early, late):
+            adapted = {}
+            for s in group:
+                adapted[s], theirs = serve(received[s], block)
+                rounds = jnp.maximum(rounds, theirs)
+            if group is early:
+                held = lax.optimization_barrier(
+                    tuple(adapted[s] for s in early) + tuple(received[s] for s in late)
+                )
+                received.update(zip(late, held[len(early) :]))
+            for s in group:
+                returned[s] = swap(adapted[s], host_count - s)
+        for s in early + late:
             base = (base + back(s, start, block, returned[s])).astype(jnp.bfloat16)
         return base, rounds
 

time: 130 us -> 113 us (0.87)
  the two profiles are of different devices: /device:TPU:24 before, /device:TPU:0 now
where the time goes in v3:
time: 113 us; the launch traced here: 112 us
  waiting for transfers between devices  48.1 us (43%)
  matrix products  25.4 us (22%)
  starting transfers between devices  24.8 us (22%)
  other arithmetic  8.26 us (7%)
  between operations  2.99 us (3%)
  local copies, waits for them, and re-layouts  1.97 us (2%)
    ppermute x6, waiting for transfers between devices, swap(): lax.ppermute(values, 'hst', [(i, (i + step) % host_count) for i in range(...  44.3 us
    ppermute x6, starting transfers between devices, swap(): lax.ppermute(values, 'hst', [(i, (i + step) % host_count) for i in range(...  18.8 us
    dot_general x4, matrix products, adapt(): lax.dot_general(inputs, flat_a, (((1,), (1,)), ((), ())), preferred_eleme...  8.83 us
    dot_general x4, matrix products, adapt(): return jnp.dot(spread, flat_b, preferred_element_type=jnp.float32)  5.81 us
    dot_general x3, matrix products, back(): lax.dot_general(place(member, start, block).astype(jnp.bfloat16), returne...  5.6 us
    dot_general x3, matrix products, pack(): jnp.dot(chosen.astype(jnp.bfloat16), flat_x, preferred_element_type=jnp.f...  4.92 us
    ppermute x4, starting transfers between devices, adapt(): lax.ppermute(partial, 'mp', [(i, (i + hop) % shares) for i in range(share...  4.4 us
    ppermute x4, waiting for transfers between devices, adapt(): lax.ppermute(partial, 'mp', [(i, (i + hop) % shares) for i in range(share...  3.77 us
  transfers between devices with their start and end apart: 12, of which 6 were waited for; matrix products, arithmetic and copies ran while one was open for 24% of the time, Pallas kernels for 0%

profile of v3, /device:TPU:0, one launch (start us, length us, event | category | flops | bytes accessed | tf_op | source)
XLA Modules:
  0.0 112.3 jit_solution(5146691036392608643)
XLA Ops:
  0.0 0.7 bitcast_add_fusion
  0.8 0.8 select_reduce_fusion.7
  1.6 0.2 select_reduce_fusion.6
  1.9 3.5 %convolution_select_fusion.9 = f32[256,512]{1,0:T(8,128)S(1)} fusion(bf16[256,3072]{1,0:T(8,128)(2,1)} %bitcast.190, bf16[512,3072]{1,0:T(8,128)(2,1)} %bitcast.185, s32[512]{0:T(512)S(1)} %fusion.122, s32[256]{0:T(256)S(1)} %get-tuple-element.281), kind=kOutput, calls=%fused_computation.137 | convolution fusion | flops 805568512 | bytes 5245952 | tf_op jit(solution)/shard_map/dot_general | solution.py:105
  5.4 3.0 %collective-permute-start.9 = (f32[256,128]{1,0:T(8,128)S(1)}, f32[256,128]{1,0:T(8,128)S(1)}, u32[]{:S(2)}, u32[]{:S(2)}) collective-permute-start(f32[256,128]{1,0:T(8,128)S(1)} %slice_add_fusion.9), channel_id=1, source_target_pairs={{0,2},{2,0},{1,3},{3,1},{4,6},{6,4},{5,7},{7,5},{8,10},{10,8},{9,1... | collective-permute-start | bytes 393224 | tf_op jit(solution)/shard_map/ppermute | solution.py:111
  8.4 0.2 fusion.80
  8.6 0.7 select_reduce_fusion.8
  10.0 0.3 select_reduce_fusion.5
  10.3 0.4 fusion.77
  10.8 1.6 %collective-permute-start.10 = (bf16[88,3072]{1,0:T(8,128)(2,1)S(1)}, bf16[88,3072]{1,0:T(8,128)(2,1)S(1)}, u32[]{:S(2)}, u32[]{:S(2)}) collective-permute-start(bf16[88,3072]{1,0:T(8,128)(2,1)S(1)} %fusion.77), channel_id=1, source_target_pairs={{0,4},{4,8},{8,12},{12,0},{1,5},{5,9},{9,13},{13,1},{2,6},{6,10},{... | collective-permute-start | bytes 1622024 | tf_op jit(solution)/shard_map/ppermute | solution.py:87
  12.4 1.8 %fusion.78 = bf16[88,3072]{1,0:T(8,128)(2,1)S(1)} fusion(bf16[256,3072]{1,0:T(8,128)(2,1)} %bitcast.191, bf16[3072]{0:T(1024)(128)(2,1)S(1)} %pad.31, pred[88]{0:T(512)(128)(4,1)S(1)} %get-tuple-element.300, s32[256]{0:T(256)S(1)} %fusion.80, pred[88]{0:T(512)(128)(4,1)S(1)} %get-tuple-element.299, pred[256]{0:T(512)(128)(4,1)S(1)} %get-tuple-element.294), kind=kOutput, calls=%fused_computation.136 | convolution fusion | flops 138749952 | bytes 2121136 | tf_op jit(solution)/shard_map/dot_general | solution.py:82
  14.3 2.4 %collective-permute-start.13 = (bf16[88,3072]{1,0:T(8,128)(2,1)S(1)}, bf16[88,3072]{1,0:T(8,128)(2,1)S(1)}, u32[]{:S(2)}, u32[]{:S(2)}) collective-permute-start(bf16[88,3072]{1,0:T(8,128)(2,1)S(1)} %fusion.78), channel_id=1, source_target_pairs={{0,12},{4,0},{8,4},{12,8},{1,13},{5,1},{9,5},{13,9},{2,14},{6,2},{... | collective-permute-start | bytes 1622024 | tf_op jit(solution)/shard_map/ppermute | solution.py:87
  16.7 2.6 %fusion.76 = bf16[88,3072]{1,0:T(8,128)(2,1)} fusion(bf16[256,3072]{1,0:T(8,128)(2,1)} %bitcast.192, bf16[3072]{0:T(1024)(128)(2,1)S(1)} %pad.29, pred[88]{0:T(512)(128)(4,1)S(1)} %get-tuple-element.300, s32[256]{0:T(256)S(1)} %fusion.80, pred[88]{0:T(512)(128)(4,1)S(1)} %get-tuple-element.299, pred[256]{0:T(512)(128)(4,1)S(1)} %get-tuple-element.296), kind=kOutput, calls=%fused_computation.134 | convolution fusion | flops 138749952 | bytes 2121136 | tf_op jit(solution)/shard_map/dot_general | solution.py:82
  19.4 0.9 compare_select_fusion.7
  20.3 2.1 %convolution_convert_fusion.3 = bf16[256,3072]{1,0:T(8,128)(2,1)} fusion(bf16[512,3072]{1,0:T(8,128)(2,1)S(1)} %bitcast.180, bf16[32,8,4,128]{3,2,1,0:T(4,128)(2,1)S(1)} %bitcast.201), kind=kOutput, calls=%fused_computation.127 | convolution fusion | flops 806092800 | bytes 4980736 | tf_op jit(solution)/shard_map/dot_general | solution.py:116
  22.5 0.6 collective-permute-start.16
  23.1 4.8 %collective-permute-done.10 = bf16[88,3072]{1,0:T(8,128)(2,1)S(1)} collective-permute-done((bf16[88,3072]{1,0:T(8,128)(2,1)S(1)}, bf16[88,3072]{1,0:T(8,128)(2,1)S(1)}, u32[]{:S(2)}, u32[]{:S(2)}) %collective-permute-start.10) | collective-permute-done | bytes 540704 | tf_op jit(solution)/shard_map/ppermute | solution.py:87
  27.9 1.1 convolution_select_fusion.12
  29.0 0.6 slice_add_fusion.18
  29.6 0.3 collective-permute-start.11
  29.9 8.1 %collective-permute-done.13 = bf16[88,3072]{1,0:T(8,128)(2,1)S(1)} collective-permute-done((bf16[88,3072]{1,0:T(8,128)(2,1)S(1)}, bf16[88,3072]{1,0:T(8,128)(2,1)S(1)}, u32[]{:S(2)}, u32[]{:S(2)}) %collective-permute-start.13) | collective-permute-done | bytes 540704 | tf_op jit(solution)/shard_map/ppermute | solution.py:87
  38.0 1.1 convolution_select_fusion.11
  39.1 0.6 slice_add_fusion.15
  39.8 0.6 slice.255
  40.4 0.6 slice.256
  41.0 0.5 collective-permute-start.14
  42.8 0.8 add_convert_fusion.6
  43.6 1.8 %collective-permute-done.14 = f32[88,128]{1,0:T(8,128)} collective-permute-done((f32[88,128]{1,0:T(8,128)}, f32[88,128]{1,0:T(8,128)}, u32[]{:S(2)}, u32[]{:S(2)}) %collective-permute-start.14) | collective-permute-done | bytes 45088 | tf_op jit(solution)/shard_map/ppermute | solution.py:111
  45.4 0.8 add_convert_fusion.5
  46.2 0.3 compare_select_fusion.9
  46.4 1.5 %convolution_convert_fusion.5 = bf16[88,3072]{1,0:T(8,128)(2,1)} fusion(bf16[512,3072]{1,0:T(8,128)(2,1)S(1)} %bitcast.181, bf16[11,8,4,128]{3,2,1,0:T(4,128)(2,1)S(1)} %bitcast.205), kind=kOutput, calls=%fused_computation.132 | convolution fusion | flops 277094400 | bytes 3776512 | tf_op jit(solution)/shard_map/dot_general | solution.py:116
  48.0 14.0 %collective-permute-start.15 = (bf16[88,3072]{1,0:T(8,128)(2,1)}, bf16[88,3072]{1,0:T(8,128)(2,1)}, u32[]{:S(2)}, u32[]{:S(2)}) collective-permute-start(bf16[88,3072]{1,0:T(8,128)(2,1)} %convolution_convert_fusion.5), channel_id=1, source_target_pairs={{0,4},{4,8},{8,12},{12,0},{1,5},{5,9},{9,13},{13,1},{2,6},{6,10},{... | collective-permute-start | bytes 1622024 | tf_op jit(solution)/shard_map/ppermute | solution.py:87
  62.0 1.5 %convolution_convert_fusion.6 = bf16[88,3072]{1,0:T(8,128)(2,1)} fusion(bf16[512,3072]{1,0:T(8,128)(2,1)S(1)} %bitcast.182, bf16[11,8,4,128]{3,2,1,0:T(4,128)(2,1)S(1)} %bitcast.204), kind=kOutput, calls=%fused_computation.133 | convolution fusion | flops 277094400 | bytes 3776512 | tf_op jit(solution)/shard_map/dot_general | solution.py:116
  63.5 9.5 %collective-permute-done.16 = bf16[88,3072]{1,0:T(8,128)(2,1)} collective-permute-done((bf16[88,3072]{1,0:T(8,128)(2,1)}, bf16[88,3072]{1,0:T(8,128)(2,1)}, u32[]{:S(2)}, u32[]{:S(2)}) %collective-permute-start.16) | collective-permute-done | bytes 540704 | tf_op jit(solution)/shard_map/ppermute | solution.py:87
  73.0 0.7 fusion.130
  73.7 0.6 slice.257
  75.0 3.2 %convolution_select_fusion.10 = f32[88,512]{1,0:T(8,128)S(1)} fusion(bf16[88,3072]{1,0:T(8,128)(2,1)} %collective-permute-done.16, bf16[512,3072]{1,0:T(8,128)(2,1)} %bitcast.186, s32[512]{0:T(512)S(1)} %fusion.122, s32[88]{0:T(128)S(1)} %select_bitcast_fusion.3), kind=kOutput, calls=%fused_computation.138 | convolution fusion | flops 276914176 | bytes 3869024 | tf_op jit(solution)/shard_map/dot_general | solution.py:105
  78.2 0.6 collective-permute-start.17
  78.8 1.5 %collective-permute-start.20 = (s32[1,128]{1,0:T(1,128)S(1)}, s32[1,128]{1,0:T(1,128)S(1)}, u32[]{:S(2)}, u32[]{:S(2)}) collective-permute-start(s32[1,128]{1,0:T(1,128)S(1)} %broadcast_maximum_fusion), channel_id=1, source_target_pairs={{0,16},{16,0},{1,17},{17,1},{2,18},{18,2},{3,19},{19,3},{4,20},{20... | collective-permute-start | bytes 1544 | tf_op jit(solution)/shard_map/ppermute | solution.py:173
  80.3 2.0 %collective-permute-done.17 = f32[88,128]{1,0:T(8,128)S(1)} collective-permute-done((f32[88,128]{1,0:T(8,128)S(1)}, f32[88,128]{1,0:T(8,128)S(1)}, u32[]{:S(2)}, u32[]{:S(2)}) %collective-permute-start.17) | collective-permute-done | bytes 45088 | tf_op jit(solution)/shard_map/ppermute | solution.py:111
  82.3 0.2 compare_select_fusion.8
  82.5 0.7 convolution_convert_fusion.4
  83.2 0.6 fusion.167
  83.8 1.8 %fusion.95 = f32[256,3072]{1,0:T(8,128)S(1)} fusion(bf16[88,3072]{1,0:T(8,128)(2,1)} %collective-permute-done.15, s32[256]{0:T(256)S(1)} %fusion.80, pred[88]{0:T(512)(128)(4,1)S(1)} %get-tuple-element.299, pred[256]{0:T(512)(128)(4,1)S(1)} %get-tuple-element.294), kind=kOutput, calls=%fused_computation.176 | convolution fusion | flops 138479616 | bytes 3687768 | tf_op jit(solution)/shard_map/dot_general | solution.py:125
  85.7 21.9 %collective-permute-done.18 = bf16[88,3072]{1,0:T(8,128)(2,1)S(1)} collective-permute-done((bf16[88,3072]{1,0:T(8,128)(2,1)S(1)}, bf16[88,3072]{1,0:T(8,128)(2,1)S(1)}, u32[]{:S(2)}, u32[]{:S(2)}) %collective-permute-start.18) | collective-permute-done | bytes 540704 | tf_op jit(solution)/shard_map/ppermute | solution.py:87
  107.6 0.7 fusion.100
  108.3 3.1 %fusion.75 = bf16[256,3072]{1,0:T(8,128)(2,1)} fusion(f32[256,3072]{1,0:T(8,128)S(1)} %fusion.100, f32[256,3072]{1,0:T(8,128)S(1)} %fusion.95, bf16[88,3072]{1,0:T(8,128)(2,1)} %collective-permute-done.12, bf16[256,3072]{1,0:T(8,128)(2,1)S(1)} %copy-done.6, s32[256]{0:T(256)S(1)} %fusion.80, pred[88]{0:T(512)(128)(4,1)S(1)} %get-tuple-element.299, ...), kind=kOutput, calls=%fused_computation.126 | convolution fusion | flops 145557504 | bytes 9979224 | tf_op jit(solution)/shard_map/dot_general | solution.py:125
  111.4 0.8 while.14
  (45 shorter events, 0.5 us)
Async XLA Ops:
  1.9 8.5 %copy-start.3 = (bf16[4,64,3072]{2,1,0:T(8,128)(2,1)S(1)}, bf16[4,64,3072]{2,1,0:T(8,128)(2,1)}, u32[]{:S(2)}) copy-start(bf16[4,64,3072]{2,1,0:T(8,128)(2,1)} %param.9) | copy-start | bytes 4718596
  5.4 4.9 %copy-start.7 = (f32[256,512]{1,0:T(8,128)}, f32[256,512]{1,0:T(8,128)S(1)}, u32[]{:S(2)}) copy-start(f32[256,512]{1,0:T(8,128)S(1)} %convolution_select_fusion.9) | copy-start | bytes 1572868
  5.4 14.0 %collective-permute-start.9 = (f32[256,128]{1,0:T(8,128)S(1)}, f32[256,128]{1,0:T(8,128)S(1)}, u32[]{:S(2)}, u32[]{:S(2)}) collective-permute-start(f32[256,128]{1,0:T(8,128)S(1)} %slice_add_fusion.9), channel_id=1, source_target_pairs={{0,2},{2,0},{1,3},{3,1},{4,6},{6,4},{5,7},{7,5},{8,10},{10,8},{9,1... | collective-permute-start | bytes 393224 | tf_op jit(solution)/shard_map/ppermute | solution.py:111
  10.8 8.6 %copy-start.8 = (f32[256,512]{1,0:T(8,128)S(1)}, f32[256,512]{1,0:T(8,128)}, u32[]{:S(2)}) copy-start(f32[256,512]{1,0:T(8,128)} %copy-done.7) | copy-start | bytes 1572868
  10.8 9.5 %copy-start = (bf16[32,16,3072]{2,1,0:T(8,128)(2,1)S(1)}, bf16[32,16,3072]{2,1,0:T(8,128)(2,1)}, u32[]{:S(2)}) copy-start(bf16[32,16,3072]{2,1,0:T(8,128)(2,1)} %param.11) | copy-start | bytes 9437188
  10.8 17.1 %collective-permute-start.10 = (bf16[88,3072]{1,0:T(8,128)(2,1)S(1)}, bf16[88,3072]{1,0:T(8,128)(2,1)S(1)}, u32[]{:S(2)}, u32[]{:S(2)}) collective-permute-start(bf16[88,3072]{1,0:T(8,128)(2,1)S(1)} %fusion.77), channel_id=1, source_target_pairs={{0,4},{4,8},{8,12},{12,0},{1,5},{5,9},{9,13},{13,1},{2,6},{6,10},{... | collective-permute-start | bytes 1622024 | tf_op jit(solution)/shard_map/ppermute | solution.py:87
  14.3 23.8 %collective-permute-start.13 = (bf16[88,3072]{1,0:T(8,128)(2,1)S(1)}, bf16[88,3072]{1,0:T(8,128)(2,1)S(1)}, u32[]{:S(2)}, u32[]{:S(2)}) collective-permute-start(bf16[88,3072]{1,0:T(8,128)(2,1)S(1)} %fusion.78), channel_id=1, source_target_pairs={{0,12},{4,0},{8,4},{12,8},{1,13},{5,1},{9,5},{13,9},{2,14},{6,2},{... | collective-permute-start | bytes 1622024 | tf_op jit(solution)/shard_map/ppermute | solution.py:87
  19.4 8.5 %copy-start.1 = (bf16[32,16,3072]{2,1,0:T(8,128)(2,1)S(1)}, bf16[32,16,3072]{2,1,0:T(8,128)(2,1)}, u32[]{:S(2)}) copy-start(bf16[32,16,3072]{2,1,0:T(8,128)(2,1)} %param.10) | copy-start | bytes 9437188
  22.5 50.6 %collective-permute-start.16 = (bf16[88,3072]{1,0:T(8,128)(2,1)}, bf16[88,3072]{1,0:T(8,128)(2,1)}, u32[]{:S(2)}, u32[]{:S(2)}) collective-permute-start(bf16[88,3072]{1,0:T(8,128)(2,1)} %fusion.76), channel_id=1, source_target_pairs={{0,8},{4,12},{8,0},{12,4},{1,9},{5,13},{9,1},{13,5},{2,10},{6,14},... | collective-permute-start | bytes 1622024 | tf_op jit(solution)/shard_map/ppermute | solution.py:87
  29.6 13.2 %collective-permute-start.11 = (f32[88,128]{1,0:T(8,128)}, f32[88,128]{1,0:T(8,128)}, u32[]{:S(2)}, u32[]{:S(2)}) collective-permute-start(f32[88,128]{1,0:T(8,128)} %slice_add_fusion.18), channel_id=1, source_target_pairs={{0,2},{2,0},{1,3},{3,1},{4,6},{6,4},{5,7},{7,5},{8,10},{10,8},{9,1... | collective-permute-start | bytes 135176 | tf_op jit(solution)/shard_map/ppermute | solution.py:111
  41.0 4.4 %collective-permute-start.14 = (f32[88,128]{1,0:T(8,128)}, f32[88,128]{1,0:T(8,128)}, u32[]{:S(2)}, u32[]{:S(2)}) collective-permute-start(f32[88,128]{1,0:T(8,128)} %slice_add_fusion.15), channel_id=1, source_target_pairs={{0,2},{2,0},{1,3},{3,1},{4,6},{6,4},{5,7},{7,5},{8,10},{10,8},{9,1... | collective-permute-start | bytes 135176 | tf_op jit(solution)/shard_map/ppermute | solution.py:111
  48.0 35.9 %collective-permute-start.15 = (bf16[88,3072]{1,0:T(8,128)(2,1)}, bf16[88,3072]{1,0:T(8,128)(2,1)}, u32[]{:S(2)}, u32[]{:S(2)}) collective-permute-start(bf16[88,3072]{1,0:T(8,128)(2,1)} %convolution_convert_fusion.5), channel_id=1, source_target_pairs={{0,4},{4,8},{8,12},{12,0},{1,5},{5,9},{9,13},{13,1},{2,6},{6,10},{... | collective-permute-start | bytes 1622024 | tf_op jit(solution)/shard_map/ppermute | solution.py:87
  63.5 44.8 %collective-permute-start.12 = (bf16[88,3072]{1,0:T(8,128)(2,1)}, bf16[88,3072]{1,0:T(8,128)(2,1)}, u32[]{:S(2)}, u32[]{:S(2)}) collective-permute-start(bf16[88,3072]{1,0:T(8,128)(2,1)} %convolution_convert_fusion.6), channel_id=1, source_target_pairs={{0,12},{4,0},{8,4},{12,8},{1,13},{5,1},{9,5},{13,9},{2,14},{6,2},{... | collective-permute-start | bytes 1622024 | tf_op jit(solution)/shard_map/ppermute | solution.py:87
  74.9 3.9 %collective-permute-start.19 = (s32[1,128]{1,0:T(1,128)S(1)}, s32[1,128]{1,0:T(1,128)S(1)}, u32[]{:S(2)}, u32[]{:S(2)}) collective-permute-start(s32[1,128]{1,0:T(1,128)S(1)} %broadcast_in_dim.359), channel_id=1, source_target_pairs={{0,1},{1,0},{2,3},{3,2},{4,5},{5,4},{6,7},{7,6},{8,9},{9,8},{10,11... | collective-permute-start | bytes 1544 | tf_op jit(solution)/shard_map/ppermute | solution.py:173
  78.2 4.1 %collective-permute-start.17 = (f32[88,128]{1,0:T(8,128)S(1)}, f32[88,128]{1,0:T(8,128)S(1)}, u32[]{:S(2)}, u32[]{:S(2)}) collective-permute-start(f32[88,128]{1,0:T(8,128)S(1)} %slice_add_fusion.12), channel_id=1, source_target_pairs={{0,2},{2,0},{1,3},{3,1},{4,6},{6,4},{5,7},{7,5},{8,10},{10,8},{9,1... | collective-permute-start | bytes 135176 | tf_op jit(solution)/shard_map/ppermute | solution.py:111
  78.8 4.5 %collective-permute-start.20 = (s32[1,128]{1,0:T(1,128)S(1)}, s32[1,128]{1,0:T(1,128)S(1)}, u32[]{:S(2)}, u32[]{:S(2)}) collective-permute-start(s32[1,128]{1,0:T(1,128)S(1)} %broadcast_maximum_fusion), channel_id=1, source_target_pairs={{0,16},{16,0},{1,17},{17,1},{2,18},{18,2},{3,19},{19,3},{4,20},{20... | collective-permute-start | bytes 1544 | tf_op jit(solution)/shard_map/ppermute | solution.py:173
  83.1 24.4 %collective-permute-start.18 = (bf16[88,3072]{1,0:T(8,128)(2,1)S(1)}, bf16[88,3072]{1,0:T(8,128)(2,1)S(1)}, u32[]{:S(2)}, u32[]{:S(2)}) collective-permute-start(bf16[88,3072]{1,0:T(8,128)(2,1)S(1)} %convolution_convert_fusion.4), channel_id=1, source_target_pairs={{0,8},{4,12},{8,0},{12,4},{1,9},{5,13},{9,1},{13,5},{2,10},{6,14},... | collective-permute-start | bytes 1622024 | tf_op jit(solution)/shard_map/ppermute | solution.py:87
  83.8 24.5 %copy-start.6 = (bf16[256,3072]{1,0:T(8,128)(2,1)S(1)}, bf16[256,3072]{1,0:T(8,128)(2,1)}, u32[]{:S(2)}) copy-start(bf16[256,3072]{1,0:T(8,128)(2,1)} %convolution_convert_fusion.3) | copy-start | bytes 4718596

commit v4 on v2

--- a/solution.py
+++ b/solution.py
@@ -1,14 +1,194 @@
+import functools
+
 import jax
 import jax.numpy as jnp
 from jax import lax
+from jax.experimental import pallas as pl
+from jax.experimental.pallas import tpu as pltpu
 from jax.sharding import PartitionSpec as P
 
-MOST_SHIFTS = 8
+MOST_PAIRED = 8
 LANES = 128
+VMEM_BYTES = 32 << 20
 
 
 def round_up(value, unit):
     return unit * -(-value // unit)
+
+
+def block_names(block):
+    count = block.shape[0]
+    lane = lax.broadcasted_iota(jnp.int32, (count, LANES), 1)
+    row = lax.broadcasted_iota(jnp.int32, (count, LANES), 0)
+    last = block[count - 1 :, :LANES].astype(jnp.float32)
+    return jnp.sum(
+        jnp.where((lane == row) & (row < count - 1), last, 0.0), axis=1, keepdims=True
+    )
+
+
+def lane_adapter(first, rank_extent):
+    lane = lax.broadcasted_iota(jnp.int32, (1, LANES), 1)
+    return (first + lane // rank_extent + 1).astype(jnp.float32)
+
+
+def shrink_kernel(counts, own, pieces, rank_extent, first_ref, *refs):
+    blocks, refs = refs[: len(counts)], refs[len(counts) :]
+    own_names = None
+    if own:
+        own_names, refs = refs[0], refs[1:]
+    weights, (partial_ref, names_ref) = refs[:pieces], refs[pieces:]
+    offset = 0
+    for index, count in enumerate(counts):
+        rows = blocks[index][...]
+        names = own_names[...] if own and index == 0 else block_names(rows)
+        total = jnp.zeros((count, LANES), jnp.float32)
+        number = 0
+        for weight in weights:
+            for start in range(0, weight.shape[0], LANES):
+                product = lax.dot_general(
+                    rows,
+                    weight[start : start + LANES, :],
+                    (((1,), (1,)), ((), ())),
+                    preferred_element_type=jnp.float32,
+                )
+                here = names == lane_adapter(first_ref[number], rank_extent)
+                total = total + jnp.where(here, product, 0.0)
+                number += 1
+        partial_ref[offset : offset + count, :] = total
+        names_ref[offset : offset + count, :] = jnp.broadcast_to(names, (count, LANES))
+        offset += count
+
+
+def expand_kernel(counts, shares, pieces, rank_extent, told, first_ref, *refs):
+    if told:
+        told_ref, refs = refs[0], refs[1:]
+    partials, refs = refs[:shares], refs[shares:]
+    names_ref, refs = refs[0], refs[1:]
+    weights, refs = refs[:pieces], refs[pieces:]
+    outs, spread_ref = refs[:-1], refs[-1]
+
+    @pl.when(pl.program_id(0) == 0)
+    def _():
+        total = partials[0][...]
+        for partial in partials[1:]:
+            total = total + partial[...]
+        shrink = total.astype(jnp.bfloat16).astype(jnp.float32)
+        for number in range(spread_ref.shape[1] // LANES):
+            here = names_ref[...] == lane_adapter(first_ref[number], rank_extent)
+            spread_ref[:, number * LANES : (number + 1) * LANES] = jnp.where(
+                here, shrink, 0.0
+            ).astype(jnp.bfloat16)
+
+    total = None
+    column = 0
+    for weight in weights:
+        depth = weight.shape[0]
+        product = jnp.dot(
+            spread_ref[:, column : column + depth],
+            weight[...],
+            preferred_element_type=jnp.float32,
+        )
+        total = product if total is None else total + product
+        column += depth
+    offset = 0
+    for count, out in zip(counts, outs):
+        values = total[offset : offset + count, :]
+        if told:
+            row = lax.broadcasted_iota(jnp.int32, values.shape, 0)
+            values = jnp.where(row == count - 1, told_ref[0].astype(jnp.float32), values)
+        out[...] = values.astype(out.dtype)
+        offset += count
+
+
+def back_kernel(blocks, base_ref, *refs):
+    places, returned, outs = refs[:blocks], refs[blocks : 2 * blocks], refs[2 * blocks :]
+    out_ref = outs[0]
+    total = base_ref[...].astype(jnp.float32)
+    for place, block in zip(places, returned):
+        total = total + jnp.dot(place[...], block[...], preferred_element_type=jnp.float32)
+    out_ref[...] = total.astype(out_ref.dtype)
+    if len(outs) == 1:
+        return
+
+    @pl.when(pl.program_id(0) == 0)
+    def _():
+        told = jnp.float32(0)
+        for block in returned:
+            rows = block[...]
+            told = jnp.maximum(told, jnp.max(rows[rows.shape[0] - 1 :, :LANES].astype(jnp.float32)))
+        outs[1][0] = told.astype(jnp.int32)
+
+
+def shrink_call(blocks, own_names, weights, firsts, rank_extent):
+    counts = [block.shape[0] for block in blocks]
+    rows = sum(counts)
+    width = blocks[0].shape[1]
+    spots = sum(weight.shape[0] for weight in weights)
+    names = [] if own_names is None else [own_names]
+    whole = pl.BlockSpec(memory_space=pltpu.VMEM)
+    return pl.pallas_call(
+        functools.partial(
+            shrink_kernel, counts, own_names is not None, len(weights), rank_extent
+        ),
+        out_shape=(jax.ShapeDtypeStruct((rows, LANES), jnp.float32),) * 2,
+        in_specs=[pl.BlockSpec(memory_space=pltpu.SMEM)]
+        + [whole] * (len(blocks) + len(names) + len(weights)),
+        out_specs=(whole, whole),
+        compiler_params=pltpu.CompilerParams(vmem_limit_bytes=VMEM_BYTES),
+        cost_estimate=pl.CostEstimate(
+            flops=2 * rows * spots * width,
+            bytes_accessed=2 * (rows + spots) * width,
+            transcendentals=0,
+        ),
+    )(firsts, *blocks, *names, *weights)
+
+
+def back_call(base, places, returned, told, weight=1):
+    rows, width = base.shape
+    tile = width // 6 if width % (6 * LANES) == 0 else width
+    tiles = lambda count: pl.BlockSpec((count, tile), lambda i: (0, i))
+    return pl.pallas_call(
+        functools.partial(back_kernel, len(returned)),
+        grid=(width // tile,),
+        out_shape=[jax.ShapeDtypeStruct((rows, width), jnp.bfloat16)]
+        + [jax.ShapeDtypeStruct((1,), jnp.int32)] * told,
+        in_specs=[tiles(rows)]
+        + [pl.BlockSpec(place.shape, lambda i: (0, 0)) for place in places]
+        + [tiles(block.shape[0]) for block in returned],
+        out_specs=[tiles(rows)] + [pl.BlockSpec(memory_space=pltpu.SMEM)] * told,
+        compiler_params=pltpu.CompilerParams(vmem_limit_bytes=VMEM_BYTES),
+        cost_estimate=pl.CostEstimate(
+            flops=2 * weight * rows * width * sum(block.shape[0] for block in returned),
+            bytes_accessed=4 * weight * rows * width,
+            transcendentals=0,
+        ),
+    )(base, *places, *returned)
+
+
+def expand_call(partials, names, weights, firsts, counts, rank_extent, told=None):
+    width = weights[0].shape[1]
+    rows = names.shape[0]
+    spots = sum(weight.shape[0] for weight in weights)
+    tile = width // 6 if width % (6 * LANES) == 0 else width
+    whole = pl.BlockSpec(memory_space=pltpu.VMEM)
+    return pl.pallas_call(
+        functools.partial(
+            expand_kernel, counts, len(partials), len(weights), rank_extent, told is not None
+        ),
+        grid=(width // tile,),
+        out_shape=[jax.ShapeDtypeStruct((count, width), jnp.bfloat16) for count in counts],
+        in_specs=[pl.BlockSpec(memory_space=pltpu.SMEM)] * (1 if told is None else 2)
+        + [whole] * (len(partials) + 1)
+        + [pl.BlockSpec((weight.shape[0], tile), lambda i: (0, i)) for weight in weights],
+        out_specs=[pl.BlockSpec((count, tile), lambda i: (0, i)) for count in counts],
+        scratch_shapes=[pltpu.VMEM((rows, spots), jnp.bfloat16)],
+        compiler_params=pltpu.CompilerParams(vmem_limit_bytes=VMEM_BYTES),
+        cost_estimate=pl.CostEstimate(
+            flops=2 * rows * spots * width,
+            bytes_accessed=2 * (rows + spots) * width,
+            transcendentals=0,
+        ),
+    )(firsts, *([] if told is None else [told]), *partials, names, *weights)
 
 
 def local(
@@ -29,7 +209,7 @@
     spots = local_adapters * rank_extent
     folded = LANES if spots % LANES == 0 and LANES % rank_extent == 0 else spots
     table_size = former_layout_list.shape[0]
-    by_shift = host_count <= MOST_SHIFTS
+    paired = host_count <= MOST_PAIRED and host_count & (host_count - 1) == 0
     first_block = round_up(11 * rows // (8 * host_count), 8)
     more_block = min(first_block, 16)
 
@@ -46,8 +226,8 @@
     served = jnp.sum(jnp.where(wanted[:, None] == table[None, :], source[None, :], 0), axis=1)
     owner = served // local_adapters
     named_row = served % local_adapters + 1
-    ahead = lax.rem(owner - me + host_count, host_count)
-    key = ahead if by_shift else jnp.where(ahead == 0, host_count, owner)
+    stays = owner == me
+    key = owner ^ me if paired else jnp.where(stays, host_count, owner)
 
     hosts = jnp.arange(host_count, dtype=jnp.int32)
     in_block = key[:, None] == hosts[None, :]
@@ -57,36 +237,37 @@
         earlier, in_block.astype(jnp.bfloat16), preferred_element_type=jnp.float32
     ).astype(jnp.int32)
     row_rank = jnp.sum(jnp.where(in_block, before, 0), axis=1)
-    left = jnp.max(jnp.where(ahead == 0, 0, row_rank + 1)) - (first_block - 1)
+    left = jnp.max(jnp.where(stays, 0, row_rank + 1)) - (first_block - 1)
     own_rounds = jnp.maximum(0, (left + more_block - 2) // (more_block - 1))
 
     columns = jnp.arange(width, dtype=jnp.int32)
     spot_adapter = jnp.arange(spots, dtype=jnp.int32) // rank_extent + 1
 
-    def place(member, start, block):
+    def place(member, start, block, key, row_rank):
         slot = jnp.arange(block, dtype=jnp.int32)[:, None]
         chosen = (
             (key[None, :] == member)
             & (slot + start == row_rank[None, :])
             & (slot < block - 1)
         )
-        return chosen
-
-    def pack(member, start, block):
-        chosen = place(member, start, block)
+        return chosen.astype(jnp.bfloat16)
+
+    def pack(member, start, block, key, row_rank, told):
         at_column = (key[:, None] == member) & (row_rank[:, None] == columns[None, :LANES] + start)
         names = jnp.sum(jnp.where(at_column, named_row[:, None], 0), axis=0)
         lane = columns[:LANES]
-        names = jnp.where(lane < block - 1, names, jnp.where(lane == block - 1, own_rounds, 0))
+        names = jnp.where(lane < block - 1, names, jnp.where(lane == block - 1, told, 0))
         names = jnp.pad(names.astype(jnp.float32), (0, width - LANES))
-        rows_out = jnp.dot(chosen.astype(jnp.bfloat16), flat_x, preferred_element_type=jnp.float32)
+        rows_out = jnp.dot(
+            place(member, start, block, key, row_rank),
+            flat_x,
+            preferred_element_type=jnp.float32,
+        )
         last = (jnp.arange(block) == block - 1)[:, None]
         return jnp.where(last, names[None, :], rows_out).astype(jnp.bfloat16)
 
     def swap(values, step):
-        return lax.ppermute(
-            values, "hst", [(i, (i + step) % host_count) for i in range(host_count)]
-        )
+        return lax.ppermute(values, "hst", [(i, i ^ step) for i in range(host_count)])
 
     def exchange(values):
         split = values.reshape(host_count, -1, values.shape[-1])
@@ -123,44 +304,108 @@
 
     def back(member, start, block, returned):
         return lax.dot_general(
-            place(member, start, block).astype(jnp.bfloat16),
+            place(member, start, block, key, row_rank),
             returned,
             (((0,), (0,)), ((), ())),
             preferred_element_type=jnp.float32,
         )
 
     def one_round(start, block, base):
-        if not by_shift:
-            packed = jnp.concatenate([pack(member, start, block) for member in range(host_count)])
+        if not paired:
+            packed = jnp.concatenate([pack(member, start, block, key, row_rank, own_rounds) for member in range(host_count)])
             adapted, rounds = serve(exchange(packed), block)
             returned = exchange(adapted).reshape(host_count, block, width)
             for member in range(host_count):
                 base = base + back(member, start, block, returned[member])
             return base.astype(jnp.bfloat16), jnp.maximum(rounds, own_rounds)
-        order = sorted(range(1, host_count), key=lambda s: min(s, host_count - s))
-        received = {s: swap(pack(s, start, block), s) for s in order}
+        received = {s: swap(pack(s, start, block, key, row_rank, own_rounds), s) for s in range(1, host_count)}
         rounds = own_rounds
-        returned = {}
-        for s in order:
+        for s in range(1, host_count):
             adapted, theirs = serve(received[s], block)
             rounds = jnp.maximum(rounds, theirs)
-            returned[s] = swap(adapted, host_count - s)
-        for s in order:
-            base = (base + back(s, start, block, returned[s])).astype(jnp.bfloat16)
+            returned = swap(adapted, s)
+            base = (base + back(s, start, block, returned)).astype(jnp.bfloat16)
         return base, rounds
 
-    own = adapt(flat_x, jnp.where(ahead == 0, named_row, 0)).astype(jnp.bfloat16)
-    result, rounds = one_round(0, first_block, own)
-    rounds = jnp.full((1, LANES), rounds, jnp.int32)
-    for axis in ("rep", "groups"):
-        size = lax.axis_size(axis)
-        most = rounds
-        for hop in range(1, size):
-            most = jnp.maximum(
-                most, lax.ppermute(rounds, axis, [(i, (i + hop) % size) for i in range(size)])
+    def agree(rounds):
+        rounds = jnp.full((1, LANES), rounds, jnp.int32)
+        for axis in ("rep", "groups"):
+            size = lax.axis_size(axis)
+            most = rounds
+            for hop in range(1, size):
+                most = jnp.maximum(
+                    most,
+                    lax.ppermute(rounds, axis, [(i, (i + hop) % size) for i in range(size)]),
+                )
+            rounds = most
+        return rounds
+
+    def over_shares(partial):
+        return [partial] + [
+            lax.ppermute(partial, "mp", [(i, (i + hop) % shares) for i in range(shares)])
+            for hop in range(1, shares)
+        ]
+
+    def paired_round(key, row_rank):
+        firsts = (LANES // rank_extent) * jnp.arange(spots // LANES, dtype=jnp.int32)
+        block = first_block
+
+        def shrink(blocks, names):
+            return shrink_call(blocks, names, [flat_a], firsts, rank_extent)
+
+        def expand(blocks, partial, names, told=None):
+            return expand_call(
+                over_shares(partial),
+                names,
+                [flat_b],
+                firsts,
+                [rows_in.shape[0] for rows_in in blocks],
+                rank_extent,
+                told,
             )
-        rounds = most
-
+
+        near = list(range(1, host_count // 2))
+        far = list(range(host_count // 2, host_count))
+        order = near + far
+        order = far[:1] + near + far[1:]
+        first, last = far[0], far[-1]
+        packed = pack(first, 0, block, key, row_rank, 0)
+        received = {first: swap(packed, first)}
+        own_names = jnp.where(stays, named_row, 0).astype(jnp.float32)[:, None]
+        own_names, rounds, _ = lax.optimization_barrier((own_names, own_rounds, packed))
+        rounds = agree(rounds)[0]
+        partial, names = shrink([flat_x], own_names)
+        partial, key, row_rank = lax.optimization_barrier((partial, key, row_rank))
+        for s in near + far[1:-1]:
+            received[s] = swap(pack(s, 0, block, key, row_rank, 0), s)
+        packed = pack(last, 0, block, key, row_rank, rounds[0])
+        (base,) = expand([flat_x], partial, names)
+        base, packed = lax.optimization_barrier((base, packed))
+        received[last] = swap(packed, last)
+        returned = {}
+        for number, s in enumerate(order):
+            told = None if s == last else rounds
+            (adapted,) = expand([received[s]], *shrink([received[s]], None), told)
+            if s != last:
+                later = order[number + 1]
+                _, received[later] = lax.optimization_barrier((adapted, received[later]))
+            returned[s] = swap(adapted, s)
+        places = {s: place(s, 0, block, key, row_rank).T for s in order}
+        early = order[:-1]
+        base, told = back_call(
+            base, [places[s] for s in early], [returned[s] for s in early], True, 30
+        )
+        result = jnp.dot(places[last], returned[last], preferred_element_type=jnp.float32)
+        result = (result + base).astype(jnp.bfloat16)
+        told = jnp.maximum(told[0], received[last][block - 1, block - 1].astype(jnp.int32))
+        return result, jnp.maximum(told, rounds[0])
+
+    if paired and spots % LANES == 0 and LANES % rank_extent == 0:
+        result, rounds = paired_round(key, row_rank)
+    else:
+        own = adapt(flat_x, jnp.where(stays, named_row, 0)).astype(jnp.bfloat16)
+        result, rounds = one_round(0, first_block, own)
+        rounds = agree(rounds)[0, 0]
     def more(state):
         number, so_far = state
         start = first_block - 1 + number * (more_block - 1)
@@ -168,7 +413,7 @@
         return number + 1, so_far
 
     _, result = lax.while_loop(
-        lambda state: state[0] < rounds[0, 0], more, (jnp.int32(0), result)
+        lambda state: state[0] < rounds, more, (jnp.int32(0), result)
     )
     return result.reshape(steps, step_rows, width)
 

time: 130 us -> 107 us (0.82)
  the two profiles are of different devices: /device:TPU:24 before, /device:TPU:0 now
where the time goes in v4:
time: 107 us; the launch traced here: 106 us
  waiting for transfers between devices  39.7 us (37%)
  starting transfers between devices  27.7 us (26%)
  Pallas kernels  26.1 us (24%)
  matrix products  6.6 us (6%)
  other arithmetic  3.31 us (3%)
  between operations  2.21 us (2%)
    ppermute x6, waiting for transfers between devices, swap(): lax.ppermute(values, 'hst', [(i, i ^ step) for i in range(host_count)])  33.2 us
    ppermute x4, starting transfers between devices, over_shares(): lax.ppermute(partial, 'mp', [(i, (i + hop) % shares) for i in range(share...  16.5 us
    pallas_call x4, Pallas kernels, expand_call(): pl.pallas_call(functools.partial(expand_kernel, counts, len(partials), le...  12.5 us
    ppermute x6, starting transfers between devices, swap(): lax.ppermute(values, 'hst', [(i, i ^ step) for i in range(host_count)])  9.53 us
    pallas_call x4, Pallas kernels, shrink_call(): pl.pallas_call(functools.partial(shrink_kernel, counts, own_names is not...  8.69 us
    ppermute x4, waiting for transfers between devices, over_shares(): lax.ppermute(partial, 'mp', [(i, (i + hop) % shares) for i in range(share...  6.56 us
    pallas_call x1, Pallas kernels, back_call(): pl.pallas_call(functools.partial(back_kernel, len(returned)), grid=(width...  4.83 us
    dot_general x3, matrix products, pack(): jnp.dot(place(member, start, block, key, row_rank), flat_x, preferred_ele...  3.52 us
  transfers between devices with their start and end apart: 12, of which 7 were waited for; matrix products, arithmetic and copies ran while one was open for 3% of the time, Pallas kernels for 24%

profile of v4, /device:TPU:0, one launch (start us, length us, event | category | flops | bytes accessed | tf_op | source)
XLA Modules:
  0.0 106.4 jit_solution(1148306218239734058)
XLA Ops:
  0.0 0.8 bitcast_add_fusion
  0.8 0.1 eq.461
  0.9 0.8 select_reduce_fusion.7
  1.8 0.2 select_reduce_fusion.6
  2.0 0.2 fusion.74
  2.2 0.2 select_reduce_fusion.5
  2.4 2.6 %fusion.70 = bf16[88,3072]{1,0:T(8,128)(2,1)} fusion(bf16[256,3072]{1,0:T(8,128)(2,1)} %bitcast.140, bf16[3072]{0:T(1024)(128)(2,1)S(1)} %pad.29, pred[88]{0:T(512)(128)(4,1)S(1)} %get-tuple-element.320, s32[256]{0:T(256)S(1)} %fusion.74, pred[88]{0:T(512)(128)(4,1)S(1)} %get-tuple-element.319, pred[256]{0:T(512)(128)(4,1)S(1)} %get-tuple-element.303), kind=kOutput, calls=%fused_computation.124 | convolution fusion | flops 138749952 | bytes 2121136 | tf_op jit(solution)/shard_map/dot_general | solution.py:261
  5.0 4.0 %collective-permute-start.11 = (bf16[88,3072]{1,0:T(8,128)(2,1)}, bf16[88,3072]{1,0:T(8,128)(2,1)S(1)}, u32[]{:S(2)}, u32[]{:S(2)}) collective-permute-start(bf16[88,3072]{1,0:T(8,128)(2,1)} %fusion.70), channel_id=1, source_target_pairs={{0,8},{4,12},{8,0},{12,4},{1,9},{5,13},{9,1},{13,5},{2,10},{6,14},... | collective-permute-start | bytes 1622024 | tf_op jit(solution)/shard_map/ppermute | solution.py:270
  9.1 0.6 fusion.110
  10.4 0.1 copy.15
  10.5 0.1 fusion.78.refs_1_
  10.7 0.1 collective-permute-start.9
  10.8 3.7 %shard_map.73 = (f32[256,128]{1,0:T(8,128)S(1)}, f32[256,128]{1,0:T(8,128)S(1)}) custom-call(s32[4]{0:T(128)S(1)} %iota_multiply_fusion.first_ref, bf16[256,3072]{1,0:T(8,128)(2,1)S(1)} %bitcast.142, f32[256,1]{1,0:T(8,128)S(1)} %fusion.78.refs_1_, bf16[512,3072]{1,0:T(8,128)(2,1)} %bitcast.130), custom_call_target="tpu_custom_call" | custom-call | flops 805306368 | bytes 4718592 | tf_op jit(solution)/shard_map/pallas_call | solution.py:129
  14.5 0.0 copy-start.2
  14.5 1.6 %collective-permute-start.15 = (f32[256,128]{1,0:T(8,128)S(1)}, f32[256,128]{1,0:T(8,128)S(1)}, u32[]{:S(2)}, u32[]{:S(2)}) collective-permute-start(f32[256,128]{1,0:T(8,128)S(1)} %get-tuple-element.205.refs_0_), channel_id=1, source_target_pairs={{0,2},{2,0},{1,3},{3,1},{4,6},{6,4},{5,7},{7,5},{8,10},{10,8},{9,1... | collective-permute-start | bytes 393224 | tf_op jit(solution)/shard_map/ppermute | solution.py:345
  16.0 0.2 select_reduce_fusion.3
  16.3 0.0 collective-permute-done.9
  16.3 1.6 %collective-permute-start.10 = (s32[1,128]{1,0:T(1,128)S(1)}, s32[1,128]{1,0:T(1,128)S(1)}, u32[]{:S(2)}, u32[]{:S(2)}) collective-permute-start(s32[1,128]{1,0:T(1,128)S(1)} %broadcast_maximum_fusion), channel_id=1, source_target_pairs={{0,16},{16,0},{1,17},{17,1},{2,18},{18,2},{3,19},{19,3},{4,20},{20... | collective-permute-start | bytes 1544 | tf_op jit(solution)/shard_map/ppermute | solution.py:338
  17.9 0.4 fusion.71
  18.3 1.6 %collective-permute-start.13 = (bf16[88,3072]{1,0:T(8,128)(2,1)S(1)}, bf16[88,3072]{1,0:T(8,128)(2,1)S(1)}, u32[]{:S(2)}, u32[]{:S(2)}) collective-permute-start(bf16[88,3072]{1,0:T(8,128)(2,1)S(1)} %fusion.71), channel_id=1, source_target_pairs={{0,4},{4,0},{8,12},{12,8},{1,5},{5,1},{9,13},{13,9},{2,6},{6,2},{1... | collective-permute-start | bytes 1622024 | tf_op jit(solution)/shard_map/ppermute | solution.py:270
  20.0 0.0 collective-permute-done.10
  20.0 0.0 copy-start
  20.0 0.4 fusion.72
  20.5 0.0 collective-permute-done.15.refs_1_
  20.5 2.8 %shard_map.78.base_ref = bf16[256,3072]{1,0:T(8,128)(2,1)S(1)} custom-call(s32[4]{0:T(128)S(1)} %iota_multiply_fusion.first_ref, f32[256,128]{1,0:T(8,128)S(1)} %get-tuple-element.205.refs_0_, f32[256,128]{1,0:T(8,128)S(1)} %collective-permute-done.15.refs_1_, f32[256,128]{1,0:T(8,128)S(1)} %get-tuple-element.206.refs_2_, bf16[512,3072]{1,0:T(8,128)(2,1)S(1)} %bitcast.137), custom_call_target="tpu_custom_call" | custom-call | flops 805306368 | bytes 4718592 | tf_op jit(solution)/shard_map/pallas_call | solution.py:174
  23.3 1.4 %collective-permute-start.16 = (bf16[88,3072]{1,0:T(8,128)(2,1)S(1)}, bf16[88,3072]{1,0:T(8,128)(2,1)S(1)}, u32[]{:S(2)}, u32[]{:S(2)}) collective-permute-start(bf16[88,3072]{1,0:T(8,128)(2,1)S(1)} %fusion.72), channel_id=1, source_target_pairs={{0,12},{4,8},{8,4},{12,0},{1,13},{5,9},{9,5},{13,1},{2,14},{6,10},... | collective-permute-start | bytes 1622024 | tf_op jit(solution)/shard_map/ppermute | solution.py:270
  24.6 10.2 %collective-permute-done.11.refs_0_ = bf16[88,3072]{1,0:T(8,128)(2,1)S(1)} collective-permute-done((bf16[88,3072]{1,0:T(8,128)(2,1)}, bf16[88,3072]{1,0:T(8,128)(2,1)S(1)}, u32[]{:S(2)}, u32[]{:S(2)}) %collective-permute-start.11) | collective-permute-done | bytes 540704 | tf_op jit(solution)/shard_map/ppermute | solution.py:270
  34.9 1.7 %shard_map.74 = (f32[88,128]{1,0:T(8,128)S(1)}, f32[88,128]{1,0:T(8,128)S(1)}) custom-call(s32[4]{0:T(128)S(1)} %iota_multiply_fusion.first_ref, bf16[88,3072]{1,0:T(8,128)(2,1)S(1)} %collective-permute-done.11.refs_0_, bf16[512,3072]{1,0:T(8,128)(2,1)S(1)} %bitcast.132), custom_call_target="tpu_custom_call" | custom-call | flops 276824064 | bytes 3686400 | tf_op jit(solution)/shard_map/pallas_call | solution.py:129
  36.6 12.7 %collective-permute-start.12 = (f32[88,128]{1,0:T(8,128)S(1)}, f32[88,128]{1,0:T(8,128)S(1)}, u32[]{:S(2)}, u32[]{:S(2)}) collective-permute-start(f32[88,128]{1,0:T(8,128)S(1)} %get-tuple-element.200.refs_1_), channel_id=1, source_target_pairs={{0,2},{2,0},{1,3},{3,1},{4,6},{6,4},{5,7},{7,5},{8,10},{10,8},{9,1... | collective-permute-start | bytes 135176 | tf_op jit(solution)/shard_map/ppermute | solution.py:345
  49.2 2.0 %collective-permute-done.12.refs_2_ = f32[88,128]{1,0:T(8,128)S(1)} collective-permute-done((f32[88,128]{1,0:T(8,128)S(1)}, f32[88,128]{1,0:T(8,128)S(1)}, u32[]{:S(2)}, u32[]{:S(2)}) %collective-permute-start.12) | collective-permute-done | bytes 45088 | tf_op jit(solution)/shard_map/ppermute | solution.py:345
  51.3 2.3 %shard_map.75 = bf16[88,3072]{1,0:T(8,128)(2,1)S(1)} custom-call(s32[4]{0:T(128)S(1)} %iota_multiply_fusion.first_ref, s32[128]{0:T(128)S(1)} %bitcast.127, f32[88,128]{1,0:T(8,128)S(1)} %get-tuple-element.200.refs_1_, f32[88,128]{1,0:T(8,128)S(1)} %collective-permute-done.12.refs_2_, f32[88,128]{1,0:T(8,128)S(1)} %get-tuple-element.201.refs_3_, ...), custom_call_target="tpu_custom_call" | custom-call | flops 276824064 | bytes 3686400 | tf_op jit(solution)/shard_map/pallas_call | solution.py:174
  53.5 1.0 collective-permute-done.13.refs_0_
  54.5 1.7 %shard_map.76 = (f32[88,128]{1,0:T(8,128)S(1)}, f32[88,128]{1,0:T(8,128)S(1)}) custom-call(s32[4]{0:T(128)S(1)} %iota_multiply_fusion.first_ref, bf16[88,3072]{1,0:T(8,128)(2,1)S(1)} %collective-permute-done.13.refs_0_, bf16[512,3072]{1,0:T(8,128)(2,1)S(1)} %bitcast.133), custom_call_target="tpu_custom_call" | custom-call | flops 276824064 | bytes 3686400 | tf_op jit(solution)/shard_map/pallas_call | solution.py:129
  56.2 1.1 %collective-permute-start.14 = (f32[88,128]{1,0:T(8,128)S(1)}, f32[88,128]{1,0:T(8,128)S(1)}, u32[]{:S(2)}, u32[]{:S(2)}) collective-permute-start(f32[88,128]{1,0:T(8,128)S(1)} %get-tuple-element.203.refs_1_), channel_id=1, source_target_pairs={{0,2},{2,0},{1,3},{3,1},{4,6},{6,4},{5,7},{7,5},{8,10},{10,8},{9,1... | collective-permute-start | bytes 135176 | tf_op jit(solution)/shard_map/ppermute | solution.py:345
  57.3 3.0 %collective-permute-done.14.refs_2_ = f32[88,128]{1,0:T(8,128)S(1)} collective-permute-done((f32[88,128]{1,0:T(8,128)S(1)}, f32[88,128]{1,0:T(8,128)S(1)}, u32[]{:S(2)}, u32[]{:S(2)}) %collective-permute-start.14) | collective-permute-done | bytes 45088 | tf_op jit(solution)/shard_map/ppermute | solution.py:345
  60.3 2.3 %shard_map.77 = bf16[88,3072]{1,0:T(8,128)(2,1)S(1)} custom-call(s32[4]{0:T(128)S(1)} %iota_multiply_fusion.first_ref, s32[128]{0:T(128)S(1)} %bitcast.128, f32[88,128]{1,0:T(8,128)S(1)} %get-tuple-element.203.refs_1_, f32[88,128]{1,0:T(8,128)S(1)} %collective-permute-done.14.refs_2_, f32[88,128]{1,0:T(8,128)S(1)} %get-tuple-element.204.refs_3_, ...), custom_call_target="tpu_custom_call" | custom-call | flops 276824064 | bytes 3686400 | tf_op jit(solution)/shard_map/pallas_call | solution.py:174
  62.6 0.1 collective-permute-start.20
  62.6 1.7 %shard_map.79 = (f32[88,128]{1,0:T(8,128)S(1)}, f32[88,128]{1,0:T(8,128)S(1)}) custom-call(s32[4]{0:T(128)S(1)} %iota_multiply_fusion.first_ref, bf16[88,3072]{1,0:T(8,128)(2,1)S(1)} %collective-permute-done.16.refs_0_, bf16[512,3072]{1,0:T(8,128)(2,1)S(1)} %bitcast.134), custom_call_target="tpu_custom_call" | custom-call | flops 276824064 | bytes 3686400 | tf_op jit(solution)/shard_map/pallas_call | solution.py:129
  64.3 1.1 %collective-permute-start.17 = (f32[88,128]{1,0:T(8,128)S(1)}, f32[88,128]{1,0:T(8,128)S(1)}, u32[]{:S(2)}, u32[]{:S(2)}) collective-permute-start(f32[88,128]{1,0:T(8,128)S(1)} %get-tuple-element.209.refs_0_), channel_id=1, source_target_pairs={{0,2},{2,0},{1,3},{3,1},{4,6},{6,4},{5,7},{7,5},{8,10},{10,8},{9,1... | collective-permute-start | bytes 135176 | tf_op jit(solution)/shard_map/ppermute | solution.py:345
  65.4 0.2 fusion.85
  65.6 0.6 slice.164
  66.9 1.6 %collective-permute-done.17.refs_1_ = f32[88,128]{1,0:T(8,128)S(1)} collective-permute-done((f32[88,128]{1,0:T(8,128)S(1)}, f32[88,128]{1,0:T(8,128)S(1)}, u32[]{:S(2)}, u32[]{:S(2)}) %collective-permute-start.17) | collective-permute-done | bytes 45088 | tf_op jit(solution)/shard_map/ppermute | solution.py:345
  68.4 5.2 %shard_map.80 = bf16[88,3072]{1,0:T(8,128)(2,1)} custom-call(s32[4]{0:T(128)S(1)} %iota_multiply_fusion.first_ref, f32[88,128]{1,0:T(8,128)S(1)} %get-tuple-element.209.refs_0_, f32[88,128]{1,0:T(8,128)S(1)} %collective-permute-done.17.refs_1_, f32[88,128]{1,0:T(8,128)S(1)} %get-tuple-element.210.refs_2_, bf16[512,3072]{1,0:T(8,128)(2,1)} %bitcast.135), custom_call_target="tpu_custom_call" | custom-call | flops 276824064 | bytes 3686400 | tf_op jit(solution)/shard_map/pallas_call | solution.py:174
  73.7 2.4 %collective-permute-start.18 = (bf16[88,3072]{1,0:T(8,128)(2,1)}, bf16[88,3072]{1,0:T(8,128)(2,1)}, u32[]{:S(2)}, u32[]{:S(2)}) collective-permute-start(bf16[88,3072]{1,0:T(8,128)(2,1)} %shard_map.80), channel_id=1, source_target_pairs={{0,12},{4,8},{8,4},{12,0},{1,13},{5,9},{9,5},{13,1},{2,14},{6,10},... | collective-permute-start | bytes 1622024 | tf_op jit(solution)/shard_map/ppermute | solution.py:270
  76.1 8.1 %collective-permute-done.19.refs_2_ = bf16[88,3072]{1,0:T(8,128)(2,1)} collective-permute-done((bf16[88,3072]{1,0:T(8,128)(2,1)S(1)}, bf16[88,3072]{1,0:T(8,128)(2,1)}, u32[]{:S(2)}, u32[]{:S(2)}) %collective-permute-start.19) | collective-permute-done | bytes 540704 | tf_op jit(solution)/shard_map/ppermute | solution.py:270
  84.2 13.8 %collective-permute-done.20.refs_3_ = bf16[88,3072]{1,0:T(8,128)(2,1)} collective-permute-done((bf16[88,3072]{1,0:T(8,128)(2,1)S(1)}, bf16[88,3072]{1,0:T(8,128)(2,1)}, u32[]{:S(2)}, u32[]{:S(2)}) %collective-permute-start.20) | collective-permute-done | bytes 540704 | tf_op jit(solution)/shard_map/ppermute | solution.py:270
  98.0 4.8 %shard_map.81 = (bf16[256,3072]{1,0:T(8,128)(2,1)S(1)}, s32[1]{0:T(128)}) custom-call(bf16[256,3072]{1,0:T(8,128)(2,1)S(1)} %shard_map.78.base_ref, bf16[256,88]{1,0:T(8,128)(2,1)S(1)} %get-tuple-element.315.refs_0_, bf16[256,88]{1,0:T(8,128)(2,1)S(1)} %get-tuple-element.314.refs_1_, bf16[88,3072]{1,0:T(8,128)(2,1)} %collective-permute-done.19.refs_2_, ...), custom_call_target="tpu_custom_call" | custom-call | flops 8304721920 | bytes 94371840 | tf_op jit(solution)/shard_map/pallas_call | solution.py:150
  103.5 2.9 %fusion.69 = bf16[256,3072]{1,0:T(8,128)(2,1)} fusion(bf16[88,3072]{1,0:T(8,128)(2,1)} %collective-permute-done.18, bf16[256,3072]{1,0:T(8,128)(2,1)S(1)} %get-tuple-element.212, s32[256]{0:T(256)S(1)} %fusion.74, pred[88]{0:T(512)(128)(4,1)S(1)} %get-tuple-element.319, pred[256]{0:T(512)(128)(4,1)S(1)} %get-tuple-element.318), kind=kOutput, calls=%fused_computation.120 | convolution fusion | flops 140838912 | bytes 3687768 | tf_op jit(solution)/shard_map/dot_general | solution.py:398
  (24 shorter events, 0.2 us)
Async XLA Ops:
  0.0 10.8 %copy-start.4 = (bf16[4,64,3072]{2,1,0:T(8,128)(2,1)S(1)}, bf16[4,64,3072]{2,1,0:T(8,128)(2,1)}, u32[]{:S(2)}) copy-start(bf16[4,64,3072]{2,1,0:T(8,128)(2,1)} %param.9) | copy-start | bytes 4718596
  5.0 29.9 %collective-permute-start.11 = (bf16[88,3072]{1,0:T(8,128)(2,1)}, bf16[88,3072]{1,0:T(8,128)(2,1)S(1)}, u32[]{:S(2)}, u32[]{:S(2)}) collective-permute-start(bf16[88,3072]{1,0:T(8,128)(2,1)} %fusion.70), channel_id=1, source_target_pairs={{0,8},{4,12},{8,0},{12,4},{1,9},{5,13},{9,1},{13,5},{2,10},{6,14},... | collective-permute-start | bytes 1622024 | tf_op jit(solution)/shard_map/ppermute | solution.py:270
  10.7 5.6 %collective-permute-start.9 = (s32[1,128]{1,0:T(1,128)S(1)}, s32[1,128]{1,0:T(1,128)S(1)}, u32[]{:S(2)}, u32[]{:S(2)}) collective-permute-start(s32[1,128]{1,0:T(1,128)S(1)} %broadcast_in_dim.320), channel_id=1, source_target_pairs={{0,1},{1,0},{2,3},{3,2},{4,5},{5,4},{6,7},{7,6},{8,9},{9,8},{10,11... | collective-permute-start | bytes 1544 | tf_op jit(solution)/shard_map/ppermute | solution.py:338
  14.5 6.0 %copy-start.2 = (bf16[32,16,3072]{2,1,0:T(8,128)(2,1)S(1)}, bf16[32,16,3072]{2,1,0:T(8,128)(2,1)}, u32[]{:S(2)}) copy-start(bf16[32,16,3072]{2,1,0:T(8,128)(2,1)} %param.11) | copy-start | bytes 9437188
  14.5 6.0 %collective-permute-start.15 = (f32[256,128]{1,0:T(8,128)S(1)}, f32[256,128]{1,0:T(8,128)S(1)}, u32[]{:S(2)}, u32[]{:S(2)}) collective-permute-start(f32[256,128]{1,0:T(8,128)S(1)} %get-tuple-element.205.refs_0_), channel_id=1, source_target_pairs={{0,2},{2,0},{1,3},{3,1},{4,6},{6,4},{5,7},{7,5},{8,10},{10,8},{9,1... | collective-permute-start | bytes 393224 | tf_op jit(solution)/shard_map/ppermute | solution.py:345
  16.3 3.7 %collective-permute-start.10 = (s32[1,128]{1,0:T(1,128)S(1)}, s32[1,128]{1,0:T(1,128)S(1)}, u32[]{:S(2)}, u32[]{:S(2)}) collective-permute-start(s32[1,128]{1,0:T(1,128)S(1)} %broadcast_maximum_fusion), channel_id=1, source_target_pairs={{0,16},{16,0},{1,17},{17,1},{2,18},{18,2},{3,19},{19,3},{4,20},{20... | collective-permute-start | bytes 1544 | tf_op jit(solution)/shard_map/ppermute | solution.py:338
  18.3 36.2 %collective-permute-start.13 = (bf16[88,3072]{1,0:T(8,128)(2,1)S(1)}, bf16[88,3072]{1,0:T(8,128)(2,1)S(1)}, u32[]{:S(2)}, u32[]{:S(2)}) collective-permute-start(bf16[88,3072]{1,0:T(8,128)(2,1)S(1)} %fusion.71), channel_id=1, source_target_pairs={{0,4},{4,0},{8,12},{12,8},{1,5},{5,1},{9,13},{13,9},{2,6},{6,2},{1... | collective-permute-start | bytes 1622024 | tf_op jit(solution)/shard_map/ppermute | solution.py:270
  20.0 14.9 %copy-start = (bf16[32,16,3072]{2,1,0:T(8,128)(2,1)S(1)}, bf16[32,16,3072]{2,1,0:T(8,128)(2,1)}, u32[]{:S(2)}) copy-start(bf16[32,16,3072]{2,1,0:T(8,128)(2,1)} %param.10) | copy-start | bytes 9437188
  23.3 39.3 %collective-permute-start.16 = (bf16[88,3072]{1,0:T(8,128)(2,1)S(1)}, bf16[88,3072]{1,0:T(8,128)(2,1)S(1)}, u32[]{:S(2)}, u32[]{:S(2)}) collective-permute-start(bf16[88,3072]{1,0:T(8,128)(2,1)S(1)} %fusion.72), channel_id=1, source_target_pairs={{0,12},{4,8},{8,4},{12,0},{1,13},{5,9},{9,5},{13,1},{2,14},{6,10},... | collective-permute-start | bytes 1622024 | tf_op jit(solution)/shard_map/ppermute | solution.py:270
  36.6 14.7 %collective-permute-start.12 = (f32[88,128]{1,0:T(8,128)S(1)}, f32[88,128]{1,0:T(8,128)S(1)}, u32[]{:S(2)}, u32[]{:S(2)}) collective-permute-start(f32[88,128]{1,0:T(8,128)S(1)} %get-tuple-element.200.refs_1_), channel_id=1, source_target_pairs={{0,2},{2,0},{1,3},{3,1},{4,6},{6,4},{5,7},{7,5},{8,10},{10,8},{9,1... | collective-permute-start | bytes 135176 | tf_op jit(solution)/shard_map/ppermute | solution.py:345
  56.2 4.1 %collective-permute-start.14 = (f32[88,128]{1,0:T(8,128)S(1)}, f32[88,128]{1,0:T(8,128)S(1)}, u32[]{:S(2)}, u32[]{:S(2)}) collective-permute-start(f32[88,128]{1,0:T(8,128)S(1)} %get-tuple-element.203.refs_1_), channel_id=1, source_target_pairs={{0,2},{2,0},{1,3},{3,1},{4,6},{6,4},{5,7},{7,5},{8,10},{10,8},{9,1... | collective-permute-start | bytes 135176 | tf_op jit(solution)/shard_map/ppermute | solution.py:345
  57.3 26.9 %collective-permute-start.19 = (bf16[88,3072]{1,0:T(8,128)(2,1)S(1)}, bf16[88,3072]{1,0:T(8,128)(2,1)}, u32[]{:S(2)}, u32[]{:S(2)}) collective-permute-start(bf16[88,3072]{1,0:T(8,128)(2,1)S(1)} %shard_map.75), channel_id=1, source_target_pairs={{0,8},{4,12},{8,0},{12,4},{1,9},{5,13},{9,1},{13,5},{2,10},{6,14},... | collective-permute-start | bytes 1622024 | tf_op jit(solution)/shard_map/ppermute | solution.py:270
  62.6 35.5 %collective-permute-start.20 = (bf16[88,3072]{1,0:T(8,128)(2,1)S(1)}, bf16[88,3072]{1,0:T(8,128)(2,1)}, u32[]{:S(2)}, u32[]{:S(2)}) collective-permute-start(bf16[88,3072]{1,0:T(8,128)(2,1)S(1)} %shard_map.77), channel_id=1, source_target_pairs={{0,4},{4,0},{8,12},{12,8},{1,5},{5,1},{9,13},{13,9},{2,6},{6,2},{1... | collective-permute-start | bytes 1622024 | tf_op jit(solution)/shard_map/ppermute | solution.py:270
  64.3 4.1 %collective-permute-start.17 = (f32[88,128]{1,0:T(8,128)S(1)}, f32[88,128]{1,0:T(8,128)S(1)}, u32[]{:S(2)}, u32[]{:S(2)}) collective-permute-start(f32[88,128]{1,0:T(8,128)S(1)} %get-tuple-element.209.refs_0_), channel_id=1, source_target_pairs={{0,2},{2,0},{1,3},{3,1},{4,6},{6,4},{5,7},{7,5},{8,10},{10,8},{9,1... | collective-permute-start | bytes 135176 | tf_op jit(solution)/shard_map/ppermute | solution.py:345
  73.7 29.9 %collective-permute-start.18 = (bf16[88,3072]{1,0:T(8,128)(2,1)}, bf16[88,3072]{1,0:T(8,128)(2,1)}, u32[]{:S(2)}, u32[]{:S(2)}) collective-permute-start(bf16[88,3072]{1,0:T(8,128)(2,1)} %shard_map.80), channel_id=1, source_target_pairs={{0,12},{4,8},{8,4},{12,0},{1,13},{5,9},{9,5},{13,1},{2,14},{6,10},... | collective-permute-start | bytes 1622024 | tf_op jit(solution)/shard_map/ppermute | solution.py:270

commit v5 on v4

--- a/solution.py
+++ b/solution.py
@@ -100,6 +100,66 @@
         offset += count
 
 
+def route_kernel(
+    block, member, local_adapters, me_ref, source_ref, wanted_ref, x_ref, packed_ref, route_ref, most_ref
+):
+    table = source_ref.shape[1]
+    rows = x_ref.shape[0]
+    down = lax.broadcasted_iota(jnp.int32, (table, table), 0)
+    across = lax.broadcasted_iota(jnp.int32, (table, table), 1)
+    source = jnp.sum(jnp.where(down == across, source_ref[...], 0), axis=1, keepdims=True)
+    wanted = wanted_ref[...]
+    entry = lax.broadcasted_iota(jnp.int32, (table, rows), 0)
+    served = jnp.sum(jnp.where(entry == wanted, source, 0), axis=0, keepdims=True)
+    owner = lax.div(served, jnp.int32(local_adapters))
+    name = served - owner * local_adapters + 1
+    key = owner ^ me_ref[0]
+    member_of = lax.broadcasted_iota(jnp.int32, (8, rows), 0) == key
+    earlier = lax.broadcasted_iota(jnp.int32, (rows, rows), 0) < lax.broadcasted_iota(
+        jnp.int32, (rows, rows), 1
+    )
+    before = jnp.dot(
+        member_of.astype(jnp.bfloat16),
+        earlier.astype(jnp.bfloat16),
+        preferred_element_type=jnp.float32,
+    ).astype(jnp.int32)
+    rank = jnp.sum(jnp.where(member_of, before, 0), axis=0, keepdims=True)
+    most_ref[0] = jnp.max(jnp.where(key == 0, 0, rank + 1))
+    line = lax.broadcasted_iota(jnp.int32, (8, rows), 0)
+    route_ref[...] = jnp.where(line == 0, key, jnp.where(line == 1, rank, name))
+
+    slot = lax.broadcasted_iota(jnp.int32, (block, rows), 0)
+    chosen = (key == member) & (slot == rank) & (slot < block - 1)
+    names = jnp.sum(jnp.where(chosen, name, 0), axis=1, keepdims=True)
+    turn = lax.broadcasted_iota(jnp.int32, (block, LANES), 0) == lax.broadcasted_iota(
+        jnp.int32, (block, LANES), 1
+    )
+    names = jnp.sum(jnp.where(turn, names, 0), axis=0, keepdims=True).astype(jnp.float32)
+    packed = jnp.dot(
+        chosen.astype(jnp.bfloat16), x_ref[...], preferred_element_type=jnp.float32
+    )
+    packed_ref[...] = packed.astype(packed_ref.dtype)
+    last = lax.broadcasted_iota(jnp.int32, (block, LANES), 0) == block - 1
+    packed_ref[:, :LANES] = jnp.where(last, names, packed[:, :LANES]).astype(packed_ref.dtype)
+
+
+def route_call(me, source, wanted, flat_x, block, member, local_adapters):
+    rows, width = flat_x.shape
+    whole = pl.BlockSpec(memory_space=pltpu.VMEM)
+    scalar = pl.BlockSpec(memory_space=pltpu.SMEM)
+    return pl.pallas_call(
+        functools.partial(route_kernel, block, member, local_adapters),
+        out_shape=(
+            jax.ShapeDtypeStruct((block, width), jnp.bfloat16),
+            jax.ShapeDtypeStruct((8, rows), jnp.int32),
+            jax.ShapeDtypeStruct((1,), jnp.int32),
+        ),
+        in_specs=[scalar, whole, whole, whole],
+        out_specs=(whole, whole, scalar),
+        compiler_params=pltpu.CompilerParams(vmem_limit_bytes=VMEM_BYTES),
+    )(me.reshape(1), source.reshape(1, -1), wanted.reshape(1, -1), flat_x)
+
+
 def back_kernel(blocks, base_ref, *refs):
     places, returned, outs = refs[:blocks], refs[blocks : 2 * blocks], refs[2 * blocks :]
     out_ref = outs[0]
@@ -223,21 +283,31 @@
         axis=1,
     )
     wanted = (target_host[:, :, 0] * local_adapters + target_position).reshape(rows)
-    served = jnp.sum(jnp.where(wanted[:, None] == table[None, :], source[None, :], 0), axis=1)
-    owner = served // local_adapters
-    named_row = served % local_adapters + 1
-    stays = owner == me
-    key = owner ^ me if paired else jnp.where(stays, host_count, owner)
-
-    hosts = jnp.arange(host_count, dtype=jnp.int32)
-    in_block = key[:, None] == hosts[None, :]
-    row_ids = jnp.arange(rows, dtype=jnp.int32)
-    earlier = (row_ids[None, :] < row_ids[:, None]).astype(jnp.bfloat16)
-    before = jnp.dot(
-        earlier, in_block.astype(jnp.bfloat16), preferred_element_type=jnp.float32
-    ).astype(jnp.int32)
-    row_rank = jnp.sum(jnp.where(in_block, before, 0), axis=1)
-    left = jnp.max(jnp.where(stays, 0, row_rank + 1)) - (first_block - 1)
+
+    def route():
+        served = jnp.sum(jnp.where(wanted[:, None] == table[None, :], source[None, :], 0), axis=1)
+        owner = served // local_adapters
+        key = owner ^ me if paired else jnp.where(owner == me, host_count, owner)
+        in_block = key[:, None] == jnp.arange(host_count, dtype=jnp.int32)[None, :]
+        row_ids = jnp.arange(rows, dtype=jnp.int32)
+        earlier = (row_ids[None, :] < row_ids[:, None]).astype(jnp.bfloat16)
+        before = jnp.dot(
+            earlier, in_block.astype(jnp.bfloat16), preferred_element_type=jnp.float32
+        ).astype(jnp.int32)
+        row_rank = jnp.sum(jnp.where(in_block, before, 0), axis=1)
+        most = jnp.max(jnp.where(owner == me, 0, row_rank + 1))
+        return key, row_rank, served % local_adapters + 1, owner == me, most
+
+    tiled = paired and spots % LANES == 0 and LANES % rank_extent == 0
+    if tiled:
+        first_packed, lines, most = route_call(
+            me, source, wanted, flat_x, first_block, host_count // 2, local_adapters
+        )
+        key, row_rank, named_row, most = lines[0], lines[1], lines[2], most[0]
+        stays = key == 0
+    else:
+        key, row_rank, named_row, stays, most = route()
+    left = most - (first_block - 1)
     own_rounds = jnp.maximum(0, (left + more_block - 2) // (more_block - 1))
 
     columns = jnp.arange(width, dtype=jnp.int32)
@@ -369,7 +439,7 @@
         order = near + far
         order = far[:1] + near + far[1:]
         first, last = far[0], far[-1]
-        packed = pack(first, 0, block, key, row_rank, 0)
+        packed = first_packed
         received = {first: swap(packed, first)}
         own_names = jnp.where(stays, named_row, 0).astype(jnp.float32)[:, None]
         own_names, rounds, _ = lax.optimization_barrier((own_names, own_rounds, packed))
@@ -395,12 +465,13 @@
         base, told = back_call(
             base, [places[s] for s in early], [returned[s] for s in early], True, 30
         )
-        result = jnp.dot(places[last], returned[last], preferred_element_type=jnp.float32)
+        base, place_last = lax.optimization_barrier((base, places[last]))
+        result = jnp.dot(place_last, returned[last], preferred_element_type=jnp.float32)
         result = (result + base).astype(jnp.bfloat16)
         told = jnp.maximum(told[0], received[last][block - 1, block - 1].astype(jnp.int32))
         return result, jnp.maximum(told, rounds[0])
 
-    if paired and spots % LANES == 0 and LANES % rank_extent == 0:
+    if tiled:
         result, rounds = paired_round(key, row_rank)
     else:
         own = adapt(flat_x, jnp.where(stays, named_row, 0)).astype(jnp.bfloat16)

time: 107 us -> 106 us (level)
  Pallas kernels: 26.1 us -> 29.5 us
  matrix products: 6.6 us -> 3.63 us
  other arithmetic: 3.31 us -> 2.04 us
    ppermute x6, waiting for transfers between devices: 33.2 us -> 29.8 us  [swap(): lax.ppermute(values, 'hst', [(i, i ^ step) for i in range(host_count)])]
    pallas_call x0 -> x1, Pallas kernels: none -> 2.98 us  [route_call(): pl.pallas_call(functools.partial(route_kernel, block, member, local_adapt...]
    dot_general x3 -> x2, matrix products: 3.52 us -> 0.87 us  [pack(): jnp.dot(place(member, start, block, key, row_rank), flat_x, preferred_ele...]
    ppermute x4, waiting for transfers between devices: 6.56 us -> 8.73 us  [over_shares(): lax.ppermute(partial, 'mp', [(i, (i + hop) % shares) for i in range(share...]
    ppermute x2, waiting for transfers between devices: 0.01 us -> 2.02 us  [agree(): lax.ppermute(rounds, axis, [(i, (i + hop) % size) for i in range(size)])]
    ppermute x6, starting transfers between devices: 9.53 us -> 8.35 us  [swap(): lax.ppermute(values, 'hst', [(i, i ^ step) for i in range(host_count)])]
    dot_general x2 -> x1, matrix products: 3.08 us -> 2.76 us  [paired_round(): jnp.dot(place_last, returned[last], preferred_element_type=jnp.float32)]
  transfers between devices with their start and end apart: 12 -> 12, of which waited for: 7 -> 9; matrix products, arithmetic and copies ran while one was open for 3% -> 2% of each run, Pallas kernels for 24% -> 25%
where the time goes in v5:
time: 106 us
  waiting for transfers between devices  40.6 us (38%)
  Pallas kernels  29.5 us (28%)
  starting transfers between devices  26.9 us (25%)
  matrix products  3.63 us (3%)
  between operations  2.23 us (2%)
  other arithmetic  2.04 us (2%)
    ppermute x6, waiting for transfers between devices, swap(): lax.ppermute(values, 'hst', [(i, i ^ step) for i in range(host_count)])  29.8 us
    ppermute x4, starting transfers between devices, over_shares(): lax.ppermute(partial, 'mp', [(i, (i + hop) % shares) for i in range(share...  16.9 us
    pallas_call x4, Pallas kernels, expand_call(): pl.pallas_call(functools.partial(expand_kernel, counts, len(partials), le...  12.5 us
    pallas_call x4, Pallas kernels, shrink_call(): pl.pallas_call(functools.partial(shrink_kernel, counts, own_names is not...  9.16 us
    ppermute x4, waiting for transfers between devices, over_shares(): lax.ppermute(partial, 'mp', [(i, (i + hop) % shares) for i in range(share...  8.73 us
    ppermute x6, starting transfers between devices, swap(): lax.ppermute(values, 'hst', [(i, i ^ step) for i in range(host_count)])  8.35 us
    pallas_call x1, Pallas kernels, back_call(): pl.pallas_call(functools.partial(back_kernel, len(returned)), grid=(width...  4.83 us
    pallas_call x1, Pallas kernels, route_call(): pl.pallas_call(functools.partial(route_kernel, block, member, local_adapt...  2.98 us
  transfers between devices with their start and end apart: 12, of which 9 were waited for; matrix products, arithmetic and copies ran while one was open for 2% of the time, Pallas kernels for 25%

profile of v5, /device:TPU:0, one launch (start us, length us, event | category | flops | bytes accessed | tf_op | source)
XLA Modules:
  0.0 105.7 jit_solution(8938591827309478241)
XLA Ops:
  0.0 0.7 bitcast_add_fusion
  0.7 0.1 reshape_reshape.3.wanted_ref
  0.8 0.8 select_reduce_fusion.5
  1.6 0.0 copy-start.4
  1.6 3.0 %shard_map.73 = (bf16[88,3072]{1,0:T(8,128)(2,1)}, s32[8,256]{1,0:T(8,128)S(1)}, s32[1]{0:T(128)}) custom-call(s32[1]{0:T(128)} %bitcast.1.me_ref, s32[1,128]{1,0:T(1,128)S(1)} %bitcast.144, s32[1,256]{1,0:T(1,128)S(1)} %reshape_reshape.3.wanted_ref, bf16[256,3072]{1,0:T(8,128)(2,1)} %bitcast.155), custom_call_target="tpu_custom_call" | custom-call | tf_op jit(solution)/shard_map/pallas_call | solution.py:150
  4.6 4.1 %collective-permute-start.12 = (bf16[88,3072]{1,0:T(8,128)(2,1)}, bf16[88,3072]{1,0:T(8,128)(2,1)S(1)}, u32[]{:S(2)}, u32[]{:S(2)}) collective-permute-start(bf16[88,3072]{1,0:T(8,128)(2,1)} %get-tuple-element.202), channel_id=1, source_target_pairs={{0,8},{4,12},{8,0},{12,4},{1,9},{5,13},{9,1},{13,5},{2,10},{6,14},... | collective-permute-start | bytes 1622024 | tf_op jit(solution)/shard_map/ppermute | solution.py:340
  9.5 0.1 collective-permute-start.10
  9.6 0.1 copy.12.refs_1_
  9.7 4.2 %shard_map.74 = (f32[256,128]{1,0:T(8,128)S(1)}, f32[256,128]{1,0:T(8,128)S(1)}) custom-call(s32[4]{0:T(128)S(1)} %iota_multiply_fusion.first_ref, bf16[256,3072]{1,0:T(8,128)(2,1)} %bitcast.156, f32[256,1]{1,0:T(8,128)S(1)} %copy.12.refs_1_, bf16[512,3072]{1,0:T(8,128)(2,1)} %bitcast.145), custom_call_target="tpu_custom_call" | custom-call | flops 805306368 | bytes 4718592 | tf_op jit(solution)/shard_map/pallas_call | solution.py:189
  13.9 0.0 copy-start.2
  13.9 0.2 select_reduce_fusion.3
  14.1 0.0 collective-permute-done.10
  14.1 1.6 %collective-permute-start.11 = (s32[1,128]{1,0:T(1,128)S(1)}, s32[1,128]{1,0:T(1,128)S(1)}, u32[]{:S(2)}, u32[]{:S(2)}) collective-permute-start(s32[1,128]{1,0:T(1,128)S(1)} %broadcast_maximum_fusion), channel_id=1, source_target_pairs={{0,16},{16,0},{1,17},{17,1},{2,18},{18,2},{3,19},{19,3},{4,20},{20... | collective-permute-start | bytes 1544 | tf_op jit(solution)/shard_map/ppermute | solution.py:408
  15.7 2.0 %collective-permute-done.11 = s32[1,128]{1,0:T(1,128)S(1)} collective-permute-done((s32[1,128]{1,0:T(1,128)S(1)}, s32[1,128]{1,0:T(1,128)S(1)}, u32[]{:S(2)}, u32[]{:S(2)}) %collective-permute-start.11) | collective-permute-done | bytes 544 | tf_op jit(solution)/shard_map/ppermute | solution.py:408
  17.8 0.0 copy-done.4
  17.8 0.4 fusion.71
  18.3 1.6 %collective-permute-start.15 = (bf16[88,3072]{1,0:T(8,128)(2,1)S(1)}, bf16[88,3072]{1,0:T(8,128)(2,1)S(1)}, u32[]{:S(2)}, u32[]{:S(2)}) collective-permute-start(bf16[88,3072]{1,0:T(8,128)(2,1)S(1)} %fusion.71), channel_id=1, source_target_pairs={{0,4},{4,0},{8,12},{12,8},{1,5},{5,1},{9,13},{13,9},{2,6},{6,2},{1... | collective-permute-start | bytes 1622024 | tf_op jit(solution)/shard_map/ppermute | solution.py:340
  19.9 1.5 %collective-permute-start.9 = (f32[256,128]{1,0:T(8,128)S(1)}, f32[256,128]{1,0:T(8,128)S(1)}, u32[]{:S(2)}, u32[]{:S(2)}) collective-permute-start(f32[256,128]{1,0:T(8,128)S(1)} %get-tuple-element.205.refs_0_), channel_id=1, source_target_pairs={{0,2},{2,0},{1,3},{3,1},{4,6},{6,4},{5,7},{7,5},{8,10},{10,8},{9,1... | collective-permute-start | bytes 393224 | tf_op jit(solution)/shard_map/ppermute | solution.py:415
  21.4 0.4 fusion.70
  21.8 3.0 %collective-permute-done.9.refs_1_ = f32[256,128]{1,0:T(8,128)S(1)} collective-permute-done((f32[256,128]{1,0:T(8,128)S(1)}, f32[256,128]{1,0:T(8,128)S(1)}, u32[]{:S(2)}, u32[]{:S(2)}) %collective-permute-start.9) | collective-permute-done | bytes 131104 | tf_op jit(solution)/shard_map/ppermute | solution.py:415
  24.9 2.8 %shard_map.75.base_ref = bf16[256,3072]{1,0:T(8,128)(2,1)S(1)} custom-call(s32[4]{0:T(128)S(1)} %iota_multiply_fusion.first_ref, f32[256,128]{1,0:T(8,128)S(1)} %get-tuple-element.205.refs_0_, f32[256,128]{1,0:T(8,128)S(1)} %collective-permute-done.9.refs_1_, f32[256,128]{1,0:T(8,128)S(1)} %get-tuple-element.206.refs_2_, bf16[512,3072]{1,0:T(8,128)(2,1)S(1)} %bitcast.152), custom_call_target="tpu_custom_call" | custom-call | flops 805306368 | bytes 4718592 | tf_op jit(solution)/shard_map/pallas_call | solution.py:234
  27.6 0.1 collective-permute-start.18
  27.7 6.8 %collective-permute-done.12.refs_0_ = bf16[88,3072]{1,0:T(8,128)(2,1)S(1)} collective-permute-done((bf16[88,3072]{1,0:T(8,128)(2,1)}, bf16[88,3072]{1,0:T(8,128)(2,1)S(1)}, u32[]{:S(2)}, u32[]{:S(2)}) %collective-permute-start.12) | collective-permute-done | bytes 540704 | tf_op jit(solution)/shard_map/ppermute | solution.py:340
  34.5 0.0 copy-done
  34.5 1.7 %shard_map.76 = (f32[88,128]{1,0:T(8,128)S(1)}, f32[88,128]{1,0:T(8,128)S(1)}) custom-call(s32[4]{0:T(128)S(1)} %iota_multiply_fusion.first_ref, bf16[88,3072]{1,0:T(8,128)(2,1)S(1)} %collective-permute-done.12.refs_0_, bf16[512,3072]{1,0:T(8,128)(2,1)S(1)} %bitcast.147), custom_call_target="tpu_custom_call" | custom-call | flops 276824064 | bytes 3686400 | tf_op jit(solution)/shard_map/pallas_call | solution.py:189
  36.2 12.7 %collective-permute-start.13 = (f32[88,128]{1,0:T(8,128)S(1)}, f32[88,128]{1,0:T(8,128)S(1)}, u32[]{:S(2)}, u32[]{:S(2)}) collective-permute-start(f32[88,128]{1,0:T(8,128)S(1)} %get-tuple-element.211.refs_1_), channel_id=1, source_target_pairs={{0,2},{2,0},{1,3},{3,1},{4,6},{6,4},{5,7},{7,5},{8,10},{10,8},{9,1... | collective-permute-start | bytes 135176 | tf_op jit(solution)/shard_map/ppermute | solution.py:415
  48.9 2.0 %collective-permute-done.13.refs_2_ = f32[88,128]{1,0:T(8,128)S(1)} collective-permute-done((f32[88,128]{1,0:T(8,128)S(1)}, f32[88,128]{1,0:T(8,128)S(1)}, u32[]{:S(2)}, u32[]{:S(2)}) %collective-permute-start.13) | collective-permute-done | bytes 45088 | tf_op jit(solution)/shard_map/ppermute | solution.py:415
  50.9 2.3 %shard_map.77 = bf16[88,3072]{1,0:T(8,128)(2,1)S(1)} custom-call(s32[4]{0:T(128)S(1)} %iota_multiply_fusion.first_ref, s32[128]{0:T(128)S(1)} %bitcast.141, f32[88,128]{1,0:T(8,128)S(1)} %get-tuple-element.211.refs_1_, f32[88,128]{1,0:T(8,128)S(1)} %collective-permute-done.13.refs_2_, f32[88,128]{1,0:T(8,128)S(1)} %get-tuple-element.212.refs_3_, ...), custom_call_target="tpu_custom_call" | custom-call | flops 276824064 | bytes 3686400 | tf_op jit(solution)/shard_map/pallas_call | solution.py:234
  53.2 1.0 collective-permute-done.15.refs_0_
  54.1 1.7 %shard_map.78 = (f32[88,128]{1,0:T(8,128)S(1)}, f32[88,128]{1,0:T(8,128)S(1)}) custom-call(s32[4]{0:T(128)S(1)} %iota_multiply_fusion.first_ref, bf16[88,3072]{1,0:T(8,128)(2,1)S(1)} %collective-permute-done.15.refs_0_, bf16[512,3072]{1,0:T(8,128)(2,1)S(1)} %bitcast.148), custom_call_target="tpu_custom_call" | custom-call | flops 276824064 | bytes 3686400 | tf_op jit(solution)/shard_map/pallas_call | solution.py:189
  55.8 1.4 %collective-permute-start.16 = (f32[88,128]{1,0:T(8,128)S(1)}, f32[88,128]{1,0:T(8,128)S(1)}, u32[]{:S(2)}, u32[]{:S(2)}) collective-permute-start(f32[88,128]{1,0:T(8,128)S(1)} %get-tuple-element.214.refs_1_), channel_id=1, source_target_pairs={{0,2},{2,0},{1,3},{3,1},{4,6},{6,4},{5,7},{7,5},{8,10},{10,8},{9,1... | collective-permute-start | bytes 135176 | tf_op jit(solution)/shard_map/ppermute | solution.py:415
  57.3 0.3 collective-permute-start.14
  57.6 2.3 %collective-permute-done.16.refs_2_ = f32[88,128]{1,0:T(8,128)S(1)} collective-permute-done((f32[88,128]{1,0:T(8,128)S(1)}, f32[88,128]{1,0:T(8,128)S(1)}, u32[]{:S(2)}, u32[]{:S(2)}) %collective-permute-start.16) | collective-permute-done | bytes 45088 | tf_op jit(solution)/shard_map/ppermute | solution.py:415
  59.9 2.3 %shard_map.79 = bf16[88,3072]{1,0:T(8,128)(2,1)S(1)} custom-call(s32[4]{0:T(128)S(1)} %iota_multiply_fusion.first_ref, s32[128]{0:T(128)S(1)} %bitcast.142, f32[88,128]{1,0:T(8,128)S(1)} %get-tuple-element.214.refs_1_, f32[88,128]{1,0:T(8,128)S(1)} %collective-permute-done.16.refs_2_, f32[88,128]{1,0:T(8,128)S(1)} %get-tuple-element.215.refs_3_, ...), custom_call_target="tpu_custom_call" | custom-call | flops 276824064 | bytes 3686400 | tf_op jit(solution)/shard_map/pallas_call | solution.py:234
  62.2 0.2 collective-permute-start.17
  62.4 0.0 collective-permute-done.18.refs_0_
  62.4 1.7 %shard_map.81 = (f32[88,128]{1,0:T(8,128)S(1)}, f32[88,128]{1,0:T(8,128)S(1)}) custom-call(s32[4]{0:T(128)S(1)} %iota_multiply_fusion.first_ref, bf16[88,3072]{1,0:T(8,128)(2,1)S(1)} %collective-permute-done.18.refs_0_, bf16[512,3072]{1,0:T(8,128)(2,1)S(1)} %bitcast.149), custom_call_target="tpu_custom_call" | custom-call | flops 276824064 | bytes 3686400 | tf_op jit(solution)/shard_map/pallas_call | solution.py:189
  64.1 1.3 %collective-permute-start.19 = (f32[88,128]{1,0:T(8,128)S(1)}, f32[88,128]{1,0:T(8,128)S(1)}, u32[]{:S(2)}, u32[]{:S(2)}) collective-permute-start(f32[88,128]{1,0:T(8,128)S(1)} %get-tuple-element.220.refs_0_), channel_id=1, source_target_pairs={{0,2},{2,0},{1,3},{3,1},{4,6},{6,4},{5,7},{7,5},{8,10},{10,8},{9,1... | collective-permute-start | bytes 135176 | tf_op jit(solution)/shard_map/ppermute | solution.py:415
  65.4 0.2 fusion.80
  65.6 0.6 slice.170
  66.8 1.3 %collective-permute-done.19.refs_1_ = f32[88,128]{1,0:T(8,128)S(1)} collective-permute-done((f32[88,128]{1,0:T(8,128)S(1)}, f32[88,128]{1,0:T(8,128)S(1)}, u32[]{:S(2)}, u32[]{:S(2)}) %collective-permute-start.19) | collective-permute-done | bytes 45088 | tf_op jit(solution)/shard_map/ppermute | solution.py:415
  68.2 5.2 %shard_map.82 = bf16[88,3072]{1,0:T(8,128)(2,1)} custom-call(s32[4]{0:T(128)S(1)} %iota_multiply_fusion.first_ref, f32[88,128]{1,0:T(8,128)S(1)} %get-tuple-element.220.refs_0_, f32[88,128]{1,0:T(8,128)S(1)} %collective-permute-done.19.refs_1_, f32[88,128]{1,0:T(8,128)S(1)} %get-tuple-element.221.refs_2_, bf16[512,3072]{1,0:T(8,128)(2,1)} %bitcast.150), custom_call_target="tpu_custom_call" | custom-call | flops 276824064 | bytes 3686400 | tf_op jit(solution)/shard_map/pallas_call | solution.py:234
  73.4 2.0 %collective-permute-start.20 = (bf16[88,3072]{1,0:T(8,128)(2,1)}, bf16[88,3072]{1,0:T(8,128)(2,1)}, u32[]{:S(2)}, u32[]{:S(2)}) collective-permute-start(bf16[88,3072]{1,0:T(8,128)(2,1)} %shard_map.82), channel_id=1, source_target_pairs={{0,12},{4,8},{8,4},{12,0},{1,13},{5,9},{9,5},{13,1},{2,14},{6,10},... | collective-permute-start | bytes 1622024 | tf_op jit(solution)/shard_map/ppermute | solution.py:340
  75.4 9.1 %collective-permute-done.14.refs_2_ = bf16[88,3072]{1,0:T(8,128)(2,1)} collective-permute-done((bf16[88,3072]{1,0:T(8,128)(2,1)S(1)}, bf16[88,3072]{1,0:T(8,128)(2,1)}, u32[]{:S(2)}, u32[]{:S(2)}) %collective-permute-start.14) | collective-permute-done | bytes 540704 | tf_op jit(solution)/shard_map/ppermute | solution.py:340
  84.5 13.0 %collective-permute-done.17.refs_3_ = bf16[88,3072]{1,0:T(8,128)(2,1)} collective-permute-done((bf16[88,3072]{1,0:T(8,128)(2,1)S(1)}, bf16[88,3072]{1,0:T(8,128)(2,1)}, u32[]{:S(2)}, u32[]{:S(2)}) %collective-permute-start.17) | collective-permute-done | bytes 540704 | tf_op jit(solution)/shard_map/ppermute | solution.py:340
  97.5 4.8 %shard_map.80 = (bf16[256,3072]{1,0:T(8,128)(2,1)S(1)}, s32[1]{0:T(128)}) custom-call(bf16[256,3072]{1,0:T(8,128)(2,1)S(1)} %shard_map.75.base_ref, bf16[256,88]{1,0:T(8,128)(2,1)S(1)} %get-tuple-element.327.refs_0_, bf16[256,88]{1,0:T(8,128)(2,1)S(1)} %get-tuple-element.326.refs_1_, bf16[88,3072]{1,0:T(8,128)(2,1)} %collective-permute-done.14.refs_2_, ...), custom_call_target="tpu_custom_call" | custom-call | flops 8304721920 | bytes 94371840 | tf_op jit(solution)/shard_map/pallas_call | solution.py:210
  103.0 0.0 collective-permute-done.20
  103.0 2.8 %fusion.69 = bf16[256,3072]{1,0:T(8,128)(2,1)} fusion(bf16[256,88]{1,0:T(8,128)(2,1)S(1)} %get-tuple-element.217, bf16[88,3072]{1,0:T(8,128)(2,1)} %collective-permute-done.20, bf16[256,3072]{1,0:T(8,128)(2,1)S(1)} %get-tuple-element.222), kind=kOutput, calls=%fused_computation.120 | convolution fusion | flops 140771328 | bytes 3731456 | tf_op jit(solution)/shard_map/dot_general | solution.py:469
  (15 shorter events, 0.1 us)
Async XLA Ops:
  1.6 16.2 %copy-start.4 = (bf16[4,64,3072]{2,1,0:T(8,128)(2,1)S(1)}, bf16[4,64,3072]{2,1,0:T(8,128)(2,1)}, u32[]{:S(2)}) copy-start(bf16[4,64,3072]{2,1,0:T(8,128)(2,1)} %param.9) | copy-start | bytes 4718596
  4.6 29.9 %collective-permute-start.12 = (bf16[88,3072]{1,0:T(8,128)(2,1)}, bf16[88,3072]{1,0:T(8,128)(2,1)S(1)}, u32[]{:S(2)}, u32[]{:S(2)}) collective-permute-start(bf16[88,3072]{1,0:T(8,128)(2,1)} %get-tuple-element.202), channel_id=1, source_target_pairs={{0,8},{4,12},{8,0},{12,4},{1,9},{5,13},{9,1},{13,5},{2,10},{6,14},... | collective-permute-start | bytes 1622024 | tf_op jit(solution)/shard_map/ppermute | solution.py:340
  9.5 4.7 %collective-permute-start.10 = (s32[1,128]{1,0:T(1,128)S(1)}, s32[1,128]{1,0:T(1,128)S(1)}, u32[]{:S(2)}, u32[]{:S(2)}) collective-permute-start(s32[1,128]{1,0:T(1,128)S(1)} %broadcast_in_dim.254), channel_id=1, source_target_pairs={{0,1},{1,0},{2,3},{3,2},{4,5},{5,4},{6,7},{7,6},{8,9},{9,8},{10,11... | collective-permute-start | bytes 1544 | tf_op jit(solution)/shard_map/ppermute | solution.py:408
  13.9 11.0 %copy-start.2 = (bf16[32,16,3072]{2,1,0:T(8,128)(2,1)S(1)}, bf16[32,16,3072]{2,1,0:T(8,128)(2,1)}, u32[]{:S(2)}) copy-start(bf16[32,16,3072]{2,1,0:T(8,128)(2,1)} %param.11) | copy-start | bytes 9437188
  14.1 3.6 %collective-permute-start.11 = (s32[1,128]{1,0:T(1,128)S(1)}, s32[1,128]{1,0:T(1,128)S(1)}, u32[]{:S(2)}, u32[]{:S(2)}) collective-permute-start(s32[1,128]{1,0:T(1,128)S(1)} %broadcast_maximum_fusion), channel_id=1, source_target_pairs={{0,16},{16,0},{1,17},{17,1},{2,18},{18,2},{3,19},{19,3},{4,20},{20... | collective-permute-start | bytes 1544 | tf_op jit(solution)/shard_map/ppermute | solution.py:408
  18.3 35.9 %collective-permute-start.15 = (bf16[88,3072]{1,0:T(8,128)(2,1)S(1)}, bf16[88,3072]{1,0:T(8,128)(2,1)S(1)}, u32[]{:S(2)}, u32[]{:S(2)}) collective-permute-start(bf16[88,3072]{1,0:T(8,128)(2,1)S(1)} %fusion.71), channel_id=1, source_target_pairs={{0,4},{4,0},{8,12},{12,8},{1,5},{5,1},{9,13},{13,9},{2,6},{6,2},{1... | collective-permute-start | bytes 1622024 | tf_op jit(solution)/shard_map/ppermute | solution.py:340
  19.9 5.0 %collective-permute-start.9 = (f32[256,128]{1,0:T(8,128)S(1)}, f32[256,128]{1,0:T(8,128)S(1)}, u32[]{:S(2)}, u32[]{:S(2)}) collective-permute-start(f32[256,128]{1,0:T(8,128)S(1)} %get-tuple-element.205.refs_0_), channel_id=1, source_target_pairs={{0,2},{2,0},{1,3},{3,1},{4,6},{6,4},{5,7},{7,5},{8,10},{10,8},{9,1... | collective-permute-start | bytes 393224 | tf_op jit(solution)/shard_map/ppermute | solution.py:415
  21.4 13.1 %copy-start = (bf16[32,16,3072]{2,1,0:T(8,128)(2,1)S(1)}, bf16[32,16,3072]{2,1,0:T(8,128)(2,1)}, u32[]{:S(2)}) copy-start(bf16[32,16,3072]{2,1,0:T(8,128)(2,1)} %param.10) | copy-start | bytes 9437188
  27.6 34.8 %collective-permute-start.18 = (bf16[88,3072]{1,0:T(8,128)(2,1)S(1)}, bf16[88,3072]{1,0:T(8,128)(2,1)S(1)}, u32[]{:S(2)}, u32[]{:S(2)}) collective-permute-start(bf16[88,3072]{1,0:T(8,128)(2,1)S(1)} %fusion.70), channel_id=1, source_target_pairs={{0,12},{4,8},{8,4},{12,0},{1,13},{5,9},{9,5},{13,1},{2,14},{6,10},... | collective-permute-start | bytes 1622024 | tf_op jit(solution)/shard_map/ppermute | solution.py:340
  36.2 14.7 %collective-permute-start.13 = (f32[88,128]{1,0:T(8,128)S(1)}, f32[88,128]{1,0:T(8,128)S(1)}, u32[]{:S(2)}, u32[]{:S(2)}) collective-permute-start(f32[88,128]{1,0:T(8,128)S(1)} %get-tuple-element.211.refs_1_), channel_id=1, source_target_pairs={{0,2},{2,0},{1,3},{3,1},{4,6},{6,4},{5,7},{7,5},{8,10},{10,8},{9,1... | collective-permute-start | bytes 135176 | tf_op jit(solution)/shard_map/ppermute | solution.py:415
  55.8 4.1 %collective-permute-start.16 = (f32[88,128]{1,0:T(8,128)S(1)}, f32[88,128]{1,0:T(8,128)S(1)}, u32[]{:S(2)}, u32[]{:S(2)}) collective-permute-start(f32[88,128]{1,0:T(8,128)S(1)} %get-tuple-element.214.refs_1_), channel_id=1, source_target_pairs={{0,2},{2,0},{1,3},{3,1},{4,6},{6,4},{5,7},{7,5},{8,10},{10,8},{9,1... | collective-permute-start | bytes 135176 | tf_op jit(solution)/shard_map/ppermute | solution.py:415
  57.3 27.2 %collective-permute-start.14 = (bf16[88,3072]{1,0:T(8,128)(2,1)S(1)}, bf16[88,3072]{1,0:T(8,128)(2,1)}, u32[]{:S(2)}, u32[]{:S(2)}) collective-permute-start(bf16[88,3072]{1,0:T(8,128)(2,1)S(1)} %shard_map.77), channel_id=1, source_target_pairs={{0,8},{4,12},{8,0},{12,4},{1,9},{5,13},{9,1},{13,5},{2,10},{6,14},... | collective-permute-start | bytes 1622024 | tf_op jit(solution)/shard_map/ppermute | solution.py:340
  62.2 35.3 %collective-permute-start.17 = (bf16[88,3072]{1,0:T(8,128)(2,1)S(1)}, bf16[88,3072]{1,0:T(8,128)(2,1)}, u32[]{:S(2)}, u32[]{:S(2)}) collective-permute-start(bf16[88,3072]{1,0:T(8,128)(2,1)S(1)} %shard_map.79), channel_id=1, source_target_pairs={{0,4},{4,0},{8,12},{12,8},{1,5},{5,1},{9,13},{13,9},{2,6},{6,2},{1... | collective-permute-start | bytes 1622024 | tf_op jit(solution)/shard_map/ppermute | solution.py:340
  64.1 4.1 %collective-permute-start.19 = (f32[88,128]{1,0:T(8,128)S(1)}, f32[88,128]{1,0:T(8,128)S(1)}, u32[]{:S(2)}, u32[]{:S(2)}) collective-permute-start(f32[88,128]{1,0:T(8,128)S(1)} %get-tuple-element.220.refs_0_), channel_id=1, source_target_pairs={{0,2},{2,0},{1,3},{3,1},{4,6},{6,4},{5,7},{7,5},{8,10},{10,8},{9,1... | collective-permute-start | bytes 135176 | tf_op jit(solution)/shard_map/ppermute | solution.py:415
  73.4 29.6 %collective-permute-start.20 = (bf16[88,3072]{1,0:T(8,128)(2,1)}, bf16[88,3072]{1,0:T(8,128)(2,1)}, u32[]{:S(2)}, u32[]{:S(2)}) collective-permute-start(bf16[88,3072]{1,0:T(8,128)(2,1)} %shard_map.82), channel_id=1, source_target_pairs={{0,12},{4,8},{8,4},{12,0},{1,13},{5,9},{9,5},{13,1},{2,14},{6,10},... | collective-permute-start | bytes 1622024 | tf_op jit(solution)/shard_map/ppermute | solution.py:340

commit v6 on v4

--- a/solution.py
+++ b/solution.py
@@ -100,6 +100,157 @@
         offset += count
 
 
+def column_of(line, where):
+    return jnp.sum(jnp.where(where, line, 0), axis=1, keepdims=True)
+
+
+def as_line(column):
+    shape = (column.shape[0], LANES)
+    turn = lax.broadcasted_iota(jnp.int32, shape, 0) == lax.broadcasted_iota(jnp.int32, shape, 1)
+    return jnp.sum(jnp.where(turn, column, 0), axis=0, keepdims=True)
+
+
+def counted(marked):
+    lanes = marked.shape[1]
+    earlier = lax.broadcasted_iota(jnp.int32, (lanes, lanes), 0) < lax.broadcasted_iota(
+        jnp.int32, (lanes, lanes), 1
+    )
+    return jnp.dot(
+        marked.astype(jnp.bfloat16),
+        earlier.astype(jnp.bfloat16),
+        preferred_element_type=jnp.float32,
+    ).astype(jnp.int32)
+
+
+def put_block(ref, rows, last):
+    count = rows.shape[0]
+    ref[...] = rows.astype(ref.dtype)
+    row = lax.broadcasted_iota(jnp.int32, (count, LANES), 0)
+    head = jnp.where(row == count - 1, last.astype(jnp.float32), rows[:, :LANES])
+    ref[:, :LANES] = head.astype(ref.dtype)
+
+
+def slots_of(block, rows):
+    return lax.broadcasted_iota(jnp.int32, (block, rows), 0)
+
+
+def route_kernel(member, local_adapters, me_ref, source_ref, wanted_ref, x_ref, packed_ref, route_ref):
+    table = source_ref.shape[1]
+    rows = x_ref.shape[0]
+    block = packed_ref.shape[0]
+    diagonal = lax.broadcasted_iota(jnp.int32, (table, table), 0) == lax.broadcasted_iota(
+        jnp.int32, (table, table), 1
+    )
+    source = column_of(source_ref[...], diagonal)
+    entry = lax.broadcasted_iota(jnp.int32, (table, rows), 0)
+    served = jnp.sum(jnp.where(entry == wanted_ref[...], source, 0), axis=0, keepdims=True)
+    owner = lax.div(served, jnp.int32(local_adapters))
+    name = served - owner * local_adapters + 1
+    key = owner ^ me_ref[0]
+    line = lax.broadcasted_iota(jnp.int32, (8, rows), 0)
+    rank = jnp.sum(jnp.where(line == key, counted(line == key), 0), axis=0, keepdims=True)
+    route_ref[...] = jnp.where(line == 0, key, jnp.where(line == 1, rank, name))
+    slot = slots_of(block, rows)
+    chosen = (key == member) & (slot == rank) & (slot < block - 1)
+    packed = jnp.dot(chosen.astype(jnp.bfloat16), x_ref[...], preferred_element_type=jnp.float32)
+    put_block(packed_ref, packed, as_line(column_of(name, chosen)))
+
+
+def spill_kernel(far, room, shared, route_ref, x_ref, spill_ref, index_ref):
+    rows = x_ref.shape[0]
+    block = spill_ref.shape[0]
+    key, rank, name = route_ref[0:1, :], route_ref[1:2, :], route_ref[2:3, :]
+    spilled = (key >= far) & (rank >= room + shared)
+    line = lax.broadcasted_iota(jnp.int32, (8, rows), 0)
+    index = counted((line >= 0) & spilled)
+    index = jnp.where(spilled, index[0:1, :], -1)
+    index_ref[...] = jnp.where(line >= 0, index, 0)
+    slot = slots_of(block, rows)
+    chosen = (slot == index) & (slot < block - 1)
+    code = name + jnp.where(key > far, LANES // 2, 0)
+    last = as_line(column_of(code, chosen))
+    lane = lax.broadcasted_iota(jnp.int32, (1, LANES), 1)
+    for number in range(2):
+        free = shared - own_share(key, rank, far + number, room, shared)
+        last = jnp.where(lane == LANES // 2 + number, free, last)
+    packed = jnp.dot(chosen.astype(jnp.bfloat16), x_ref[...], preferred_element_type=jnp.float32)
+    put_block(spill_ref, packed, last)
+
+
+def own_share(key, rank, member, room, shared):
+    held = jnp.max(jnp.where(key == member, rank + 1, 0), axis=1, keepdims=True)
+    return jnp.clip(held - room, 0, shared)
+
+
+def settle_kernel(
+    far, room, shared, near_room, more, route_ref, index_ref, x_ref, guest_ref,
+    first_ref, second_ref, placed_ref, left_ref, rounds_ref,
+):
+    rows = x_ref.shape[0]
+    block = first_ref.shape[0]
+    key, rank, name = route_ref[0:1, :], route_ref[1:2, :], route_ref[2:3, :]
+    index = index_ref[0:1, :]
+    told = guest_ref[...][block - 1 :, :LANES].astype(jnp.float32).astype(jnp.int32)
+    lane = lax.broadcasted_iota(jnp.int32, (1, LANES), 1)
+    code = jnp.where(lane < block - 1, told, 0)
+    second = code > LANES // 2
+    guest_name = code - jnp.where(second, LANES // 2, 0)
+    line = lax.broadcasted_iota(jnp.int32, (8, LANES), 0)
+    mine = (code > 0) & ((line > 0) == second)
+    order = jnp.sum(jnp.where(mine & (line < 2), counted(mine), 0), axis=0, keepdims=True)
+    start = jnp.where(key == 0, rows, near_room)
+    kept = jnp.full_like(key, -1)
+    for number, packed_ref in enumerate((first_ref, second_ref)):
+        member = far + number
+        share = own_share(key, rank, member, room, shared)
+        slot = slots_of(block, rows)
+        own = (key == member) & (slot + room == rank) & (slot < block - 1)
+        slot = slots_of(block, LANES)
+        guest = (code > 0) & (second == (number == 1)) & (slot == order + share) & (slot < block - 1)
+        placed_ref[number, :, :] = guest.astype(jnp.float32)
+        packed = jnp.dot(own.astype(jnp.bfloat16), x_ref[...], preferred_element_type=jnp.float32)
+        packed = packed + jnp.dot(
+            guest.astype(jnp.bfloat16)[:, :block], guest_ref[...], preferred_element_type=jnp.float32
+        )
+        names = column_of(name, own) + column_of(guest_name, guest)
+        put_block(packed_ref, packed, as_line(names))
+        free = jnp.sum(jnp.where(lane == LANES // 2 + number, told, 0), axis=1, keepdims=True)
+        over = rank - (room + shared)
+        taken = (key == member) & (over >= 0) & (over < free) & (index < block - 1)
+        kept = jnp.where(taken, index, kept)
+        reached = room + shared + jnp.max(jnp.where(taken, over + 1, 0), axis=1, keepdims=True)
+        start = jnp.where(key == member, reached, start)
+    left = rank - start
+    line = lax.broadcasted_iota(jnp.int32, (8, rows), 0)
+    left_ref[...] = jnp.where(line == 0, left, kept)
+    rounds_ref[0] = lax.div(jnp.max(jnp.maximum(left + 1, 0)) + (more - 1), jnp.int32(more))
+
+
+def hand_kernel(placed_ref, first_ref, second_ref, out_ref):
+    total = None
+    for number, ref in enumerate((first_ref, second_ref)):
+        part = lax.dot_general(
+            placed_ref[number, :, :].astype(jnp.bfloat16),
+            ref[...],
+            (((0,), (0,)), ((), ())),
+            preferred_element_type=jnp.float32,
+        )
+        total = part if total is None else total + part
+    out_ref[...] = total[: out_ref.shape[0], :].astype(out_ref.dtype)
+
+
+def small_call(kernel, outs, scalars, *args):
+    whole = pl.BlockSpec(memory_space=pltpu.VMEM)
+    scalar = pl.BlockSpec(memory_space=pltpu.SMEM)
+    return pl.pallas_call(
+        kernel,
+        out_shape=[jax.ShapeDtypeStruct(shape, dtype) for shape, dtype in outs],
+        in_specs=[scalar] * scalars + [whole] * (len(args) - scalars),
+        out_specs=[scalar if shape == (1,) else whole for shape, _ in outs],
+        compiler_params=pltpu.CompilerParams(vmem_limit_bytes=VMEM_BYTES),
+    )(*args)
+
+
 def back_kernel(blocks, base_ref, *refs):
     places, returned, outs = refs[:blocks], refs[blocks : 2 * blocks], refs[2 * blocks :]
     out_ref = outs[0]
@@ -223,22 +374,48 @@
         axis=1,
     )
     wanted = (target_host[:, :, 0] * local_adapters + target_position).reshape(rows)
-    served = jnp.sum(jnp.where(wanted[:, None] == table[None, :], source[None, :], 0), axis=1)
-    owner = served // local_adapters
-    named_row = served % local_adapters + 1
-    stays = owner == me
-    key = owner ^ me if paired else jnp.where(stays, host_count, owner)
-
-    hosts = jnp.arange(host_count, dtype=jnp.int32)
-    in_block = key[:, None] == hosts[None, :]
-    row_ids = jnp.arange(rows, dtype=jnp.int32)
-    earlier = (row_ids[None, :] < row_ids[:, None]).astype(jnp.bfloat16)
-    before = jnp.dot(
-        earlier, in_block.astype(jnp.bfloat16), preferred_element_type=jnp.float32
-    ).astype(jnp.int32)
-    row_rank = jnp.sum(jnp.where(in_block, before, 0), axis=1)
-    left = jnp.max(jnp.where(stays, 0, row_rank + 1)) - (first_block - 1)
-    own_rounds = jnp.maximum(0, (left + more_block - 2) // (more_block - 1))
+
+    def route():
+        served = jnp.sum(jnp.where(wanted[:, None] == table[None, :], source[None, :], 0), axis=1)
+        owner = served // local_adapters
+        key = owner ^ me if paired else jnp.where(owner == me, host_count, owner)
+        in_block = key[:, None] == jnp.arange(host_count, dtype=jnp.int32)[None, :]
+        row_ids = jnp.arange(rows, dtype=jnp.int32)
+        earlier = (row_ids[None, :] < row_ids[:, None]).astype(jnp.bfloat16)
+        before = jnp.dot(
+            earlier, in_block.astype(jnp.bfloat16), preferred_element_type=jnp.float32
+        ).astype(jnp.int32)
+        row_rank = jnp.sum(jnp.where(in_block, before, 0), axis=1)
+        most = jnp.max(jnp.where(owner == me, 0, row_rank + 1))
+        return key, row_rank, served % local_adapters + 1, owner == me, most
+
+    tiled = (
+        host_count == 4
+        and lax.axis_size("rep") == 2
+        and spots % LANES == 0
+        and LANES % rank_extent == 0
+        and 2 * local_adapters < LANES
+    )
+    main_block = round_up(rows // host_count, 16)
+    shared_block = 16
+    if tiled:
+        wide = ((main_block, width), jnp.bfloat16)
+        first_packed, lines = small_call(
+            functools.partial(route_kernel, 2, local_adapters),
+            [wide, ((8, rows), jnp.int32)],
+            1,
+            me.reshape(1),
+            source.reshape(1, -1),
+            wanted.reshape(1, -1),
+            flat_x,
+        )
+        key, row_rank, named_row = lines[0], lines[1], lines[2]
+        stays = key == 0
+        own_rounds = 0
+    else:
+        key, row_rank, named_row, stays, most = route()
+        left = most - (first_block - 1)
+        own_rounds = jnp.maximum(0, (left + more_block - 2) // (more_block - 1))
 
     columns = jnp.arange(width, dtype=jnp.int32)
     spot_adapter = jnp.arange(spots, dtype=jnp.int32) // rank_extent + 1
@@ -302,7 +479,7 @@
         names = jnp.where(jnp.arange(block)[None, :] < block - 1, names[:, :block], 0)
         return adapt(received, names.reshape(-1)).astype(jnp.bfloat16), rounds
 
-    def back(member, start, block, returned):
+    def back(member, start, block, row_rank, returned):
         return lax.dot_general(
             place(member, start, block, key, row_rank),
             returned,
@@ -310,13 +487,13 @@
             preferred_element_type=jnp.float32,
         )
 
-    def one_round(start, block, base):
+    def one_round(start, block, base, row_rank):
         if not paired:
             packed = jnp.concatenate([pack(member, start, block, key, row_rank, own_rounds) for member in range(host_count)])
             adapted, rounds = serve(exchange(packed), block)
             returned = exchange(adapted).reshape(host_count, block, width)
             for member in range(host_count):
-                base = base + back(member, start, block, returned[member])
+                base = base + back(member, start, block, row_rank, returned[member])
             return base.astype(jnp.bfloat16), jnp.maximum(rounds, own_rounds)
         received = {s: swap(pack(s, start, block, key, row_rank, own_rounds), s) for s in range(1, host_count)}
         rounds = own_rounds
@@ -324,7 +501,7 @@
             adapted, theirs = serve(received[s], block)
             rounds = jnp.maximum(rounds, theirs)
             returned = swap(adapted, s)
-            base = (base + back(s, start, block, returned)).astype(jnp.bfloat16)
+            base = (base + back(s, start, block, row_rank, returned)).astype(jnp.bfloat16)
         return base, rounds
 
     def agree(rounds):
@@ -364,52 +541,95 @@
                 told,
             )
 
-        near = list(range(1, host_count // 2))
-        far = list(range(host_count // 2, host_count))
-        order = near + far
-        order = far[:1] + near + far[1:]
-        first, last = far[0], far[-1]
-        packed = pack(first, 0, block, key, row_rank, 0)
-        received = {first: swap(packed, first)}
+        near, first, last = 1, 2, 3
+        room, shared = main_block - 1, shared_block - 1
+        share = ((shared_block, width), jnp.bfloat16)
+        came = {"F": [swap(first_packed, first)]}
+        spill, index = small_call(
+            functools.partial(spill_kernel, first, room, shared),
+            [share, ((8, rows), jnp.int32)],
+            0,
+            lines,
+            flat_x,
+        )
+        cores = [(0, 1), (1, 0)]
+        guests = lax.ppermute(spill, "rep", cores)
         own_names = jnp.where(stays, named_row, 0).astype(jnp.float32)[:, None]
-        own_names, rounds, _ = lax.optimization_barrier((own_names, own_rounds, packed))
-        rounds = agree(rounds)[0]
+        own_names, _ = lax.optimization_barrier((own_names, spill))
         partial, names = shrink([flat_x], own_names)
-        partial, key, row_rank = lax.optimization_barrier((partial, key, row_rank))
-        for s in near + far[1:-1]:
-            received[s] = swap(pack(s, 0, block, key, row_rank, 0), s)
-        packed = pack(last, 0, block, key, row_rank, rounds[0])
+        partial, key, row_rank, guests = lax.optimization_barrier((partial, key, row_rank, guests))
+        came["L"] = [swap(pack(last, 0, main_block, key, row_rank, 0), last)]
+        came["N"] = [swap(pack(near, 0, block, key, row_rank, 0), near)]
+        shared_first, shared_last, placed, remaining, rounds = small_call(
+            functools.partial(settle_kernel, first, room, shared, block - 1, more_block - 1),
+            [
+                share,
+                share,
+                ((2, shared_block, LANES), jnp.float32),
+                ((8, rows), jnp.int32),
+                ((1,), jnp.int32),
+            ],
+            0,
+            lines,
+            index,
+            flat_x,
+            guests,
+        )
+        came["b"] = [swap(shared_first, first), swap(shared_last, last)]
         (base,) = expand([flat_x], partial, names)
-        base, packed = lax.optimization_barrier((base, packed))
-        received[last] = swap(packed, last)
-        returned = {}
-        for number, s in enumerate(order):
-            told = None if s == last else rounds
-            (adapted,) = expand([received[s]], *shrink([received[s]], None), told)
-            if s != last:
-                later = order[number + 1]
-                _, received[later] = lax.optimization_barrier((adapted, received[later]))
-            returned[s] = swap(adapted, s)
-        places = {s: place(s, 0, block, key, row_rank).T for s in order}
-        early = order[:-1]
+        rounds = agree(rounds[0])[0]
+        across = {"F": [first], "N": [near], "b": [first, last], "L": [last]}
+        gone = {}
+        order = ['F', 'b', 'N', 'L']
+        for number, together in enumerate(order):
+            blocks = sum((came[part] for part in together), [])
+            partial, names = shrink(blocks, None)
+            adapted = expand(blocks, partial, names, None if together == "L" else rounds)
+            if number + 1 < len(order):
+                for part in order[number + 1]:
+                    _, came[part] = lax.optimization_barrier((tuple(adapted), came[part]))
+            if together == "L":
+                adapted, gone["F"] = lax.optimization_barrier((adapted, gone["F"]))
+                adapted, gone["b"] = lax.optimization_barrier((adapted, gone["b"]))
+            steps_across = sum((across[part] for part in together), [])
+            sent = [swap(values, s) for values, s in zip(adapted, steps_across)]
+            for part in together:
+                gone[part], sent = sent[: len(across[part])], sent[len(across[part]) :]
+        shared_first, shared_last = gone["b"]
+        (hosted,) = small_call(hand_kernel, [share], 0, placed, shared_first, shared_last)
+        handed = lax.ppermute(hosted, "rep", cores)
+        slot = jnp.arange(shared_block, dtype=jnp.int32)[None, :]
+        home = (remaining[1][:, None] == slot).astype(jnp.bfloat16)
         base, told = back_call(
-            base, [places[s] for s in early], [returned[s] for s in early], True, 30
-        )
-        result = jnp.dot(places[last], returned[last], preferred_element_type=jnp.float32)
+            base,
+            [
+                place(first, 0, main_block, key, row_rank).T,
+                place(near, 0, block, key, row_rank).T,
+                place(first, room, shared_block, key, row_rank).T,
+                place(last, room, shared_block, key, row_rank).T,
+                home,
+            ],
+            gone["F"] + gone["N"] + [shared_first, shared_last, handed],
+            True,
+            5,
+        )
+        place_last = place(last, 0, main_block, key, row_rank).T
+        base, place_last = lax.optimization_barrier((base, place_last))
+        result = jnp.dot(place_last, gone["L"][0], preferred_element_type=jnp.float32)
         result = (result + base).astype(jnp.bfloat16)
-        told = jnp.maximum(told[0], received[last][block - 1, block - 1].astype(jnp.int32))
-        return result, jnp.maximum(told, rounds[0])
-
-    if paired and spots % LANES == 0 and LANES % rank_extent == 0:
-        result, rounds = paired_round(key, row_rank)
+        return result, jnp.maximum(told[0], rounds[0]), remaining[0]
+
+    if tiled:
+        result, rounds, left_rank = paired_round(key, row_rank)
     else:
         own = adapt(flat_x, jnp.where(stays, named_row, 0)).astype(jnp.bfloat16)
-        result, rounds = one_round(0, first_block, own)
+        result, rounds = one_round(0, first_block, own, row_rank)
         rounds = agree(rounds)[0, 0]
+        left_rank = row_rank - (first_block - 1)
     def more(state):
         number, so_far = state
-        start = first_block - 1 + number * (more_block - 1)
-        so_far, _ = one_round(start, more_block, so_far)
+        start = number * (more_block - 1)
+        so_far, _ = one_round(start, more_block, so_far, left_rank)
         return number + 1, so_far
 
     _, result = lax.while_loop(

time: 107 us -> 102 us (0.953)
  Pallas kernels: 26.1 us -> 32.2 us
  starting transfers between devices: 27.7 us -> 22.9 us
  matrix products: 6.6 us -> 2.56 us
  waiting for transfers between devices: 39.7 us -> 37.9 us
  between operations: 2.21 us -> 0.99 us
    ppermute x4 -> x5, starting transfers between devices: 16.5 us -> 5.05 us  [over_shares(): lax.ppermute(partial, 'mp', [(i, (i + hop) % shares) for i in range(share...]
    ppermute x6 -> x10, starting transfers between devices: 9.53 us -> 15.4 us  [swap(): lax.ppermute(values, 'hst', [(i, i ^ step) for i in range(host_count)])]
    pallas_call x0 -> x4, Pallas kernels: none -> 5.56 us  [small_call(): pl.pallas_call(kernel, out_shape=[jax.ShapeDtypeStruct(shape, dtype) for...]
    dot_general x3 -> x2, matrix products: 3.52 us -> 0.86 us  [pack(): jnp.dot(place(member, start, block, key, row_rank), flat_x, preferred_ele...]
    pallas_call x4 -> x5, Pallas kernels: 8.69 us -> 11.1 us  [shrink_call(): pl.pallas_call(functools.partial(shrink_kernel, counts, own_names is not...]
    ppermute x6 -> x10, waiting for transfers between devices: 33.2 us -> 31.3 us  [swap(): lax.ppermute(values, 'hst', [(i, i ^ step) for i in range(host_count)])]
    max x2, other arithmetic: 0.01 us -> 1.52 us  [agree(): jnp.maximum(most, lax.ppermute(rounds, axis, [(i, (i + hop) % size) for i...]
    dot_general x2 -> x1, matrix products: 3.08 us -> 1.7 us  [paired_round(): jnp.dot(place_last, gone['L'][0], preferred_element_type=jnp.float32)]
  transfers between devices with their start and end apart: 12 -> 19, of which waited for: 7 -> 8; matrix products, arithmetic and copies ran while one was open for 3% -> 4% of each run, Pallas kernels for 24% -> 28%
where the time goes in v6:
time: 102 us; the launch traced here: 101 us
  waiting for transfers between devices  37.9 us (37%)
  Pallas kernels  32.2 us (32%)
  starting transfers between devices  22.9 us (22%)
  other arithmetic  4.03 us (4%)
  matrix products  2.56 us (3%)
    ppermute x10, waiting for transfers between devices, swap(): lax.ppermute(values, 'hst', [(i, i ^ step) for i in range(host_count)])  31.3 us
    ppermute x10, starting transfers between devices, swap(): lax.ppermute(values, 'hst', [(i, i ^ step) for i in range(host_count)])  15.4 us
    pallas_call x5, Pallas kernels, expand_call(): pl.pallas_call(functools.partial(expand_kernel, counts, len(partials), le...  11.5 us
    pallas_call x5, Pallas kernels, shrink_call(): pl.pallas_call(functools.partial(shrink_kernel, counts, own_names is not...  11.1 us
    ppermute x5, waiting for transfers between devices, over_shares(): lax.ppermute(partial, 'mp', [(i, (i + hop) % shares) for i in range(share...  6.59 us
    pallas_call x4, Pallas kernels, small_call(): pl.pallas_call(kernel, out_shape=[jax.ShapeDtypeStruct(shape, dtype) for...  5.56 us
    ppermute x5, starting transfers between devices, over_shares(): lax.ppermute(partial, 'mp', [(i, (i + hop) % shares) for i in range(share...  5.05 us
    pallas_call x1, Pallas kernels, back_call(): pl.pallas_call(functools.partial(back_kernel, len(returned)), grid=(width...  4.03 us
  transfers between devices with their start and end apart: 19, of which 8 were waited for; matrix products, arithmetic and copies ran while one was open for 4% of the time, Pallas kernels for 28%

profile of v6, /device:TPU:0, one launch (start us, length us, event | category | flops | bytes accessed | tf_op | source)
XLA Modules:
  0.0 101.4 jit_solution(15619008040060669896)
XLA Ops:
  0.0 0.8 bitcast_add_fusion
  0.9 0.8 select_reduce_fusion.5
  1.8 2.1 %shard_map.73 = (bf16[64,3072]{1,0:T(8,128)(2,1)S(1)}, s32[8,256]{1,0:T(8,128)S(1)}) custom-call(s32[1]{0:T(128)} %bitcast.1.me_ref, s32[1,128]{1,0:T(1,128)S(1)} %bitcast.142, s32[1,256]{1,0:T(1,128)S(1)} %reshape_reshape.3.wanted_ref, bf16[256,3072]{1,0:T(8,128)(2,1)} %bitcast.155), custom_call_target="tpu_custom_call" | custom-call | tf_op jit(solution)/shard_map/pallas_call | solution.py:245
  3.8 1.9 %shard_map.74 = (bf16[16,3072]{1,0:T(8,128)(2,1)S(1)}, s32[8,256]{1,0:T(8,128)S(1)}) custom-call(s32[8,256]{1,0:T(8,128)S(1)} %get-tuple-element.200.route_ref, bf16[256,3072]{1,0:T(8,128)(2,1)} %bitcast.156), custom_call_target="tpu_custom_call" | custom-call | tf_op jit(solution)/shard_map/pallas_call | solution.py:245
  5.7 0.5 collective-permute-start.9
  6.1 3.7 %collective-permute-start.13 = (bf16[64,3072]{1,0:T(8,128)(2,1)S(1)}, bf16[64,3072]{1,0:T(8,128)(2,1)S(1)}, u32[]{:S(2)}, u32[]{:S(2)}) collective-permute-start(bf16[64,3072]{1,0:T(8,128)(2,1)S(1)} %get-tuple-element.212), channel_id=1, source_target_pairs={{0,8},{4,12},{8,0},{12,4},{1,9},{5,13},{9,1},{13,5},{2,10},{6,14},... | collective-permute-start | bytes 1179656 | tf_op jit(solution)/shard_map/ppermute | solution.py:447
  10.0 3.7 %shard_map.75 = (f32[256,128]{1,0:T(8,128)S(1)}, f32[256,128]{1,0:T(8,128)S(1)}) custom-call(s32[4]{0:T(128)S(1)} %iota_multiply_fusion.first_ref, bf16[256,3072]{1,0:T(8,128)(2,1)S(1)} %bitcast.158, f32[256,1]{1,0:T(8,128)S(1)} %copy.14.refs_1_, bf16[512,3072]{1,0:T(8,128)(2,1)} %bitcast.143), custom_call_target="tpu_custom_call" | custom-call | flops 805306368 | bytes 4718592 | tf_op jit(solution)/shard_map/pallas_call | solution.py:280
  13.8 0.2 select_reduce_fusion.3
  14.0 1.1 %shard_map.77 = (bf16[16,3072]{1,0:T(8,128)(2,1)S(1)}, bf16[16,3072]{1,0:T(8,128)(2,1)S(1)}, f32[2,16,128]{2,1,0:T(8,128)S(1)}, s32[8,256]{1,0:T(8,128)S(1)}, s32[1]{0:T(128)}) custom-call(s32[8,256]{1,0:T(8,128)S(1)} %get-tuple-element.200.route_ref, s32[8,256]{1,0:T(8,128)S(1)} %get-tuple-element.208.index_ref, bf16[256,3072]{1,0:T(8,128)(2,1)S(1)} %bitcast.159, ...), custom_call_target="tpu_custom_call" | custom-call | tf_op jit(solution)/shard_map/pallas_call | solution.py:245
  15.1 0.6 broadcast_in_dim.254
  15.8 0.2 collective-permute-start.11
  16.0 0.3 collective-permute-start.15
  16.3 3.7 %collective-permute-start.16 = (bf16[16,3072]{1,0:T(8,128)(2,1)S(1)}, bf16[16,3072]{1,0:T(8,128)(2,1)S(1)}, u32[]{:S(2)}, u32[]{:S(2)}) collective-permute-start(bf16[16,3072]{1,0:T(8,128)(2,1)S(1)} %get-tuple-element.216), channel_id=1, source_target_pairs={{0,12},{4,8},{8,4},{12,0},{1,13},{5,9},{9,5},{13,1},{2,14},{6,10},... | collective-permute-start | bytes 294920 | tf_op jit(solution)/shard_map/ppermute | solution.py:447
  20.0 0.4 fusion.71
  20.4 0.4 fusion.70
  20.8 0.2 fusion.85
  21.1 0.9 broadcast_maximum_fusion
  22.0 1.6 %collective-permute-start.12 = (s32[1,128]{1,0:T(1,128)S(1)}, s32[1,128]{1,0:T(1,128)S(1)}, u32[]{:S(2)}, u32[]{:S(2)}) collective-permute-start(s32[1,128]{1,0:T(1,128)S(1)} %broadcast_maximum_fusion), channel_id=1, source_target_pairs={{0,16},{16,0},{1,17},{17,1},{2,18},{18,2},{3,19},{19,3},{4,20},{20... | collective-permute-start | bytes 1544 | tf_op jit(solution)/shard_map/ppermute | solution.py:515
  23.6 8.9 %collective-permute-done.13.refs_0_ = bf16[64,3072]{1,0:T(8,128)(2,1)S(1)} collective-permute-done((bf16[64,3072]{1,0:T(8,128)(2,1)S(1)}, bf16[64,3072]{1,0:T(8,128)(2,1)S(1)}, u32[]{:S(2)}, u32[]{:S(2)}) %collective-permute-start.13) | collective-permute-done | bytes 393248 | tf_op jit(solution)/shard_map/ppermute | solution.py:447
  32.5 1.7 %shard_map.78 = (f32[64,128]{1,0:T(8,128)S(1)}, f32[64,128]{1,0:T(8,128)S(1)}) custom-call(s32[4]{0:T(128)S(1)} %iota_multiply_fusion.first_ref, bf16[64,3072]{1,0:T(8,128)(2,1)S(1)} %collective-permute-done.13.refs_0_, bf16[512,3072]{1,0:T(8,128)(2,1)S(1)} %bitcast.145), custom_call_target="tpu_custom_call" | custom-call | flops 201326592 | bytes 3538944 | tf_op jit(solution)/shard_map/pallas_call | solution.py:280
  34.3 1.8 %collective-permute-start.14 = (f32[64,128]{1,0:T(8,128)S(1)}, f32[64,128]{1,0:T(8,128)S(1)}, u32[]{:S(2)}, u32[]{:S(2)}) collective-permute-start(f32[64,128]{1,0:T(8,128)S(1)} %get-tuple-element.213.refs_1_), channel_id=1, source_target_pairs={{0,2},{2,0},{1,3},{3,1},{4,6},{6,4},{5,7},{7,5},{8,10},{10,8},{9,1... | collective-permute-start | bytes 98312 | tf_op jit(solution)/shard_map/ppermute | solution.py:522
  36.1 0.6 fusion.123
  36.7 3.2 %collective-permute-start.20 = (bf16[64,3072]{1,0:T(8,128)(2,1)S(1)}, bf16[64,3072]{1,0:T(8,128)(2,1)S(1)}, u32[]{:S(2)}, u32[]{:S(2)}) collective-permute-start(bf16[64,3072]{1,0:T(8,128)(2,1)S(1)} %fusion.71), channel_id=1, source_target_pairs={{0,12},{4,8},{8,4},{12,0},{1,13},{5,9},{9,5},{13,1},{2,14},{6,10},... | collective-permute-start | bytes 1179656 | tf_op jit(solution)/shard_map/ppermute | solution.py:447
  39.9 2.2 %shard_map.79 = bf16[64,3072]{1,0:T(8,128)(2,1)S(1)} custom-call(s32[4]{0:T(128)S(1)} %iota_multiply_fusion.first_ref, s32[128]{0:T(128)S(1)} %bitcast.138, f32[64,128]{1,0:T(8,128)S(1)} %get-tuple-element.213.refs_1_, f32[64,128]{1,0:T(8,128)S(1)} %collective-permute-done.14.refs_2_, f32[64,128]{1,0:T(8,128)S(1)} %get-tuple-element.214.refs_3_, ...), custom_call_target="tpu_custom_call" | custom-call | flops 201326592 | bytes 3538944 | tf_op jit(solution)/shard_map/pallas_call | solution.py:325
  42.1 2.3 %shard_map.80 = (f32[32,128]{1,0:T(8,128)S(1)}, f32[32,128]{1,0:T(8,128)S(1)}) custom-call(s32[4]{0:T(128)S(1)} %iota_multiply_fusion.first_ref, bf16[16,3072]{1,0:T(8,128)(2,1)S(1)} %collective-permute-done.15.refs_0_, bf16[16,3072]{1,0:T(8,128)(2,1)S(1)} %collective-permute-done.16.refs_1_, bf16[512,3072]{1,0:T(8,128)(2,1)S(1)} %bitcast.146), custom_call_target="tpu_custom_call" | custom-call | flops 100663296 | bytes 3342336 | tf_op jit(solution)/shard_map/pallas_call | solution.py:280
  44.4 0.5 collective-permute-start.17
  45.2 3.0 %collective-permute-done.17.refs_2_ = f32[32,128]{1,0:T(8,128)S(1)} collective-permute-done((f32[32,128]{1,0:T(8,128)S(1)}, f32[32,128]{1,0:T(8,128)S(1)}, u32[]{:S(2)}, u32[]{:S(2)}) %collective-permute-start.17) | collective-permute-done | bytes 16416 | tf_op jit(solution)/shard_map/ppermute | solution.py:522
  48.1 2.1 %shard_map.81 = (bf16[16,3072]{1,0:T(8,128)(2,1)S(1)}, bf16[16,3072]{1,0:T(8,128)(2,1)S(1)}) custom-call(s32[4]{0:T(128)S(1)} %iota_multiply_fusion.first_ref, s32[128]{0:T(128)S(1)} %bitcast.139, f32[32,128]{1,0:T(8,128)S(1)} %get-tuple-element.219.refs_1_, f32[32,128]{1,0:T(8,128)S(1)} %collective-permute-done.17.refs_2_, ...), custom_call_target="tpu_custom_call" | custom-call | flops 100663296 | bytes 3342336 | tf_op jit(solution)/shard_map/pallas_call | solution.py:325
  50.2 4.0 %collective-permute-done.18.refs_0_ = bf16[88,3072]{1,0:T(8,128)(2,1)S(1)} collective-permute-done((bf16[88,3072]{1,0:T(8,128)(2,1)S(1)}, bf16[88,3072]{1,0:T(8,128)(2,1)S(1)}, u32[]{:S(2)}, u32[]{:S(2)}) %collective-permute-start.18) | collective-permute-done | bytes 540704 | tf_op jit(solution)/shard_map/ppermute | solution.py:447
  54.2 1.7 %shard_map.82 = (f32[88,128]{1,0:T(8,128)S(1)}, f32[88,128]{1,0:T(8,128)S(1)}) custom-call(s32[4]{0:T(128)S(1)} %iota_multiply_fusion.first_ref, bf16[88,3072]{1,0:T(8,128)(2,1)S(1)} %collective-permute-done.18.refs_0_, bf16[512,3072]{1,0:T(8,128)(2,1)S(1)} %bitcast.147), custom_call_target="tpu_custom_call" | custom-call | flops 276824064 | bytes 3686400 | tf_op jit(solution)/shard_map/pallas_call | solution.py:280
  55.9 1.6 %collective-permute-start.19 = (f32[88,128]{1,0:T(8,128)S(1)}, f32[88,128]{1,0:T(8,128)S(1)}, u32[]{:S(2)}, u32[]{:S(2)}) collective-permute-start(f32[88,128]{1,0:T(8,128)S(1)} %get-tuple-element.224.refs_1_), channel_id=1, source_target_pairs={{0,2},{2,0},{1,3},{3,1},{4,6},{6,4},{5,7},{7,5},{8,10},{10,8},{9,1... | collective-permute-start | bytes 135176 | tf_op jit(solution)/shard_map/ppermute | solution.py:522
  57.8 2.0 %collective-permute-start.25 = (bf16[16,3072]{1,0:T(8,128)(2,1)S(1)}, bf16[16,3072]{1,0:T(8,128)(2,1)S(1)}, u32[]{:S(2)}, u32[]{:S(2)}) collective-permute-start(bf16[16,3072]{1,0:T(8,128)(2,1)S(1)} %get-tuple-element.222), channel_id=1, source_target_pairs={{0,12},{4,8},{8,4},{12,0},{1,13},{5,9},{9,5},{13,1},{2,14},{6,10},... | collective-permute-start | bytes 294920 | tf_op jit(solution)/shard_map/ppermute | solution.py:447
  59.8 0.2 collective-permute-done.19.refs_2_
  60.0 2.3 %shard_map.83 = bf16[88,3072]{1,0:T(8,128)(2,1)S(1)} custom-call(s32[4]{0:T(128)S(1)} %iota_multiply_fusion.first_ref, s32[128]{0:T(128)S(1)} %bitcast.140, f32[88,128]{1,0:T(8,128)S(1)} %get-tuple-element.224.refs_1_, f32[88,128]{1,0:T(8,128)S(1)} %collective-permute-done.19.refs_2_, f32[88,128]{1,0:T(8,128)S(1)} %get-tuple-element.225.refs_3_, ...), custom_call_target="tpu_custom_call" | custom-call | flops 276824064 | bytes 3686400 | tf_op jit(solution)/shard_map/pallas_call | solution.py:325
  62.3 1.3 %collective-permute-start.23 = (bf16[88,3072]{1,0:T(8,128)(2,1)S(1)}, bf16[88,3072]{1,0:T(8,128)(2,1)S(1)}, u32[]{:S(2)}, u32[]{:S(2)}) collective-permute-start(bf16[88,3072]{1,0:T(8,128)(2,1)S(1)} %shard_map.83), channel_id=1, source_target_pairs={{0,4},{4,0},{8,12},{12,8},{1,5},{5,1},{9,13},{13,9},{2,6},{6,2},{1... | collective-permute-start | bytes 1622024 | tf_op jit(solution)/shard_map/ppermute | solution.py:447
  63.6 1.7 %shard_map.84 = (f32[64,128]{1,0:T(8,128)S(1)}, f32[64,128]{1,0:T(8,128)S(1)}) custom-call(s32[4]{0:T(128)S(1)} %iota_multiply_fusion.first_ref, bf16[64,3072]{1,0:T(8,128)(2,1)S(1)} %collective-permute-done.20.refs_0_, bf16[512,3072]{1,0:T(8,128)(2,1)S(1)} %bitcast.148), custom_call_target="tpu_custom_call" | custom-call | flops 201326592 | bytes 3538944 | tf_op jit(solution)/shard_map/pallas_call | solution.py:280
  65.3 0.5 collective-permute-start.21
  65.8 3.5 %collective-permute-done.21.refs_1_ = f32[64,128]{1,0:T(8,128)S(1)} collective-permute-done((f32[64,128]{1,0:T(8,128)S(1)}, f32[64,128]{1,0:T(8,128)S(1)}, u32[]{:S(2)}, u32[]{:S(2)}) %collective-permute-start.21) | collective-permute-done | bytes 32800 | tf_op jit(solution)/shard_map/ppermute | solution.py:522
  69.3 2.2 %shard_map.85 = bf16[64,3072]{1,0:T(8,128)(2,1)S(1)} custom-call(s32[4]{0:T(128)S(1)} %iota_multiply_fusion.first_ref, f32[64,128]{1,0:T(8,128)S(1)} %get-tuple-element.227.refs_0_, f32[64,128]{1,0:T(8,128)S(1)} %collective-permute-done.21.refs_1_, f32[64,128]{1,0:T(8,128)S(1)} %get-tuple-element.228.refs_2_, bf16[512,3072]{1,0:T(8,128)(2,1)S(1)} %bitcast.153), custom_call_target="tpu_custom_call" | custom-call | flops 201326592 | bytes 3538944 | tf_op jit(solution)/shard_map/pallas_call | solution.py:325
  71.4 0.5 collective-permute-start.10
  72.0 6.0 %collective-permute-done.22.refs_5_ = bf16[64,3072]{1,0:T(8,128)(2,1)S(1)} collective-permute-done((bf16[64,3072]{1,0:T(8,128)(2,1)S(1)}, bf16[64,3072]{1,0:T(8,128)(2,1)S(1)}, u32[]{:S(2)}, u32[]{:S(2)}) %collective-permute-start.22) | collective-permute-done | bytes 393248 | tf_op jit(solution)/shard_map/ppermute | solution.py:447
  78.0 1.9 %collective-permute-done.24.first_ref.refs_7_ = bf16[16,3072]{1,0:T(8,128)(2,1)S(1)} collective-permute-done((bf16[16,3072]{1,0:T(8,128)(2,1)S(1)}, bf16[16,3072]{1,0:T(8,128)(2,1)S(1)}, u32[]{:S(2)}, u32[]{:S(2)}) %collective-permute-start.24) | collective-permute-done | bytes 98336 | tf_op jit(solution)/shard_map/ppermute | solution.py:447
  79.9 0.6 shard_map.86
  80.6 1.1 %collective-permute-start.27 = (bf16[64,3072]{1,0:T(8,128)(2,1)S(1)}, bf16[64,3072]{1,0:T(8,128)(2,1)S(1)}, u32[]{:S(2)}, u32[]{:S(2)}) collective-permute-start(bf16[64,3072]{1,0:T(8,128)(2,1)S(1)} %shard_map.85), channel_id=1, source_target_pairs={{0,12},{4,8},{8,4},{12,0},{1,13},{5,9},{9,5},{13,1},{2,14},{6,10},... | collective-permute-start | bytes 1179656 | tf_op jit(solution)/shard_map/ppermute | solution.py:447
  81.8 2.8 %shard_map.76.base_ref = bf16[256,3072]{1,0:T(8,128)(2,1)S(1)} custom-call(s32[4]{0:T(128)S(1)} %iota_multiply_fusion.first_ref, f32[256,128]{1,0:T(8,128)S(1)} %get-tuple-element.204.refs_0_, f32[256,128]{1,0:T(8,128)S(1)} %collective-permute-done.10.refs_1_, f32[256,128]{1,0:T(8,128)S(1)} %get-tuple-element.205.refs_2_, bf16[512,3072]{1,0:T(8,128)(2,1)S(1)} %bitcast.154), custom_call_target="tpu_custom_call" | custom-call | flops 805306368 | bytes 4718592 | tf_op jit(solution)/shard_map/pallas_call | solution.py:325
  84.6 10.4 %collective-permute-done.23.refs_6_ = bf16[88,3072]{1,0:T(8,128)(2,1)S(1)} collective-permute-done((bf16[88,3072]{1,0:T(8,128)(2,1)S(1)}, bf16[88,3072]{1,0:T(8,128)(2,1)S(1)}, u32[]{:S(2)}, u32[]{:S(2)}) %collective-permute-start.23) | collective-permute-done | bytes 540704 | tf_op jit(solution)/shard_map/ppermute | solution.py:447
  95.0 4.0 %shard_map.87 = (bf16[256,3072]{1,0:T(8,128)(2,1)S(1)}, s32[1]{0:T(128)}) custom-call(bf16[256,3072]{1,0:T(8,128)(2,1)S(1)} %shard_map.76.base_ref, bf16[256,64]{1,0:T(8,128)(2,1)S(1)} %get-tuple-element.338.refs_0_, bf16[256,88]{1,0:T(8,128)(2,1)S(1)} %fusion.80.refs_1_, bf16[256,16]{1,0:T(8,128)(2,1)S(1)} %get-tuple-element.336.refs_2_, ...), custom_call_target="tpu_custom_call" | custom-call | flops 1572864000 | bytes 15728640 | tf_op jit(solution)/shard_map/pallas_call | solution.py:301
  99.7 1.7 %fusion.69 = bf16[256,3072]{1,0:T(8,128)(2,1)} fusion(bf16[256,64]{1,0:T(8,128)(2,1)S(1)} %get-tuple-element.235, bf16[64,3072]{1,0:T(8,128)(2,1)S(1)} %collective-permute-done.27, bf16[256,3072]{1,0:T(8,128)(2,1)S(1)} %get-tuple-element.237), kind=kOutput, calls=%fused_computation.119 | convolution fusion | flops 103022592 | bytes 3571712 | tf_op jit(solution)/shard_map/dot_general | solution.py:618
  (41 shorter events, 1.1 us)
Async XLA Ops:
  0.0 10.0 %copy-start.4 = (bf16[4,64,3072]{2,1,0:T(8,128)(2,1)S(1)}, bf16[4,64,3072]{2,1,0:T(8,128)(2,1)}, u32[]{:S(2)}) copy-start(bf16[4,64,3072]{2,1,0:T(8,128)(2,1)} %param.9) | copy-start | bytes 4718596
  5.7 8.1 %collective-permute-start.9 = (bf16[16,3072]{1,0:T(8,128)(2,1)S(1)}, bf16[16,3072]{1,0:T(8,128)(2,1)S(1)}, u32[]{:S(2)}, u32[]{:S(2)}) collective-permute-start(bf16[16,3072]{1,0:T(8,128)(2,1)S(1)} %get-tuple-element.201), channel_id=1, source_target_pairs={{0,1},{1,0},{2,3},{3,2},{4,5},{5,4},{6,7},{7,6},{8,9},{9,8},{10,11... | collective-permute-start | bytes 294920 | tf_op jit(solution)/shard_map/ppermute | solution.py:556
  6.1 26.4 %collective-permute-start.13 = (bf16[64,3072]{1,0:T(8,128)(2,1)S(1)}, bf16[64,3072]{1,0:T(8,128)(2,1)S(1)}, u32[]{:S(2)}, u32[]{:S(2)}) collective-permute-start(bf16[64,3072]{1,0:T(8,128)(2,1)S(1)} %get-tuple-element.212), channel_id=1, source_target_pairs={{0,8},{4,12},{8,0},{12,4},{1,9},{5,13},{9,1},{13,5},{2,10},{6,14},... | collective-permute-start | bytes 1179656 | tf_op jit(solution)/shard_map/ppermute | solution.py:447
  13.7 18.8 %copy-start = (bf16[32,16,3072]{2,1,0:T(8,128)(2,1)S(1)}, bf16[32,16,3072]{2,1,0:T(8,128)(2,1)}, u32[]{:S(2)}) copy-start(bf16[32,16,3072]{2,1,0:T(8,128)(2,1)} %param.10) | copy-start | bytes 9437188
  15.8 5.3 %collective-permute-start.11 = (s32[1,128]{1,0:T(1,128)S(1)}, s32[1,128]{1,0:T(1,128)S(1)}, u32[]{:S(2)}, u32[]{:S(2)}) collective-permute-start(s32[1,128]{1,0:T(1,128)S(1)} %broadcast_in_dim.254), channel_id=1, source_target_pairs={{0,1},{1,0},{2,3},{3,2},{4,5},{5,4},{6,7},{7,6},{8,9},{9,8},{10,11... | collective-permute-start | bytes 1544 | tf_op jit(solution)/shard_map/ppermute | solution.py:515
  16.0 26.1 %collective-permute-start.15 = (bf16[16,3072]{1,0:T(8,128)(2,1)S(1)}, bf16[16,3072]{1,0:T(8,128)(2,1)S(1)}, u32[]{:S(2)}, u32[]{:S(2)}) collective-permute-start(bf16[16,3072]{1,0:T(8,128)(2,1)S(1)} %get-tuple-element.215), channel_id=1, source_target_pairs={{0,8},{4,12},{8,0},{12,4},{1,9},{5,13},{9,1},{13,5},{2,10},{6,14},... | collective-permute-start | bytes 294920 | tf_op jit(solution)/shard_map/ppermute | solution.py:447
  16.3 25.8 %collective-permute-start.16 = (bf16[16,3072]{1,0:T(8,128)(2,1)S(1)}, bf16[16,3072]{1,0:T(8,128)(2,1)S(1)}, u32[]{:S(2)}, u32[]{:S(2)}) collective-permute-start(bf16[16,3072]{1,0:T(8,128)(2,1)S(1)} %get-tuple-element.216), channel_id=1, source_target_pairs={{0,12},{4,8},{8,4},{12,0},{1,13},{5,9},{9,5},{13,1},{2,14},{6,10},... | collective-permute-start | bytes 294920 | tf_op jit(solution)/shard_map/ppermute | solution.py:447
  20.4 19.5 %copy-start.2 = (bf16[32,16,3072]{2,1,0:T(8,128)(2,1)S(1)}, bf16[32,16,3072]{2,1,0:T(8,128)(2,1)}, u32[]{:S(2)}) copy-start(bf16[32,16,3072]{2,1,0:T(8,128)(2,1)} %param.11) | copy-start | bytes 9437188
  21.0 33.2 %collective-permute-start.18 = (bf16[88,3072]{1,0:T(8,128)(2,1)S(1)}, bf16[88,3072]{1,0:T(8,128)(2,1)S(1)}, u32[]{:S(2)}, u32[]{:S(2)}) collective-permute-start(bf16[88,3072]{1,0:T(8,128)(2,1)S(1)} %fusion.70), channel_id=1, source_target_pairs={{0,4},{4,0},{8,12},{12,8},{1,5},{5,1},{9,13},{13,9},{2,6},{6,2},{1... | collective-permute-start | bytes 1622024 | tf_op jit(solution)/shard_map/ppermute | solution.py:447
  22.0 14.1 %collective-permute-start.12 = (s32[1,128]{1,0:T(1,128)S(1)}, s32[1,128]{1,0:T(1,128)S(1)}, u32[]{:S(2)}, u32[]{:S(2)}) collective-permute-start(s32[1,128]{1,0:T(1,128)S(1)} %broadcast_maximum_fusion), channel_id=1, source_target_pairs={{0,16},{16,0},{1,17},{17,1},{2,18},{18,2},{3,19},{19,3},{4,20},{20... | collective-permute-start | bytes 1544 | tf_op jit(solution)/shard_map/ppermute | solution.py:515
  34.3 5.6 %collective-permute-start.14 = (f32[64,128]{1,0:T(8,128)S(1)}, f32[64,128]{1,0:T(8,128)S(1)}, u32[]{:S(2)}, u32[]{:S(2)}) collective-permute-start(f32[64,128]{1,0:T(8,128)S(1)} %get-tuple-element.213.refs_1_), channel_id=1, source_target_pairs={{0,2},{2,0},{1,3},{3,1},{4,6},{6,4},{5,7},{7,5},{8,10},{10,8},{9,1... | collective-permute-start | bytes 98312 | tf_op jit(solution)/shard_map/ppermute | solution.py:522
  36.7 26.8 %collective-permute-start.20 = (bf16[64,3072]{1,0:T(8,128)(2,1)S(1)}, bf16[64,3072]{1,0:T(8,128)(2,1)S(1)}, u32[]{:S(2)}, u32[]{:S(2)}) collective-permute-start(bf16[64,3072]{1,0:T(8,128)(2,1)S(1)} %fusion.71), channel_id=1, source_target_pairs={{0,12},{4,8},{8,4},{12,0},{1,13},{5,9},{9,5},{13,1},{2,14},{6,10},... | collective-permute-start | bytes 1179656 | tf_op jit(solution)/shard_map/ppermute | solution.py:447
  44.4 3.8 %collective-permute-start.17 = (f32[32,128]{1,0:T(8,128)S(1)}, f32[32,128]{1,0:T(8,128)S(1)}, u32[]{:S(2)}, u32[]{:S(2)}) collective-permute-start(f32[32,128]{1,0:T(8,128)S(1)} %get-tuple-element.219.refs_1_), channel_id=1, source_target_pairs={{0,2},{2,0},{1,3},{3,1},{4,6},{6,4},{5,7},{7,5},{8,10},{10,8},{9,1... | collective-permute-start | bytes 49160 | tf_op jit(solution)/shard_map/ppermute | solution.py:522
  45.1 32.9 %collective-permute-start.22 = (bf16[64,3072]{1,0:T(8,128)(2,1)S(1)}, bf16[64,3072]{1,0:T(8,128)(2,1)S(1)}, u32[]{:S(2)}, u32[]{:S(2)}) collective-permute-start(bf16[64,3072]{1,0:T(8,128)(2,1)S(1)} %shard_map.79), channel_id=1, source_target_pairs={{0,8},{4,12},{8,0},{12,4},{1,9},{5,13},{9,1},{13,5},{2,10},{6,14},... | collective-permute-start | bytes 1179656 | tf_op jit(solution)/shard_map/ppermute | solution.py:447
  55.9 4.1 %collective-permute-start.19 = (f32[88,128]{1,0:T(8,128)S(1)}, f32[88,128]{1,0:T(8,128)S(1)}, u32[]{:S(2)}, u32[]{:S(2)}) collective-permute-start(f32[88,128]{1,0:T(8,128)S(1)} %get-tuple-element.224.refs_1_), channel_id=1, source_target_pairs={{0,2},{2,0},{1,3},{3,1},{4,6},{6,4},{5,7},{7,5},{8,10},{10,8},{9,1... | collective-permute-start | bytes 135176 | tf_op jit(solution)/shard_map/ppermute | solution.py:522
  57.7 22.3 %collective-permute-start.24 = (bf16[16,3072]{1,0:T(8,128)(2,1)S(1)}, bf16[16,3072]{1,0:T(8,128)(2,1)S(1)}, u32[]{:S(2)}, u32[]{:S(2)}) collective-permute-start(bf16[16,3072]{1,0:T(8,128)(2,1)S(1)} %get-tuple-element.221), channel_id=1, source_target_pairs={{0,8},{4,12},{8,0},{12,4},{1,9},{5,13},{9,1},{13,5},{2,10},{6,14},... | collective-permute-start | bytes 294920 | tf_op jit(solution)/shard_map/ppermute | solution.py:447
  57.8 22.1 %collective-permute-start.25 = (bf16[16,3072]{1,0:T(8,128)(2,1)S(1)}, bf16[16,3072]{1,0:T(8,128)(2,1)S(1)}, u32[]{:S(2)}, u32[]{:S(2)}) collective-permute-start(bf16[16,3072]{1,0:T(8,128)(2,1)S(1)} %get-tuple-element.222), channel_id=1, source_target_pairs={{0,12},{4,8},{8,4},{12,0},{1,13},{5,9},{9,5},{13,1},{2,14},{6,10},... | collective-permute-start | bytes 294920 | tf_op jit(solution)/shard_map/ppermute | solution.py:447
  62.3 32.8 %collective-permute-start.23 = (bf16[88,3072]{1,0:T(8,128)(2,1)S(1)}, bf16[88,3072]{1,0:T(8,128)(2,1)S(1)}, u32[]{:S(2)}, u32[]{:S(2)}) collective-permute-start(bf16[88,3072]{1,0:T(8,128)(2,1)S(1)} %shard_map.83), channel_id=1, source_target_pairs={{0,4},{4,0},{8,12},{12,8},{1,5},{5,1},{9,13},{13,9},{2,6},{6,2},{1... | collective-permute-start | bytes 1622024 | tf_op jit(solution)/shard_map/ppermute | solution.py:447
  65.3 4.0 %collective-permute-start.21 = (f32[64,128]{1,0:T(8,128)S(1)}, f32[64,128]{1,0:T(8,128)S(1)}, u32[]{:S(2)}, u32[]{:S(2)}) collective-permute-start(f32[64,128]{1,0:T(8,128)S(1)} %get-tuple-element.227.refs_0_), channel_id=1, source_target_pairs={{0,2},{2,0},{1,3},{3,1},{4,6},{6,4},{5,7},{7,5},{8,10},{10,8},{9,1... | collective-permute-start | bytes 98312 | tf_op jit(solution)/shard_map/ppermute | solution.py:522
  71.4 10.4 %collective-permute-start.10 = (f32[256,128]{1,0:T(8,128)S(1)}, f32[256,128]{1,0:T(8,128)S(1)}, u32[]{:S(2)}, u32[]{:S(2)}) collective-permute-start(f32[256,128]{1,0:T(8,128)S(1)} %get-tuple-element.204.refs_0_), channel_id=1, source_target_pairs={{0,2},{2,0},{1,3},{3,1},{4,6},{6,4},{5,7},{7,5},{8,10},{10,8},{9,1... | collective-permute-start | bytes 393224 | tf_op jit(solution)/shard_map/ppermute | solution.py:522
  80.5 4.1 %collective-permute-start.26 = (bf16[16,3072]{1,0:T(8,128)(2,1)S(1)}, bf16[16,3072]{1,0:T(8,128)(2,1)S(1)}, u32[]{:S(2)}, u32[]{:S(2)}) collective-permute-start(bf16[16,3072]{1,0:T(8,128)(2,1)S(1)} %shard_map.86), channel_id=1, source_target_pairs={{0,1},{1,0},{2,3},{3,2},{4,5},{5,4},{6,7},{7,6},{8,9},{9,8},{10,11... | collective-permute-start | bytes 294920 | tf_op jit(solution)/shard_map/ppermute | solution.py:600
  80.6 19.1 %collective-permute-start.27 = (bf16[64,3072]{1,0:T(8,128)(2,1)S(1)}, bf16[64,3072]{1,0:T(8,128)(2,1)S(1)}, u32[]{:S(2)}, u32[]{:S(2)}) collective-permute-start(bf16[64,3072]{1,0:T(8,128)(2,1)S(1)} %shard_map.85), channel_id=1, source_target_pairs={{0,12},{4,8},{8,4},{12,0},{1,13},{5,9},{9,5},{13,1},{2,14},{6,10},... | collective-permute-start | bytes 1179656 | tf_op jit(solution)/shard_map/ppermute | solution.py:447

commit v7 on v6

--- a/solution.py
+++ b/solution.py
@@ -296,7 +296,7 @@
 
 def back_call(base, places, returned, told, weight=1):
     rows, width = base.shape
-    tile = width // 6 if width % (6 * LANES) == 0 else width
+    tile = width // 3 if width % (3 * LANES) == 0 else width
     tiles = lambda count: pl.BlockSpec((count, tile), lambda i: (0, i))
     return pl.pallas_call(
         functools.partial(back_kernel, len(returned)),
@@ -320,7 +320,7 @@
     width = weights[0].shape[1]
     rows = names.shape[0]
     spots = sum(weight.shape[0] for weight in weights)
-    tile = width // 6 if width % (6 * LANES) == 0 else width
+    tile = width // 3 if width % (3 * LANES) == 0 else width
     whole = pl.BlockSpec(memory_space=pltpu.VMEM)
     return pl.pallas_call(
         functools.partial(
@@ -558,7 +558,10 @@
         own_names, _ = lax.optimization_barrier((own_names, spill))
         partial, names = shrink([flat_x], own_names)
         partial, key, row_rank, guests = lax.optimization_barrier((partial, key, row_rank, guests))
-        came["L"] = [swap(pack(last, 0, main_block, key, row_rank, 0), last)]
+        packed, guests = lax.optimization_barrier(
+            (pack(last, 0, main_block, key, row_rank, 0), guests)
+        )
+        came["L"] = [swap(packed, last)]
         came["N"] = [swap(pack(near, 0, block, key, row_rank, 0), near)]
         shared_first, shared_last, placed, remaining, rounds = small_call(
             functools.partial(settle_kernel, first, room, shared, block - 1, more_block - 1),

time: 102 us -> 101 us (level)
  Pallas kernels: 32.2 us -> 29.2 us
  waiting for transfers between devices: 37.9 us -> 39.9 us
    pallas_call x5, Pallas kernels: 11.5 us -> 9 us  [expand_call(): pl.pallas_call(functools.partial(expand_kernel, counts, len(partials), le...]
    ppermute x10, waiting for transfers between devices: 31.3 us -> 33.5 us  [swap(): lax.ppermute(values, 'hst', [(i, i ^ step) for i in range(host_count)])]
  transfers between devices with their start and end apart: 19 -> 19, of which waited for: 8 -> 7; matrix products, arithmetic and copies ran while one was open for 4% -> 4% of each run, Pallas kernels for 28% -> 25%
where the time goes in v7:
time: 101 us
  waiting for transfers between devices  39.9 us (40%)
  Pallas kernels  29.2 us (29%)
  starting transfers between devices  23 us (23%)
  other arithmetic  3.81 us (4%)
  matrix products  2.56 us (3%)
  local copies, waits for them, and re-layouts  1.05 us (1%)
    ppermute x10, waiting for transfers between devices, swap(): lax.ppermute(values, 'hst', [(i, i ^ step) for i in range(host_count)])  33.5 us
    ppermute x10, starting transfers between devices, swap(): lax.ppermute(values, 'hst', [(i, i ^ step) for i in range(host_count)])  15.6 us
    pallas_call x5, Pallas kernels, shrink_call(): pl.pallas_call(functools.partial(shrink_kernel, counts, own_names is not...  11.1 us
    pallas_call x5, Pallas kernels, expand_call(): pl.pallas_call(functools.partial(expand_kernel, counts, len(partials), le...  9 us
    ppermute x5, waiting for transfers between devices, over_shares(): lax.ppermute(partial, 'mp', [(i, (i + hop) % shares) for i in range(share...  6.39 us
    pallas_call x4, Pallas kernels, small_call(): pl.pallas_call(kernel, out_shape=[jax.ShapeDtypeStruct(shape, dtype) for...  5.56 us
    ppermute x5, starting transfers between devices, over_shares(): lax.ppermute(partial, 'mp', [(i, (i + hop) % shares) for i in range(share...  5.06 us
    pallas_call x1, Pallas kernels, back_call(): pl.pallas_call(functools.partial(back_kernel, len(returned)), grid=(width...  3.49 us
  transfers between devices with their start and end apart: 19, of which 7 were waited for; matrix products, arithmetic and copies ran while one was open for 4% of the time, Pallas kernels for 25%

profile of v7, /device:TPU:0, one launch (start us, length us, event | category | flops | bytes accessed | tf_op | source)
XLA Modules:
  0.0 100.6 jit_solution(4445561648536840319)
XLA Ops:
  0.0 0.8 bitcast_add_fusion
  0.9 0.8 select_reduce_fusion.5
  1.8 2.1 %shard_map.73 = (bf16[64,3072]{1,0:T(8,128)(2,1)S(1)}, s32[8,256]{1,0:T(8,128)S(1)}) custom-call(s32[1]{0:T(128)} %bitcast.1.me_ref, s32[1,128]{1,0:T(1,128)S(1)} %bitcast.142, s32[1,256]{1,0:T(1,128)S(1)} %reshape_reshape.3.wanted_ref, bf16[256,3072]{1,0:T(8,128)(2,1)} %bitcast.155), custom_call_target="tpu_custom_call" | custom-call | tf_op jit(solution)/shard_map/pallas_call | solution.py:245
  3.8 1.9 %shard_map.74 = (bf16[16,3072]{1,0:T(8,128)(2,1)S(1)}, s32[8,256]{1,0:T(8,128)S(1)}) custom-call(s32[8,256]{1,0:T(8,128)S(1)} %get-tuple-element.202.route_ref, bf16[256,3072]{1,0:T(8,128)(2,1)} %bitcast.156), custom_call_target="tpu_custom_call" | custom-call | tf_op jit(solution)/shard_map/pallas_call | solution.py:245
  5.7 0.5 collective-permute-start.9
  6.1 3.7 %collective-permute-start.13 = (bf16[64,3072]{1,0:T(8,128)(2,1)S(1)}, bf16[64,3072]{1,0:T(8,128)(2,1)S(1)}, u32[]{:S(2)}, u32[]{:S(2)}) collective-permute-start(bf16[64,3072]{1,0:T(8,128)(2,1)S(1)} %get-tuple-element.215), channel_id=1, source_target_pairs={{0,8},{4,12},{8,0},{12,4},{1,9},{5,13},{9,1},{13,5},{2,10},{6,14},... | collective-permute-start | bytes 1179656 | tf_op jit(solution)/shard_map/ppermute | solution.py:447
  10.0 3.7 %shard_map.75 = (f32[256,128]{1,0:T(8,128)S(1)}, f32[256,128]{1,0:T(8,128)S(1)}) custom-call(s32[4]{0:T(128)S(1)} %iota_multiply_fusion.first_ref, bf16[256,3072]{1,0:T(8,128)(2,1)S(1)} %bitcast.158, f32[256,1]{1,0:T(8,128)S(1)} %copy.14.refs_1_, bf16[512,3072]{1,0:T(8,128)(2,1)} %bitcast.143), custom_call_target="tpu_custom_call" | custom-call | flops 805306368 | bytes 4718592 | tf_op jit(solution)/shard_map/pallas_call | solution.py:280
  13.8 0.2 select_reduce_fusion.3
  14.1 0.4 fusion.71
  14.5 1.1 %shard_map.77 = (bf16[16,3072]{1,0:T(8,128)(2,1)S(1)}, bf16[16,3072]{1,0:T(8,128)(2,1)S(1)}, f32[2,16,128]{2,1,0:T(8,128)S(1)}, s32[8,256]{1,0:T(8,128)S(1)}, s32[1]{0:T(128)}) custom-call(s32[8,256]{1,0:T(8,128)S(1)} %get-tuple-element.202.route_ref, s32[8,256]{1,0:T(8,128)S(1)} %get-tuple-element.210.index_ref, bf16[256,3072]{1,0:T(8,128)(2,1)S(1)} %bitcast.160, ...), custom_call_target="tpu_custom_call" | custom-call | tf_op jit(solution)/shard_map/pallas_call | solution.py:245
  15.6 0.8 broadcast_in_dim.260
  16.4 0.2 collective-permute-start.11
  16.6 0.3 collective-permute-start.15
  16.9 3.7 %collective-permute-start.16 = (bf16[16,3072]{1,0:T(8,128)(2,1)S(1)}, bf16[16,3072]{1,0:T(8,128)(2,1)S(1)}, u32[]{:S(2)}, u32[]{:S(2)}) collective-permute-start(bf16[16,3072]{1,0:T(8,128)(2,1)S(1)} %get-tuple-element.219), channel_id=1, source_target_pairs={{0,12},{4,8},{8,4},{12,0},{1,13},{5,9},{9,5},{13,1},{2,14},{6,10},... | collective-permute-start | bytes 294920 | tf_op jit(solution)/shard_map/ppermute | solution.py:447
  20.6 0.4 fusion.70
  21.0 0.2 fusion.85
  21.3 0.7 broadcast_maximum_fusion
  21.9 1.6 %collective-permute-start.12 = (s32[1,128]{1,0:T(1,128)S(1)}, s32[1,128]{1,0:T(1,128)S(1)}, u32[]{:S(2)}, u32[]{:S(2)}) collective-permute-start(s32[1,128]{1,0:T(1,128)S(1)} %broadcast_maximum_fusion), channel_id=1, source_target_pairs={{0,16},{16,0},{1,17},{17,1},{2,18},{18,2},{3,19},{19,3},{4,20},{20... | collective-permute-start | bytes 1544 | tf_op jit(solution)/shard_map/ppermute | solution.py:515
  23.5 9.0 %collective-permute-done.13.refs_0_ = bf16[64,3072]{1,0:T(8,128)(2,1)S(1)} collective-permute-done((bf16[64,3072]{1,0:T(8,128)(2,1)S(1)}, bf16[64,3072]{1,0:T(8,128)(2,1)S(1)}, u32[]{:S(2)}, u32[]{:S(2)}) %collective-permute-start.13) | collective-permute-done | bytes 393248 | tf_op jit(solution)/shard_map/ppermute | solution.py:447
  32.5 1.7 %shard_map.78 = (f32[64,128]{1,0:T(8,128)S(1)}, f32[64,128]{1,0:T(8,128)S(1)}) custom-call(s32[4]{0:T(128)S(1)} %iota_multiply_fusion.first_ref, bf16[64,3072]{1,0:T(8,128)(2,1)S(1)} %collective-permute-done.13.refs_0_, bf16[512,3072]{1,0:T(8,128)(2,1)S(1)} %bitcast.145), custom_call_target="tpu_custom_call" | custom-call | flops 201326592 | bytes 3538944 | tf_op jit(solution)/shard_map/pallas_call | solution.py:280
  34.3 1.8 %collective-permute-start.14 = (f32[64,128]{1,0:T(8,128)S(1)}, f32[64,128]{1,0:T(8,128)S(1)}, u32[]{:S(2)}, u32[]{:S(2)}) collective-permute-start(f32[64,128]{1,0:T(8,128)S(1)} %get-tuple-element.216.refs_1_), channel_id=1, source_target_pairs={{0,2},{2,0},{1,3},{3,1},{4,6},{6,4},{5,7},{7,5},{8,10},{10,8},{9,1... | collective-permute-start | bytes 98312 | tf_op jit(solution)/shard_map/ppermute | solution.py:522
  36.1 0.6 fusion.123
  36.7 3.1 %collective-permute-start.20 = (bf16[64,3072]{1,0:T(8,128)(2,1)S(1)}, bf16[64,3072]{1,0:T(8,128)(2,1)S(1)}, u32[]{:S(2)}, u32[]{:S(2)}) collective-permute-start(bf16[64,3072]{1,0:T(8,128)(2,1)S(1)} %fusion.71), channel_id=1, source_target_pairs={{0,12},{4,8},{8,4},{12,0},{1,13},{5,9},{9,5},{13,1},{2,14},{6,10},... | collective-permute-start | bytes 1179656 | tf_op jit(solution)/shard_map/ppermute | solution.py:447
  39.9 1.7 %shard_map.79 = bf16[64,3072]{1,0:T(8,128)(2,1)S(1)} custom-call(s32[4]{0:T(128)S(1)} %iota_multiply_fusion.first_ref, s32[128]{0:T(128)S(1)} %bitcast.138, f32[64,128]{1,0:T(8,128)S(1)} %get-tuple-element.216.refs_1_, f32[64,128]{1,0:T(8,128)S(1)} %collective-permute-done.14.refs_2_, f32[64,128]{1,0:T(8,128)S(1)} %get-tuple-element.217.refs_3_, ...), custom_call_target="tpu_custom_call" | custom-call | flops 201326592 | bytes 3538944 | tf_op jit(solution)/shard_map/pallas_call | solution.py:325
  41.6 2.3 %shard_map.80 = (f32[32,128]{1,0:T(8,128)S(1)}, f32[32,128]{1,0:T(8,128)S(1)}) custom-call(s32[4]{0:T(128)S(1)} %iota_multiply_fusion.first_ref, bf16[16,3072]{1,0:T(8,128)(2,1)S(1)} %collective-permute-done.15.refs_0_, bf16[16,3072]{1,0:T(8,128)(2,1)S(1)} %collective-permute-done.16.refs_1_, bf16[512,3072]{1,0:T(8,128)(2,1)S(1)} %bitcast.146), custom_call_target="tpu_custom_call" | custom-call | flops 100663296 | bytes 3342336 | tf_op jit(solution)/shard_map/pallas_call | solution.py:280
  43.9 0.6 collective-permute-start.17
  44.7 2.9 %collective-permute-done.17.refs_2_ = f32[32,128]{1,0:T(8,128)S(1)} collective-permute-done((f32[32,128]{1,0:T(8,128)S(1)}, f32[32,128]{1,0:T(8,128)S(1)}, u32[]{:S(2)}, u32[]{:S(2)}) %collective-permute-start.17) | collective-permute-done | bytes 16416 | tf_op jit(solution)/shard_map/ppermute | solution.py:522
  47.6 1.7 %shard_map.81 = (bf16[16,3072]{1,0:T(8,128)(2,1)S(1)}, bf16[16,3072]{1,0:T(8,128)(2,1)S(1)}) custom-call(s32[4]{0:T(128)S(1)} %iota_multiply_fusion.first_ref, s32[128]{0:T(128)S(1)} %bitcast.139, f32[32,128]{1,0:T(8,128)S(1)} %get-tuple-element.222.refs_1_, f32[32,128]{1,0:T(8,128)S(1)} %collective-permute-done.17.refs_2_, ...), custom_call_target="tpu_custom_call" | custom-call | flops 100663296 | bytes 3342336 | tf_op jit(solution)/shard_map/pallas_call | solution.py:325
  49.3 4.6 %collective-permute-done.18.refs_0_ = bf16[88,3072]{1,0:T(8,128)(2,1)S(1)} collective-permute-done((bf16[88,3072]{1,0:T(8,128)(2,1)S(1)}, bf16[88,3072]{1,0:T(8,128)(2,1)S(1)}, u32[]{:S(2)}, u32[]{:S(2)}) %collective-permute-start.18) | collective-permute-done | bytes 540704 | tf_op jit(solution)/shard_map/ppermute | solution.py:447
  54.0 1.7 %shard_map.82 = (f32[88,128]{1,0:T(8,128)S(1)}, f32[88,128]{1,0:T(8,128)S(1)}) custom-call(s32[4]{0:T(128)S(1)} %iota_multiply_fusion.first_ref, bf16[88,3072]{1,0:T(8,128)(2,1)S(1)} %collective-permute-done.18.refs_0_, bf16[512,3072]{1,0:T(8,128)(2,1)S(1)} %bitcast.147), custom_call_target="tpu_custom_call" | custom-call | flops 276824064 | bytes 3686400 | tf_op jit(solution)/shard_map/pallas_call | solution.py:280
  55.6 1.6 %collective-permute-start.19 = (f32[88,128]{1,0:T(8,128)S(1)}, f32[88,128]{1,0:T(8,128)S(1)}, u32[]{:S(2)}, u32[]{:S(2)}) collective-permute-start(f32[88,128]{1,0:T(8,128)S(1)} %get-tuple-element.227.refs_1_), channel_id=1, source_target_pairs={{0,2},{2,0},{1,3},{3,1},{4,6},{6,4},{5,7},{7,5},{8,10},{10,8},{9,1... | collective-permute-start | bytes 135176 | tf_op jit(solution)/shard_map/ppermute | solution.py:522
  57.4 0.6 collective-permute-start.24
  58.0 2.0 %collective-permute-start.25 = (bf16[16,3072]{1,0:T(8,128)(2,1)S(1)}, bf16[16,3072]{1,0:T(8,128)(2,1)S(1)}, u32[]{:S(2)}, u32[]{:S(2)}) collective-permute-start(bf16[16,3072]{1,0:T(8,128)(2,1)S(1)} %get-tuple-element.225), channel_id=1, source_target_pairs={{0,12},{4,8},{8,4},{12,0},{1,13},{5,9},{9,5},{13,1},{2,14},{6,10},... | collective-permute-start | bytes 294920 | tf_op jit(solution)/shard_map/ppermute | solution.py:447
  60.0 1.7 %shard_map.83 = bf16[88,3072]{1,0:T(8,128)(2,1)S(1)} custom-call(s32[4]{0:T(128)S(1)} %iota_multiply_fusion.first_ref, s32[128]{0:T(128)S(1)} %bitcast.140, f32[88,128]{1,0:T(8,128)S(1)} %get-tuple-element.227.refs_1_, f32[88,128]{1,0:T(8,128)S(1)} %collective-permute-done.19.refs_2_, f32[88,128]{1,0:T(8,128)S(1)} %get-tuple-element.228.refs_3_, ...), custom_call_target="tpu_custom_call" | custom-call | flops 276824064 | bytes 3686400 | tf_op jit(solution)/shard_map/pallas_call | solution.py:325
  61.7 1.0 %collective-permute-start.23 = (bf16[88,3072]{1,0:T(8,128)(2,1)S(1)}, bf16[88,3072]{1,0:T(8,128)(2,1)S(1)}, u32[]{:S(2)}, u32[]{:S(2)}) collective-permute-start(bf16[88,3072]{1,0:T(8,128)(2,1)S(1)} %shard_map.83), channel_id=1, source_target_pairs={{0,4},{4,0},{8,12},{12,8},{1,5},{5,1},{9,13},{13,9},{2,6},{6,2},{1... | collective-permute-start | bytes 1622024 | tf_op jit(solution)/shard_map/ppermute | solution.py:447
  62.7 1.7 %shard_map.84 = (f32[64,128]{1,0:T(8,128)S(1)}, f32[64,128]{1,0:T(8,128)S(1)}) custom-call(s32[4]{0:T(128)S(1)} %iota_multiply_fusion.first_ref, bf16[64,3072]{1,0:T(8,128)(2,1)S(1)} %collective-permute-done.20.refs_0_, bf16[512,3072]{1,0:T(8,128)(2,1)S(1)} %bitcast.148), custom_call_target="tpu_custom_call" | custom-call | flops 201326592 | bytes 3538944 | tf_op jit(solution)/shard_map/pallas_call | solution.py:280
  64.5 0.5 collective-permute-start.21
  65.0 3.4 %collective-permute-done.21.refs_1_ = f32[64,128]{1,0:T(8,128)S(1)} collective-permute-done((f32[64,128]{1,0:T(8,128)S(1)}, f32[64,128]{1,0:T(8,128)S(1)}, u32[]{:S(2)}, u32[]{:S(2)}) %collective-permute-start.21) | collective-permute-done | bytes 32800 | tf_op jit(solution)/shard_map/ppermute | solution.py:522
  68.5 1.7 %shard_map.85 = bf16[64,3072]{1,0:T(8,128)(2,1)S(1)} custom-call(s32[4]{0:T(128)S(1)} %iota_multiply_fusion.first_ref, f32[64,128]{1,0:T(8,128)S(1)} %get-tuple-element.231.refs_0_, f32[64,128]{1,0:T(8,128)S(1)} %collective-permute-done.21.refs_1_, f32[64,128]{1,0:T(8,128)S(1)} %get-tuple-element.232.refs_2_, bf16[512,3072]{1,0:T(8,128)(2,1)S(1)} %bitcast.153), custom_call_target="tpu_custom_call" | custom-call | flops 201326592 | bytes 3538944 | tf_op jit(solution)/shard_map/pallas_call | solution.py:325
  70.2 0.5 collective-permute-start.10
  70.7 7.3 %collective-permute-done.22.refs_5_ = bf16[64,3072]{1,0:T(8,128)(2,1)S(1)} collective-permute-done((bf16[64,3072]{1,0:T(8,128)(2,1)S(1)}, bf16[64,3072]{1,0:T(8,128)(2,1)S(1)}, u32[]{:S(2)}, u32[]{:S(2)}) %collective-permute-start.22) | collective-permute-done | bytes 393248 | tf_op jit(solution)/shard_map/ppermute | solution.py:447
  78.0 1.9 %collective-permute-done.24.first_ref.refs_7_ = bf16[16,3072]{1,0:T(8,128)(2,1)S(1)} collective-permute-done((bf16[16,3072]{1,0:T(8,128)(2,1)S(1)}, bf16[16,3072]{1,0:T(8,128)(2,1)S(1)}, u32[]{:S(2)}, u32[]{:S(2)}) %collective-permute-start.24) | collective-permute-done | bytes 98336 | tf_op jit(solution)/shard_map/ppermute | solution.py:447
  79.9 0.6 shard_map.86
  80.6 1.1 %collective-permute-start.27 = (bf16[64,3072]{1,0:T(8,128)(2,1)S(1)}, bf16[64,3072]{1,0:T(8,128)(2,1)S(1)}, u32[]{:S(2)}, u32[]{:S(2)}) collective-permute-start(bf16[64,3072]{1,0:T(8,128)(2,1)S(1)} %shard_map.85), channel_id=1, source_target_pairs={{0,12},{4,8},{8,4},{12,0},{1,13},{5,9},{9,5},{13,1},{2,14},{6,10},... | collective-permute-start | bytes 1179656 | tf_op jit(solution)/shard_map/ppermute | solution.py:447
  81.8 2.2 %shard_map.76.base_ref = bf16[256,3072]{1,0:T(8,128)(2,1)S(1)} custom-call(s32[4]{0:T(128)S(1)} %iota_multiply_fusion.first_ref, f32[256,128]{1,0:T(8,128)S(1)} %get-tuple-element.206.refs_0_, f32[256,128]{1,0:T(8,128)S(1)} %collective-permute-done.10.refs_1_, f32[256,128]{1,0:T(8,128)S(1)} %get-tuple-element.207.refs_2_, bf16[512,3072]{1,0:T(8,128)(2,1)S(1)} %bitcast.154), custom_call_target="tpu_custom_call" | custom-call | flops 805306368 | bytes 4718592 | tf_op jit(solution)/shard_map/pallas_call | solution.py:325
  84.1 10.6 %collective-permute-done.23.refs_6_ = bf16[88,3072]{1,0:T(8,128)(2,1)S(1)} collective-permute-done((bf16[88,3072]{1,0:T(8,128)(2,1)S(1)}, bf16[88,3072]{1,0:T(8,128)(2,1)S(1)}, u32[]{:S(2)}, u32[]{:S(2)}) %collective-permute-start.23) | collective-permute-done | bytes 540704 | tf_op jit(solution)/shard_map/ppermute | solution.py:447
  94.7 3.5 %shard_map.87 = (bf16[256,3072]{1,0:T(8,128)(2,1)S(1)}, s32[1]{0:T(128)}) custom-call(bf16[256,3072]{1,0:T(8,128)(2,1)S(1)} %shard_map.76.base_ref, bf16[256,64]{1,0:T(8,128)(2,1)S(1)} %get-tuple-element.342.refs_0_, bf16[256,88]{1,0:T(8,128)(2,1)S(1)} %fusion.80.refs_1_, bf16[256,16]{1,0:T(8,128)(2,1)S(1)} %get-tuple-element.340.refs_2_, ...), custom_call_target="tpu_custom_call" | custom-call | flops 1572864000 | bytes 15728640 | tf_op jit(solution)/shard_map/pallas_call | solution.py:301
  98.9 1.7 %fusion.69 = bf16[256,3072]{1,0:T(8,128)(2,1)} fusion(bf16[256,64]{1,0:T(8,128)(2,1)S(1)} %get-tuple-element.239, bf16[64,3072]{1,0:T(8,128)(2,1)S(1)} %collective-permute-done.27, bf16[256,3072]{1,0:T(8,128)(2,1)S(1)} %get-tuple-element.241), kind=kOutput, calls=%fused_computation.119 | convolution fusion | flops 103022592 | bytes 3571712 | tf_op jit(solution)/shard_map/dot_general | solution.py:621
  (42 shorter events, 1.0 us)
Async XLA Ops:
  0.0 10.0 %copy-start.4 = (bf16[4,64,3072]{2,1,0:T(8,128)(2,1)S(1)}, bf16[4,64,3072]{2,1,0:T(8,128)(2,1)}, u32[]{:S(2)}) copy-start(bf16[4,64,3072]{2,1,0:T(8,128)(2,1)} %param.9) | copy-start | bytes 4718596
  5.7 8.1 %collective-permute-start.9 = (bf16[16,3072]{1,0:T(8,128)(2,1)S(1)}, bf16[16,3072]{1,0:T(8,128)(2,1)S(1)}, u32[]{:S(2)}, u32[]{:S(2)}) collective-permute-start(bf16[16,3072]{1,0:T(8,128)(2,1)S(1)} %get-tuple-element.203), channel_id=1, source_target_pairs={{0,1},{1,0},{2,3},{3,2},{4,5},{5,4},{6,7},{7,6},{8,9},{9,8},{10,11... | collective-permute-start | bytes 294920 | tf_op jit(solution)/shard_map/ppermute | solution.py:556
  6.1 26.4 %collective-permute-start.13 = (bf16[64,3072]{1,0:T(8,128)(2,1)S(1)}, bf16[64,3072]{1,0:T(8,128)(2,1)S(1)}, u32[]{:S(2)}, u32[]{:S(2)}) collective-permute-start(bf16[64,3072]{1,0:T(8,128)(2,1)S(1)} %get-tuple-element.215), channel_id=1, source_target_pairs={{0,8},{4,12},{8,0},{12,4},{1,9},{5,13},{9,1},{13,5},{2,10},{6,14},... | collective-permute-start | bytes 1179656 | tf_op jit(solution)/shard_map/ppermute | solution.py:447
  13.8 18.8 %copy-start = (bf16[32,16,3072]{2,1,0:T(8,128)(2,1)S(1)}, bf16[32,16,3072]{2,1,0:T(8,128)(2,1)}, u32[]{:S(2)}) copy-start(bf16[32,16,3072]{2,1,0:T(8,128)(2,1)} %param.10) | copy-start | bytes 9437188
  15.6 24.3 %copy-start.2 = (bf16[32,16,3072]{2,1,0:T(8,128)(2,1)S(1)}, bf16[32,16,3072]{2,1,0:T(8,128)(2,1)}, u32[]{:S(2)}) copy-start(bf16[32,16,3072]{2,1,0:T(8,128)(2,1)} %param.11) | copy-start | bytes 9437188
  16.4 4.9 %collective-permute-start.11 = (s32[1,128]{1,0:T(1,128)S(1)}, s32[1,128]{1,0:T(1,128)S(1)}, u32[]{:S(2)}, u32[]{:S(2)}) collective-permute-start(s32[1,128]{1,0:T(1,128)S(1)} %broadcast_in_dim.260), channel_id=1, source_target_pairs={{0,1},{1,0},{2,3},{3,2},{4,5},{5,4},{6,7},{7,6},{8,9},{9,8},{10,11... | collective-permute-start | bytes 1544 | tf_op jit(solution)/shard_map/ppermute | solution.py:515
  16.6 25.0 %collective-permute-start.15 = (bf16[16,3072]{1,0:T(8,128)(2,1)S(1)}, bf16[16,3072]{1,0:T(8,128)(2,1)S(1)}, u32[]{:S(2)}, u32[]{:S(2)}) collective-permute-start(bf16[16,3072]{1,0:T(8,128)(2,1)S(1)} %get-tuple-element.218), channel_id=1, source_target_pairs={{0,8},{4,12},{8,0},{12,4},{1,9},{5,13},{9,1},{13,5},{2,10},{6,14},... | collective-permute-start | bytes 294920 | tf_op jit(solution)/shard_map/ppermute | solution.py:447
  16.9 24.7 %collective-permute-start.16 = (bf16[16,3072]{1,0:T(8,128)(2,1)S(1)}, bf16[16,3072]{1,0:T(8,128)(2,1)S(1)}, u32[]{:S(2)}, u32[]{:S(2)}) collective-permute-start(bf16[16,3072]{1,0:T(8,128)(2,1)S(1)} %get-tuple-element.219), channel_id=1, source_target_pairs={{0,12},{4,8},{8,4},{12,0},{1,13},{5,9},{9,5},{13,1},{2,14},{6,10},... | collective-permute-start | bytes 294920 | tf_op jit(solution)/shard_map/ppermute | solution.py:447
  21.2 32.8 %collective-permute-start.18 = (bf16[88,3072]{1,0:T(8,128)(2,1)S(1)}, bf16[88,3072]{1,0:T(8,128)(2,1)S(1)}, u32[]{:S(2)}, u32[]{:S(2)}) collective-permute-start(bf16[88,3072]{1,0:T(8,128)(2,1)S(1)} %fusion.70), channel_id=1, source_target_pairs={{0,4},{4,0},{8,12},{12,8},{1,5},{5,1},{9,13},{13,9},{2,6},{6,2},{1... | collective-permute-start | bytes 1622024 | tf_op jit(solution)/shard_map/ppermute | solution.py:447
  21.9 14.1 %collective-permute-start.12 = (s32[1,128]{1,0:T(1,128)S(1)}, s32[1,128]{1,0:T(1,128)S(1)}, u32[]{:S(2)}, u32[]{:S(2)}) collective-permute-start(s32[1,128]{1,0:T(1,128)S(1)} %broadcast_maximum_fusion), channel_id=1, source_target_pairs={{0,16},{16,0},{1,17},{17,1},{2,18},{18,2},{3,19},{19,3},{4,20},{20... | collective-permute-start | bytes 1544 | tf_op jit(solution)/shard_map/ppermute | solution.py:515
  34.3 5.6 %collective-permute-start.14 = (f32[64,128]{1,0:T(8,128)S(1)}, f32[64,128]{1,0:T(8,128)S(1)}, u32[]{:S(2)}, u32[]{:S(2)}) collective-permute-start(f32[64,128]{1,0:T(8,128)S(1)} %get-tuple-element.216.refs_1_), channel_id=1, source_target_pairs={{0,2},{2,0},{1,3},{3,1},{4,6},{6,4},{5,7},{7,5},{8,10},{10,8},{9,1... | collective-permute-start | bytes 98312 | tf_op jit(solution)/shard_map/ppermute | solution.py:522
  36.7 26.0 %collective-permute-start.20 = (bf16[64,3072]{1,0:T(8,128)(2,1)S(1)}, bf16[64,3072]{1,0:T(8,128)(2,1)S(1)}, u32[]{:S(2)}, u32[]{:S(2)}) collective-permute-start(bf16[64,3072]{1,0:T(8,128)(2,1)S(1)} %fusion.71), channel_id=1, source_target_pairs={{0,12},{4,8},{8,4},{12,0},{1,13},{5,9},{9,5},{13,1},{2,14},{6,10},... | collective-permute-start | bytes 1179656 | tf_op jit(solution)/shard_map/ppermute | solution.py:447
  43.9 3.8 %collective-permute-start.17 = (f32[32,128]{1,0:T(8,128)S(1)}, f32[32,128]{1,0:T(8,128)S(1)}, u32[]{:S(2)}, u32[]{:S(2)}) collective-permute-start(f32[32,128]{1,0:T(8,128)S(1)} %get-tuple-element.222.refs_1_), channel_id=1, source_target_pairs={{0,2},{2,0},{1,3},{3,1},{4,6},{6,4},{5,7},{7,5},{8,10},{10,8},{9,1... | collective-permute-start | bytes 49160 | tf_op jit(solution)/shard_map/ppermute | solution.py:522
  44.6 33.4 %collective-permute-start.22 = (bf16[64,3072]{1,0:T(8,128)(2,1)S(1)}, bf16[64,3072]{1,0:T(8,128)(2,1)S(1)}, u32[]{:S(2)}, u32[]{:S(2)}) collective-permute-start(bf16[64,3072]{1,0:T(8,128)(2,1)S(1)} %shard_map.79), channel_id=1, source_target_pairs={{0,8},{4,12},{8,0},{12,4},{1,9},{5,13},{9,1},{13,5},{2,10},{6,14},... | collective-permute-start | bytes 1179656 | tf_op jit(solution)/shard_map/ppermute | solution.py:447
  55.6 4.3 %collective-permute-start.19 = (f32[88,128]{1,0:T(8,128)S(1)}, f32[88,128]{1,0:T(8,128)S(1)}, u32[]{:S(2)}, u32[]{:S(2)}) collective-permute-start(f32[88,128]{1,0:T(8,128)S(1)} %get-tuple-element.227.refs_1_), channel_id=1, source_target_pairs={{0,2},{2,0},{1,3},{3,1},{4,6},{6,4},{5,7},{7,5},{8,10},{10,8},{9,1... | collective-permute-start | bytes 135176 | tf_op jit(solution)/shard_map/ppermute | solution.py:522
  57.4 22.5 %collective-permute-start.24 = (bf16[16,3072]{1,0:T(8,128)(2,1)S(1)}, bf16[16,3072]{1,0:T(8,128)(2,1)S(1)}, u32[]{:S(2)}, u32[]{:S(2)}) collective-permute-start(bf16[16,3072]{1,0:T(8,128)(2,1)S(1)} %get-tuple-element.224), channel_id=1, source_target_pairs={{0,8},{4,12},{8,0},{12,4},{1,9},{5,13},{9,1},{13,5},{2,10},{6,14},... | collective-permute-start | bytes 294920 | tf_op jit(solution)/shard_map/ppermute | solution.py:447
  58.0 22.0 %collective-permute-start.25 = (bf16[16,3072]{1,0:T(8,128)(2,1)S(1)}, bf16[16,3072]{1,0:T(8,128)(2,1)S(1)}, u32[]{:S(2)}, u32[]{:S(2)}) collective-permute-start(bf16[16,3072]{1,0:T(8,128)(2,1)S(1)} %get-tuple-element.225), channel_id=1, source_target_pairs={{0,12},{4,8},{8,4},{12,0},{1,13},{5,9},{9,5},{13,1},{2,14},{6,10},... | collective-permute-start | bytes 294920 | tf_op jit(solution)/shard_map/ppermute | solution.py:447
  61.7 33.0 %collective-permute-start.23 = (bf16[88,3072]{1,0:T(8,128)(2,1)S(1)}, bf16[88,3072]{1,0:T(8,128)(2,1)S(1)}, u32[]{:S(2)}, u32[]{:S(2)}) collective-permute-start(bf16[88,3072]{1,0:T(8,128)(2,1)S(1)} %shard_map.83), channel_id=1, source_target_pairs={{0,4},{4,0},{8,12},{12,8},{1,5},{5,1},{9,13},{13,9},{2,6},{6,2},{1... | collective-permute-start | bytes 1622024 | tf_op jit(solution)/shard_map/ppermute | solution.py:447
  64.5 4.0 %collective-permute-start.21 = (f32[64,128]{1,0:T(8,128)S(1)}, f32[64,128]{1,0:T(8,128)S(1)}, u32[]{:S(2)}, u32[]{:S(2)}) collective-permute-start(f32[64,128]{1,0:T(8,128)S(1)} %get-tuple-element.231.refs_0_), channel_id=1, source_target_pairs={{0,2},{2,0},{1,3},{3,1},{4,6},{6,4},{5,7},{7,5},{8,10},{10,8},{9,1... | collective-permute-start | bytes 98312 | tf_op jit(solution)/shard_map/ppermute | solution.py:522
  70.2 11.7 %collective-permute-start.10 = (f32[256,128]{1,0:T(8,128)S(1)}, f32[256,128]{1,0:T(8,128)S(1)}, u32[]{:S(2)}, u32[]{:S(2)}) collective-permute-start(f32[256,128]{1,0:T(8,128)S(1)} %get-tuple-element.206.refs_0_), channel_id=1, source_target_pairs={{0,2},{2,0},{1,3},{3,1},{4,6},{6,4},{5,7},{7,5},{8,10},{10,8},{9,1... | collective-permute-start | bytes 393224 | tf_op jit(solution)/shard_map/ppermute | solution.py:522
  80.5 3.5 %collective-permute-start.26 = (bf16[16,3072]{1,0:T(8,128)(2,1)S(1)}, bf16[16,3072]{1,0:T(8,128)(2,1)S(1)}, u32[]{:S(2)}, u32[]{:S(2)}) collective-permute-start(bf16[16,3072]{1,0:T(8,128)(2,1)S(1)} %shard_map.86), channel_id=1, source_target_pairs={{0,1},{1,0},{2,3},{3,2},{4,5},{5,4},{6,7},{7,6},{8,9},{9,8},{10,11... | collective-permute-start | bytes 294920 | tf_op jit(solution)/shard_map/ppermute | solution.py:603
  80.6 18.2 %collective-permute-start.27 = (bf16[64,3072]{1,0:T(8,128)(2,1)S(1)}, bf16[64,3072]{1,0:T(8,128)(2,1)S(1)}, u32[]{:S(2)}, u32[]{:S(2)}) collective-permute-start(bf16[64,3072]{1,0:T(8,128)(2,1)S(1)} %shard_map.85), channel_id=1, source_target_pairs={{0,12},{4,8},{8,4},{12,0},{1,13},{5,9},{9,5},{13,1},{2,14},{6,10},... | collective-permute-start | bytes 1179656 | tf_op jit(solution)/shard_map/ppermute | solution.py:447
